TPU v7x, 32 devices: a whole 2x2x4 slice. The times are simulated.
32 devices in a mesh: dp: 4 (over y, core), expert: 8 (over z, x).
Axes of the slice: x: 2, y: 2, z: 4, core: 2. Of those that a mesh axis runs over, the one named last changes fastest.
Arguments:
- tokens: bfloat16 [4, 1024, 2, 2048], P('dp', 'expert'), may hold values from -6 to 6
- lengths: int32 [4, 2], replicated, may hold values from 256 to 1024, as said below
- routes: int32 [4, 1024, 2, 8], P('dp', 'expert'), may hold values from 0 to 15, all different within a row; in each aligned block of 256 rows (0 to 255, 256 to 511, ..., all dimensions but the last counted through in order) at most 192 rows name the same one
- attn_gain: float32 [2048], replicated, may hold values from 0.25 to 1.75
- q_gain: float32 [128], replicated, may hold values from 0.25 to 1.75
- k_gain: float32 [128], replicated, may hold values from 0.25 to 1.75
- qkv_weight: bfloat16 [2048, 3, 2048], P(('dp', 'expert')), may hold values from -0.125 to 0.125
- out_weight: bfloat16 [2048, 2048], P(('dp', 'expert')), may hold values from -2.5 to 2.5
- ffn_gain: float32 [2048], replicated, may hold values from 0.25 to 1.75
- router_weight: bfloat16 [2048, 16], replicated, may hold values from -0.0625 to 0.0625
- expert_in: bfloat16 [16, 2048, 2048], P('expert'), may hold values from -0.125 to 0.125
- expert_out: bfloat16 [16, 1024, 2048], P('expert'), may hold values from -0.75 to 0.75
- balance_coef: float32 [1], replicated, may hold values from 0.5 to 1.5
- cotangent: bfloat16 [4, 1024, 2, 2048], P('dp', 'expert'), may hold values from -6 to 6
Outputs:
- block_out: float32 [4, 1024, 2, 2048], P('dp', 'expert')
- balance_loss: float32 [1], replicated
- grad_tokens: float32 [4, 1024, 2, 2048], P('dp', 'expert')
- grad_attn_gain: float32 [2048], replicated
- grad_q_gain: float32 [128], replicated
- grad_k_gain: float32 [128], replicated
- grad_qkv: float32 [2048, 3, 2048], P(('dp', 'expert'))
- grad_out_weight: float32 [2048, 2048], P(('dp', 'expert'))
- grad_ffn_gain: float32 [2048], replicated
- grad_router: float32 [2048, 16], replicated
- grad_expert_in: float32 [16, 2048, 2048], P('expert', 'dp')
- grad_expert_out: float32 [16, 1024, 2048], P('expert', 'dp')
Inputs may be any that keep to these rules, and one draw needn't show every extreme that they name: `routes`: each row names 8 different experts. In the rows of one device, aligned blocks of 256 rows in the order group, slot, sequence, no expert is named by more than 192 rows. `lengths`: in each group one of the 2 sequences, which one varies, holds all 1024 slots.
All inputs are finite; a program needn't handle non-finite values.
Results may differ from a plain program's by a relative error of at most 0.02.
Values may be sent and summed in bfloat16 or wider, within the bound.
No kernel may reach another device: no remote copies, remote signals or barrier semaphores. Data moves between devices by JAX's collectives and lax.ppermute only.
A program may use at most 384 MiB of HBM per device.

v0:
```python
import math

import jax
import jax.numpy as jnp
from jax import lax
from jax.sharding import PartitionSpec as P

HEADS = 16
HD = 128
FF = 1024
TOPK = 8


NORM_EPS = 1e-05
PRECISE = lax.Precision.HIGHEST


def norm_rows(values, scale_gain):
    return (
        values
        * lax.rsqrt(jnp.mean(values * values, axis=-1, keepdims=True) + NORM_EPS)
        * scale_gain
    )


def rotary(values, positions):
    half_width = values.shape[-1] // 2
    inv_freq = jnp.exp(
        jnp.arange(half_width, dtype=jnp.float32) * (-2.0 * math.log(10000.0) / values.shape[-1])
    )
    angles = positions[:, None] * inv_freq[None, :]
    cosine = jnp.cos(angles)[:, None, None, :]
    sine = jnp.sin(angles)[:, None, None, :]
    first_half = values[..., :half_width]
    second_half = values[..., half_width:]
    return jnp.concatenate(
        [first_half * cosine - second_half * sine, second_half * cosine + first_half * sine],
        axis=-1,
    )


def body(
    tokens,
    lengths,
    routes,
    attn_gain,
    q_gain,
    k_gain,
    qkv_weight,
    out_weight,
    ffn_gain,
    router_weight,
    expert_in,
    expert_out,
    balance_coef,
    cotangent,
):
    n_expert = lax.axis_size("expert")
    group_index = lax.axis_index("dp")
    member = lax.axis_index("expert")
    slot_count = tokens.shape[1]
    seq_count = tokens.shape[2]
    width = tokens.shape[3]
    experts_here = expert_in.shape[0]
    experts_all = experts_here * n_expert
    tok_rows = slot_count * seq_count
    capacity = 3 * tok_rows * TOPK // (2 * experts_all)
    full_len = slot_count * n_expert
    head_shape = (slot_count, seq_count, HEADS, HD)
    slot_ids = member * slot_count + jnp.arange(slot_count)
    positions = slot_ids.astype(jnp.float32)
    seq_lens = lengths[group_index]
    valid_mask = (slot_ids[:, None] < seq_lens[None, :]).astype(jnp.float32)
    valid_rows = valid_mask.reshape(tok_rows)
    key_live = jnp.arange(full_len)[None, :] < seq_lens[:, None]
    inputs = tokens[0].astype(jnp.float32)
    w_qkv, w_out = (
        lax.all_gather(qkv_weight, ("dp", "expert"), axis=0, tiled=True),
        lax.all_gather(out_weight, ("dp", "expert"), axis=0, tiled=True),
    )
    normed, norm_back = jax.vjp(norm_rows, inputs, attn_gain)
    normed_low = normed.astype(jnp.bfloat16)
    project = jnp.einsum("tsd,dcf->tscf", normed_low, w_qkv, preferred_element_type=jnp.float32)

    def shape_heads(query_proj, key_proj, query_gain, key_gain):
        return (
            rotary(norm_rows(query_proj.reshape(head_shape), query_gain), positions),
            rotary(norm_rows(key_proj.reshape(head_shape), key_gain), positions),
        )

    (query_full, key_full), heads_back = jax.vjp(
        shape_heads, project[:, :, 0], project[:, :, 1], q_gain, k_gain
    )
    queries = query_full.astype(jnp.bfloat16)
    key_part = key_full.astype(jnp.bfloat16)
    value_part = project[:, :, 2].reshape(head_shape).astype(jnp.bfloat16)
    key_rows, values = (
        lax.all_gather(key_part, "expert", axis=0, tiled=True),
        lax.all_gather(value_part, "expert", axis=0, tiled=True),
    )

    def scores_of(key_source):
        raw_scores = jnp.einsum(
            "tshd,ushd->shtu", queries, key_source, preferred_element_type=jnp.float32
        ) / math.sqrt(HD)
        return jnp.where(key_live[:, None, None, :], raw_scores, -1e30)

    scores = scores_of(key_rows)
    highest = jnp.max(scores, axis=-1, keepdims=True)
    expo_scores = jnp.exp(scores - highest)
    totals = jnp.sum(expo_scores, axis=-1, keepdims=True)
    log_total = highest + jnp.log(totals)
    probs_low = (expo_scores / totals).astype(jnp.bfloat16)
    attended = jnp.einsum("shtu,ushd->tshd", probs_low, values, preferred_element_type=jnp.float32)
    attended_low = attended.reshape(tok_rows, width).astype(jnp.bfloat16)
    branch = jnp.dot(attended_low, w_out, preferred_element_type=jnp.float32)
    residual = inputs.reshape(tok_rows, width) + branch
    ffn_normed, ffn_back = jax.vjp(norm_rows, residual, ffn_gain)
    ffn_low = ffn_normed.astype(jnp.bfloat16)
    logits = jnp.dot(ffn_low, router_weight, preferred_element_type=jnp.float32)
    picked_ids = routes.reshape(tok_rows, TOPK)
    chosen = (picked_ids[:, :, None] == jnp.arange(experts_all)[None, None, :]).astype(jnp.float32)

    def route_gates(logit_rows):
        router_probs = jax.nn.softmax(logit_rows, axis=-1)
        picked = jnp.einsum("tke,te->tk", chosen, router_probs, precision=PRECISE)
        return (
            valid_rows[:, None] * picked / jnp.sum(picked, axis=-1, keepdims=True),
            router_probs,
        )

    (gate_weights, router_probs), route_back = jax.vjp(route_gates, logits)
    counts = jnp.sum(valid_rows[:, None, None] * chosen, axis=(0, 1))
    prob_sums = jnp.sum(valid_rows[:, None] * router_probs, axis=0)
    prob_total, count_total = lax.psum((prob_sums, counts), ("dp", "expert"))
    n_valid = jnp.sum(lengths).astype(jnp.float32)
    fraction = count_total / (TOPK * n_valid)
    balance_loss = balance_coef * experts_all * jnp.sum(fraction * (prob_total / n_valid))
    flat_ids = picked_ids.reshape(-1)
    expert_hits = (flat_ids[:, None] == jnp.arange(experts_all)[None, :]).astype(jnp.int32)
    slot_order = jnp.sum((jnp.cumsum(expert_hits, axis=0) - 1) * expert_hits, axis=1)
    slot_index = flat_ids * capacity + slot_order
    source_row = jnp.arange(flat_ids.shape[0]) // TOPK
    buffer_shape = (n_expert, experts_here, capacity, width)
    dispatch_rows = (
        jnp.zeros((experts_all * capacity, width), jnp.bfloat16)
        .at[slot_index]
        .set(ffn_low[source_row])
        .reshape(buffer_shape)
    )
    received = lax.all_to_all(dispatch_rows, "expert", split_axis=0, concat_axis=0, tiled=True)
    gate_up = jnp.einsum("secd,edf->secf", received, expert_in, preferred_element_type=jnp.float32)
    hidden = (jax.nn.silu(gate_up[..., :FF]) * gate_up[..., FF:]).astype(jnp.bfloat16)
    result = jnp.einsum(
        "secf,efd->secd", hidden, expert_out, preferred_element_type=jnp.float32
    ).astype(jnp.bfloat16)
    returned = lax.all_to_all(result, "expert", split_axis=0, concat_axis=0, tiled=True)
    returned, received, gate_up, hidden = (returned, received, gate_up, hidden)
    paired = returned.reshape(experts_all * capacity, width)[slot_index].reshape(
        tok_rows, TOPK, width
    )
    paired_full = paired.astype(jnp.float32)
    mixture = jnp.sum(gate_weights[:, :, None] * paired_full, axis=1)
    block_out = (residual + mixture).reshape(1, slot_count, seq_count, width)
    out_grad = cotangent[0].astype(jnp.float32).reshape(tok_rows, width) * valid_rows[:, None]
    gate_grads = jnp.sum(paired_full * out_grad[:, None, :], axis=-1)
    pair_grads = (
        (gate_weights[:, :, None] * out_grad[:, None, :]).astype(jnp.bfloat16).reshape(-1, width)
    )
    grad_rows = (
        jnp.zeros((experts_all * capacity, width), jnp.bfloat16)
        .at[slot_index]
        .set(pair_grads)
        .reshape(buffer_shape)
    )
    result_grad = lax.all_to_all(grad_rows, "expert", split_axis=0, concat_axis=0, tiled=True)
    hidden_grad = jnp.einsum(
        "secd,efd->secf", result_grad, expert_out, preferred_element_type=jnp.float32
    )
    gate_pre = gate_up[..., :FF]
    up_pre = gate_up[..., FF:]
    gate_sigmoid = jax.nn.sigmoid(gate_pre)
    gate_up_grad = jnp.concatenate(
        [
            hidden_grad * up_pre * gate_sigmoid * (1.0 + gate_pre * (1.0 - gate_sigmoid)),
            hidden_grad * gate_pre * gate_sigmoid,
        ],
        axis=-1,
    ).astype(jnp.bfloat16)
    received_grad = jnp.einsum(
        "secf,edf->secd", gate_up_grad, expert_in, preferred_element_type=jnp.float32
    ).astype(jnp.bfloat16)
    sent_grad = lax.all_to_all(received_grad, "expert", split_axis=0, concat_axis=0, tiled=True)
    ffn_grad = jnp.sum(
        sent_grad.reshape(experts_all * capacity, width)[slot_index]
        .reshape(tok_rows, TOPK, width)
        .astype(jnp.float32),
        axis=1,
    )
    in_terms = jnp.einsum(
        "secd,secf->edf", received, gate_up_grad, preferred_element_type=jnp.float32
    )
    out_terms = jnp.einsum(
        "secf,secd->efd", hidden, result_grad, preferred_element_type=jnp.float32
    )
    grad_expert_in, grad_expert_out = (
        lax.psum_scatter(
            in_terms.astype(jnp.bfloat16), "dp", scatter_dimension=1, tiled=True
        ).astype(jnp.float32),
        lax.psum_scatter(
            out_terms.astype(jnp.bfloat16), "dp", scatter_dimension=1, tiled=True
        ).astype(jnp.float32),
    )
    balance_grad = balance_coef * experts_all * fraction[None, :] / n_valid * valid_rows[:, None]
    (logit_grad,) = route_back((gate_grads, balance_grad))
    ffn_grad = ffn_grad + jnp.dot(
        logit_grad, router_weight.astype(jnp.float32).T, precision=PRECISE
    )
    router_terms = jnp.dot(ffn_low.astype(jnp.float32).T, logit_grad, precision=PRECISE)
    residual_norm_grad, ffn_gain_terms = ffn_back(ffn_grad)
    residual_grad = out_grad + residual_norm_grad
    branch_grad = residual_grad.astype(jnp.bfloat16)
    attended_grad = (
        jnp.dot(branch_grad, w_out.T, preferred_element_type=jnp.float32)
        .astype(jnp.bfloat16)
        .reshape(head_shape)
    )
    keys_back, values_back = (key_rows, values)
    probs_back = jnp.exp(scores_of(keys_back) - log_total)
    prob_grad = jnp.einsum(
        "tshd,ushd->shtu", attended_grad, values_back, preferred_element_type=jnp.float32
    )
    row_dot = jnp.sum(probs_back * prob_grad, axis=-1, keepdims=True)
    score_grad = (probs_back * (prob_grad - row_dot)).astype(jnp.bfloat16)
    query_grad = jnp.einsum(
        "shtu,ushd->tshd", score_grad, keys_back, preferred_element_type=jnp.float32
    ) / math.sqrt(HD)
    key_terms = jnp.einsum(
        "shtu,tshd->ushd", score_grad, queries, preferred_element_type=jnp.float32
    ) / math.sqrt(HD)
    value_terms = jnp.einsum(
        "shtu,tshd->ushd",
        probs_back.astype(jnp.bfloat16),
        attended_grad,
        preferred_element_type=jnp.float32,
    )
    key_grad, value_grad = (
        lax.psum_scatter(
            key_terms.astype(jnp.bfloat16), "expert", scatter_dimension=0, tiled=True
        ).astype(jnp.float32),
        lax.psum_scatter(
            value_terms.astype(jnp.bfloat16), "expert", scatter_dimension=0, tiled=True
        ).astype(jnp.float32),
    )
    query_proj_grad, key_proj_grad, q_gain_terms, k_gain_terms = heads_back((query_grad, key_grad))
    proj_grad = jnp.stack(
        [query_proj_grad, key_proj_grad, value_grad.reshape(slot_count, seq_count, width)], axis=2
    ).astype(jnp.bfloat16)
    normed_grad = jnp.einsum("tscf,dcf->tsd", proj_grad, w_qkv, preferred_element_type=jnp.float32)
    input_norm_grad, attn_gain_terms = norm_back(normed_grad)
    grad_tokens = (residual_grad.reshape(slot_count, seq_count, width) + input_norm_grad)[None]
    normed_flat = normed_low.reshape(tok_rows, width)
    proj_flat = proj_grad.reshape(tok_rows, 3, width)
    proj_terms = jnp.einsum(
        "tr,tcf->rcf", normed_flat, proj_flat, preferred_element_type=jnp.float32
    )
    output_terms = jnp.einsum(
        "tr,tf->rf", attended_low, branch_grad, preferred_element_type=jnp.float32
    )
    summed_terms = lax.psum_scatter(
        jnp.concatenate([proj_terms, output_terms[:, None, :]], axis=1),
        ("dp", "expert"),
        scatter_dimension=0,
        tiled=True,
    )
    grad_attn_gain, grad_q_gain, grad_k_gain, grad_ffn_gain, grad_router = lax.psum(
        (attn_gain_terms, q_gain_terms, k_gain_terms, ffn_gain_terms, router_terms),
        ("dp", "expert"),
    )
    return (
        block_out,
        balance_loss,
        grad_tokens,
        grad_attn_gain,
        grad_q_gain,
        grad_k_gain,
        summed_terms[:, :3],
        summed_terms[:, 3],
        grad_ffn_gain,
        grad_router,
        grad_expert_in,
        grad_expert_out,
    )


def solution(mesh):
    placed = (
        P("dp", "expert", None, None),
        P(),
        P("dp", "expert", None, None),
        P(),
        P(),
        P(),
        P(("dp", "expert"), None, None),
        P(("dp", "expert"), None),
        P(),
        P(),
        P("expert", None, None),
        P("expert", None, None),
        P(),
        P("dp", "expert", None, None),
    )
    return jax.shard_map(
        body,
        mesh=mesh,
        in_specs=placed,
        out_specs=(
            P("dp", "expert", None, None),
            P(),
            P("dp", "expert", None, None),
            P(),
            P(),
            P(),
            P(("dp", "expert"), None, None),
            P(("dp", "expert"), None),
            P(),
            P(),
            P("expert", "dp", None),
            P("expert", "dp", None),
        ),
        check_vma=False,
    )
```

profile of v0, /device:TPU:0, one launch (start us, length us, event | category | flops | bytes accessed | tf_op | source)
XLA Modules:
  0.0 3918.4 jit_solution(8730103915984962696)
XLA Ops:
  10.6 157.7 %all-gather.5.cloned.1.call-done = bf16[2048,3,2048]{2,0,1:T(8,128)(2,1)} async-done(((bf16[64,3,2048]{2,0,1:T(8,128)(2,1)}), bf16[2048,3,2048]{2,0,1:T(8,128)(2,1)}) %all-gather.5.cloned.1.call-update) | async-done | bytes 25165840 | tf_op jit(solution)/shard_map/all_gather | solution.py:78
  168.3 12.9 fusion.2
  217.4 100.2 %all-gather.9.cloned.1.call-done = bf16[1024,2,16,128]{3,0,2,1:T(8,128)(2,1)} async-done(((bf16[128,2,16,128]{3,0,2,1:T(8,128)(2,1)}), bf16[1024,2,16,128]{3,0,2,1:T(8,128)(2,1)}) %all-gather.9.cloned.1.call-update) | async-done | bytes 8388624 | tf_op jit(solution)/shard_map/all_gather | solution.py:98
  333.5 110.3 %all-gather.7.cloned.1.call-done = bf16[1024,2,16,128]{0,3,2,1:T(8,128)(2,1)} async-done(((bf16[128,2,16,128]{0,3,2,1:T(8,128)(2,1)}), bf16[1024,2,16,128]{0,3,2,1:T(8,128)(2,1)}) %all-gather.7.cloned.1.call-update) | async-done | bytes 8388624 | tf_op jit(solution)/shard_map/all_gather | solution.py:99
  443.8 11.8 fusion.70
  457.6 64.7 %all-gather.11.cloned.1.call-done = bf16[2048,2048]{1,0:T(8,128)(2,1)} async-done(((bf16[64,2048]{1,0:T(8,128)(2,1)}), bf16[2048,2048]{1,0:T(8,128)(2,1)}) %all-gather.11.cloned.1.call-update) | async-done | bytes 8388624 | tf_op jit(solution)/shard_map/all_gather | solution.py:79
  529.7 46.4 %scatter_custom_fusion = bf16[3072,2048]{1,0:T(8,128)(2,1)} fusion(s32[2048]{0:T(1024)S(1)} %bitcast.226, bf16[256,2048]{1,0:T(8,128)(2,1)S(1)} %multiply_convert_fusion.3, s32[2048]{0:T(1024)S(1)} %broadcast_clamp_fusion.1, bf16[]{:T(256)} %constant.81.clone.1), kind=kCustom, calls=%fused_computation.59 | custom fusion | bytes 12582914 | tf_op jit(solution)/shard_map/scatter | solution.py:148
  587.0 20.2 scatter_custom_fusion.1
  607.2 247.9 %all-to-all-done = bf16[8,2,192,2048]{3,2,1,0:T(8,128)(2,1)} async-done(((bf16[8,2,192,2048]{3,2,1,0:T(8,128)(2,1)}), bf16[8,2,192,2048]{3,2,1,0:T(8,128)(2,1)}, u32[]{:S(2)}, u32[]{:S(2)}) %all-to-all-start) | async-done | bytes 12582944 | tf_op jit(solution)/shard_map/all_to_all | solution.py:151
  860.9 33.7 fusion.24
  894.6 239.1 %all-to-all-done.2 = bf16[8,2,192,2048]{3,2,1,0:T(8,128)(2,1)} async-done(((bf16[8,2,192,2048]{3,2,1,0:T(8,128)(2,1)}), bf16[8,2,192,2048]{3,2,1,0:T(8,128)(2,1)}, u32[]{:S(2)}, u32[]{:S(2)}) %all-to-all-start.2) | async-done | bytes 12582944 | tf_op jit(solution)/shard_map/all_to_all | solution.py:176
  1133.7 27.4 fusion.15
  1161.1 33.0 convert_bitcast_fusion
  1210.3 17.5 convert_bitcast_fusion.1
  1233.0 249.3 %all-to-all-done.3 = bf16[8,2,192,2048]{3,2,1,0:T(8,128)(2,1)} async-done(((bf16[8,2,192,2048]{3,2,1,0:T(8,128)(2,1)}), bf16[8,2,192,2048]{3,2,1,0:T(8,128)(2,1)}, u32[]{:S(2)}, u32[]{:S(2)}) %all-to-all-start.3) | async-done | bytes 12582944 | tf_op jit(solution)/shard_map/all_to_all | solution.py:193
  1490.0 22.5 gather_fusion.1
  1523.8 235.4 %all-to-all-done.1 = bf16[8,2,192,2048]{3,2,1,0:T(8,128)(2,1)} async-done(((bf16[8,2,192,2048]{3,2,1,0:T(8,128)(2,1)}), bf16[8,2,192,2048]{3,2,1,0:T(8,128)(2,1)}, u32[]{:S(2)}, u32[]{:S(2)}) %all-to-all-start.1) | async-done | bytes 12582944 | tf_op jit(solution)/shard_map/all_to_all | solution.py:157
  1759.2 22.7 gather_fusion
  1792.5 38.4 psum.49
  1868.8 14.6 multiply_reduce_fusion
  1883.5 12.5 multiply_convert_fusion.1
  1905.5 20.4 bitcast_convert_fusion.1
  1925.9 33.1 bitcast_convert_fusion
  1977.6 41.7 %reduce-scatter.16.cloned.1.call-done = bf16[128,4096]{1,0:T(8,128)(2,1)} async-done(((bf16[1024,4096]{1,0:T(8,128)(2,1)}), bf16[128,4096]{1,0:T(8,128)(2,1)}) %reduce-scatter.16.cloned.1.call-update) | async-done | bytes 1048592
  2022.6 149.1 %reduce-scatter.8.cloned.1.call-done = bf16[128,2,16,128]{3,0,2,1:T(8,128)(2,1)} async-done(((bf16[1024,2,16,128]{3,0,2,1:T(8,128)(2,1)}), bf16[128,2,16,128]{3,0,2,1:T(8,128)(2,1)}) %reduce-scatter.8.cloned.1.call-update) | async-done | bytes 1048592 | tf_op jit(solution)/shard_map/reduce_scatter | solution.py:248
  2193.8 22.0 convolution_bitcast_fusion
  2215.8 47.5 %pad_maximum_fusion = f32[2048,4,2048]{2,0,1:T(8,128)} fusion(f32[2048,1,2048]{2,0,1:T(8,128)} %convolution_bitcast_fusion.1, f32[2048,3,2048]{2,0,1:T(8,128)} %convolution_bitcast_fusion), kind=kLoop, calls=%fused_computation.5 | loop fusion | flops 16777216 | bytes 134217728 | tf_op jit(solution)/shard_map/concatenate | solution.py:271
  2277.3 96.6 %reduce-scatter.12.cloned.1.call-done = bf16[2,512,2048]{2,1,0:T(8,128)(2,1)} async-done(((bf16[2,2048,2048]{2,1,0:T(8,128)(2,1)}), bf16[2,512,2048]{2,1,0:T(8,128)(2,1)}) %reduce-scatter.12.cloned.1.call-update) | async-done | bytes 4194320 | tf_op jit(solution)/shard_map/reduce_scatter | solution.py:207
  2380.6 14.8 fusion.68
  2401.8 58.9 %all-reduce.4 = (f32[16]{0:T(128)S(1)}, f32[2048]{0:T(1024)}, f32[128]{0:T(128)}, f32[128]{0:T(128)}, f32[2048]{0:T(1024)}) all-reduce(f32[16]{0:T(128)S(1)} %copy-done.95, f32[2048]{0:T(1024)S(1)} %get-tuple-element.92, f32[128]{0:T(128)S(1)} %get-tuple-element.88, ...), channel_id=1, replica_groups=mesh['dp'=4,'expert'=8] {'dp','expert'}, use_global_device_ids=true, to_apply=%region_18.19 | all-reduce | flops 4368 | bytes 34944 | tf_op jit(solution)/shard_map/psum | solution.py:135
  2461.9 1318.3 %reduce-scatter.10.cloned.1.call-done = f32[64,4,2048]{2,0,1:T(8,128)} async-done(((f32[2048,4,2048]{2,0,1:T(8,128)}), f32[64,4,2048]{2,0,1:T(8,128)}) %reduce-scatter.10.cloned.1.call-update) | async-done | bytes 2097168 | tf_op jit(solution)/shard_map/reduce_scatter | solution.py:270
  3784.8 123.8 %all-reduce.7.cloned.1.call-done = f32[2048,16]{0,1:T(8,128)} async-done(((f32[2048,16]{0,1:T(8,128)}), f32[2048,16]{0,1:T(8,128)}) %all-reduce.7.cloned.1.call-update) | async-done | bytes 131088 | tf_op jit(solution)/shard_map/psum | solution.py:276
  (331 shorter events, 255.0 us)
Async XLA Ops:
  7.2 577.7 %copy-start = (bf16[2048,16]{0,1:T(8,128)(2,1)S(1)}, bf16[2048,16]{0,1:T(8,128)(2,1)}, u32[]{:S(2)}) copy-start(bf16[2048,16]{0,1:T(8,128)(2,1)} %param.23) | copy-start | bytes 196612
  7.2 161.1 %all-gather.5.cloned.1.call-start = ((), (), s32[]{:S(2)}) async-start(), calls=%async_computation.9 | async-start | bytes 25952256 | tf_op jit(solution)/shard_map/all_gather | solution.py:78
  7.9 309.7 %all-gather.9.cloned.1.call-start = ((), (), s32[]{:S(2)}) async-start(), calls=%async_computation.11 | async-start | bytes 9437184 | tf_op jit(solution)/shard_map/all_gather | solution.py:98
  10.2 171.0 %copy-start.75 = (f32[128,2]{0,1:T(2,128)}, f32[128,2]{0,1:T(2,128)S(1)}, u32[]{:S(2)}) copy-start(f32[128,2]{0,1:T(2,128)S(1)} %fusion.92) | copy-start | bytes 3076
  10.5 180.3 %copy-start.34 = (f32[128,64]{1,0:T(8,128)}, f32[128,64]{1,0:T(8,128)S(1)}, u32[]{:S(2)}) copy-start(f32[128,64]{1,0:T(8,128)S(1)} %get-tuple-element.124) | copy-start | bytes 98308
  10.5 180.3 %copy-start.36 = (f32[128,64]{1,0:T(8,128)}, f32[128,64]{1,0:T(8,128)S(1)}, u32[]{:S(2)}) copy-start(f32[128,64]{1,0:T(8,128)S(1)} %get-tuple-element.125) | copy-start | bytes 98308
  192.3 125.3 %copy-start.21 = (bf16[128,2,16,64]{3,0,2,1:T(8,128)(2,1)}, bf16[128,2,16,64]{3,0,2,1:T(8,128)(2,1)S(1)}, u32[]{:S(2)}) copy-start(bf16[128,2,16,64]{3,0,2,1:T(8,128)(2,1)S(1)} %get-tuple-element.114) | copy-start | bytes 1572868
  192.3 125.3 %copy-start.23 = (bf16[128,2,16,64]{3,0,2,1:T(8,128)(2,1)}, bf16[128,2,16,64]{3,0,2,1:T(8,128)(2,1)S(1)}, u32[]{:S(2)}) copy-start(bf16[128,2,16,64]{3,0,2,1:T(8,128)(2,1)S(1)} %get-tuple-element.115) | copy-start | bytes 1572868
  193.9 249.9 %all-gather.7.cloned.1.call-start = ((), (), s32[]{:S(2)}) async-start(), calls=%async_computation.10 | async-start | bytes 9437184 | tf_op jit(solution)/shard_map/all_gather | solution.py:99
  199.0 323.3 %all-gather.11.cloned.1.call-start = ((), (), s32[]{:S(2)}) async-start(), calls=%async_computation.12 | async-start | bytes 8650752 | tf_op jit(solution)/shard_map/all_gather | solution.py:79
  217.3 226.5 %copy-start.41 = (pred[2,1024]{1,0:T(4,128)(4,1)}, pred[2,1024]{1,0:T(4,128)(4,1)S(1)}, u32[]{:S(2)}) copy-start(pred[2,1024]{1,0:T(4,128)(4,1)S(1)} %iota_compare_fusion.3) | copy-start | bytes 6148
  217.3 369.6 %copy-start.73 = (s32[2048,1]{0,1:T(1,128)}, s32[2048,1]{0,1:T(1,128)S(1)}, u32[]{:S(2)}) copy-start(s32[2048,1]{0,1:T(1,128)S(1)} %compare_select_fusion.1) | copy-start | bytes 24580
  333.5 188.8 %copy-start.28 = (f32[256,2048]{1,0:T(8,128)S(1)}, f32[256,2048]{1,0:T(8,128)}, u32[]{:S(2)}) copy-start(f32[256,2048]{1,0:T(8,128)} %reshape.436) | copy-start | bytes 6291460
  576.1 279.0 %all-to-all-start = ((bf16[8,2,192,2048]{3,2,1,0:T(8,128)(2,1)}), bf16[8,2,192,2048]{3,2,1,0:T(8,128)(2,1)}, u32[]{:S(2)}, u32[]{:S(2)}) async-start(bf16[8,2,192,2048]{3,2,1,0:T(8,128)(2,1)} %bitcast.211), calls=%async_computation | async-start | bytes 25165824 | tf_op jit(solution)/shard_map/all_to_all | solution.py:151
  855.1 278.6 %all-to-all-start.2 = ((bf16[8,2,192,2048]{3,2,1,0:T(8,128)(2,1)}), bf16[8,2,192,2048]{3,2,1,0:T(8,128)(2,1)}, u32[]{:S(2)}, u32[]{:S(2)}) async-start(bf16[8,2,192,2048]{3,2,1,0:T(8,128)(2,1)} %bitcast.212), calls=%async_computation.2 | async-start | bytes 25165824 | tf_op jit(solution)/shard_map/all_to_all | solution.py:176
  1205.0 277.3 %all-to-all-start.3 = ((bf16[8,2,192,2048]{3,2,1,0:T(8,128)(2,1)}), bf16[8,2,192,2048]{3,2,1,0:T(8,128)(2,1)}, u32[]{:S(2)}, u32[]{:S(2)}) async-start(bf16[8,2,192,2048]{3,2,1,0:T(8,128)(2,1)} %copy.259), calls=%async_computation.3 | async-start | bytes 25165824 | tf_op jit(solution)/shard_map/all_to_all | solution.py:193
  1233.0 255.0 %copy-start.94 = (s32[4,2]{0,1:T(2,128)S(1)}, s32[4,2]{0,1:T(2,128)}, u32[]{:S(2)}) copy-start(s32[4,2]{0,1:T(2,128)} %param.15) | copy-start | bytes 100
  1233.0 256.9 %copy-start.74 = (s32[2048,1]{0,1:T(1,128)S(1)}, s32[2048,1]{0,1:T(1,128)}, u32[]{:S(2)}) copy-start(s32[2048,1]{0,1:T(1,128)} %copy-done.73) | copy-start | bytes 24580
  1233.0 256.9 %copy-start.69 = (f32[256]{0:T(256)S(1)}, f32[256]{0:T(256)}, u32[]{:S(2)}) copy-start(f32[256]{0:T(256)} %copy-done.68) | copy-start | bytes 3076
  1233.0 256.9 %copy-start.78 = (f32[256]{0:T(256)S(1)}, f32[256]{0:T(256)}, u32[]{:S(2)}) copy-start(f32[256]{0:T(256)} %copy-done.77) | copy-start | bytes 3076
  1233.0 257.0 %copy-start.50 = (f32[2,16,128]{2,1,0:T(8,128)S(1)}, f32[2,16,128]{2,1,0:T(8,128)}, u32[]{:S(2)}) copy-start(f32[2,16,128]{2,1,0:T(8,128)} %copy-done.49) | copy-start | bytes 49156
  1233.0 257.0 %copy-start.64 = (f32[2,16,128]{2,1,0:T(8,128)S(1)}, f32[2,16,128]{2,1,0:T(8,128)}, u32[]{:S(2)}) copy-start(f32[2,16,128]{2,1,0:T(8,128)} %copy-done.63) | copy-start | bytes 49156
  1482.3 276.9 %all-to-all-start.1 = ((bf16[8,2,192,2048]{3,2,1,0:T(8,128)(2,1)}), bf16[8,2,192,2048]{3,2,1,0:T(8,128)(2,1)}, u32[]{:S(2)}, u32[]{:S(2)}) async-start(bf16[8,2,192,2048]{3,2,1,0:T(8,128)(2,1)} %copy.257), calls=%async_computation.1 | async-start | bytes 25165824 | tf_op jit(solution)/shard_map/all_to_all | solution.py:157
  1487.7 531.6 %reduce-scatter.16.cloned.1.call-start = ((), (), s32[]{:S(2)}) async-start(), calls=%async_computation.18 | async-start | bytes 9437184
  1868.8 302.9 %reduce-scatter.8.cloned.1.call-start = ((), (), s32[]{:S(2)}) async-start(), calls=%async_computation.13 | async-start | bytes 9437184 | tf_op jit(solution)/shard_map/reduce_scatter | solution.py:248
  1905.4 358.1 %reduce-scatter.14.cloned.1.call-start = ((), (), s32[]{:S(2)}) async-start(), calls=%async_computation.17 | async-start | bytes 10485760 | tf_op jit(solution)/shard_map/reduce_scatter | solution.py:210
  1925.9 448.1 %reduce-scatter.12.cloned.1.call-start = ((), (), s32[]{:S(2)}) async-start(), calls=%async_computation.16 | async-start | bytes 20971520 | tf_op jit(solution)/shard_map/reduce_scatter | solution.py:207
  1959.0 1821.2 %reduce-scatter.10.cloned.1.call-start = ((), (), s32[]{:S(2)}) async-start(), calls=%async_computation.14 | async-start | bytes 69206016 | tf_op jit(solution)/shard_map/reduce_scatter | solution.py:270
  1977.6 195.6 %copy-start.35 = (f32[128,64]{1,0:T(8,128)S(1)}, f32[128,64]{1,0:T(8,128)}, u32[]{:S(2)}) copy-start(f32[128,64]{1,0:T(8,128)} %copy-done.34) | copy-start | bytes 98308
  1977.6 195.6 %copy-start.37 = (f32[128,64]{1,0:T(8,128)S(1)}, f32[128,64]{1,0:T(8,128)}, u32[]{:S(2)}) copy-start(f32[128,64]{1,0:T(8,128)} %copy-done.36) | copy-start | bytes 98308
  2263.5 1645.2 %all-reduce.7.cloned.1.call-start = ((), (), s32[]{:S(2)}) async-start(), calls=%async_computation.15 | async-start | bytes 262144 | tf_op jit(solution)/shard_map/psum | solution.py:276
  2395.5 1514.8 %copy-start.1 = (bf16[2048,16]{0,1:T(8,128)(2,1)S(1)}, bf16[2048,16]{0,1:T(8,128)(2,1)}, u32[]{:S(2)}) copy-start(bf16[2048,16]{0,1:T(8,128)(2,1)} %param.23) | copy-start | bytes 196612
  (79 other events, 1438.0 us)
Sparse Core Ops, SparseCore 0:
  11.1 157.1 all-gather.4
  194.0 123.4 all-gather.8
  320.2 123.5 all-gather.6
  446.6 75.5 all-gather.10
  1868.9 150.3 reduce-scatter.15
  2023.2 148.4 reduce-scatter.7
  2174.3 70.7 reduce-scatter.13
  2247.8 126.1 reduce-scatter.11
  2376.3 1403.9 reduce-scatter.9
  3786.2 122.4 all-reduce.6
where the time goes:
time: 3930 us; the launch traced here: 3920 us
  waiting for transfers between devices  3140 us (80%)
  matrix products  300 us (8%)
  local copies, waits for them, and re-layouts  180 us (5%)
  other arithmetic  164 us (4%)
  blocking collectives  97.2 us (2%)
    reduce_scatter x1, waiting for transfers between devices, body(): lax.psum_scatter(jnp.concatenate([proj_terms, output_terms[:, None, :]],...  1320 us
    all_to_all x1, waiting for transfers between devices, body(): lax.all_to_all(received_grad, 'expert', split_axis=0, concat_axis=0, tile...  249 us
    all_to_all x1, waiting for transfers between devices, body(): lax.all_to_all(dispatch_rows, 'expert', split_axis=0, concat_axis=0, tile...  248 us
    all_to_all x1, waiting for transfers between devices, body(): lax.all_to_all(grad_rows, 'expert', split_axis=0, concat_axis=0, tiled=True)  239 us
    all_to_all x1, waiting for transfers between devices, body(): lax.all_to_all(result, 'expert', split_axis=0, concat_axis=0, tiled=True)  235 us
    all_gather x1, waiting for transfers between devices, body(): lax.all_gather(qkv_weight, ('dp', 'expert'), axis=0, tiled=True)  158 us
    reduce_scatter x1, waiting for transfers between devices, body(): lax.psum_scatter(key_terms.astype(jnp.bfloat16), 'expert', scatter_dimens...  149 us
    psum x1, waiting for transfers between devices, body(): lax.psum((attn_gain_terms, q_gain_terms, k_gain_terms, ffn_gain_terms, ro...  124 us
  transfers between devices with their start and end apart: 14, of which 13 were waited for; matrix products, arithmetic and copies ran while one was open for 10% of the time, Pallas kernels for 0%

commit v1 on v0

v1 whole, which is shorter than its diff:
```python
import math

import jax
import jax.numpy as jnp
from jax import lax
from jax.sharding import PartitionSpec as P

HEADS = 16
HD = 128
FF = 1024
TOPK = 8


NORM_EPS = 1e-05
PRECISE = lax.Precision.HIGHEST


def norm_rows(values, scale_gain):
    return (
        values
        * lax.rsqrt(jnp.mean(values * values, axis=-1, keepdims=True) + NORM_EPS)
        * scale_gain
    )


def rotary(values, positions):
    half_width = values.shape[-1] // 2
    inv_freq = jnp.exp(
        jnp.arange(half_width, dtype=jnp.float32) * (-2.0 * math.log(10000.0) / values.shape[-1])
    )
    angles = positions[:, None] * inv_freq[None, :]
    cosine = jnp.cos(angles)[:, None, None, :]
    sine = jnp.sin(angles)[:, None, None, :]
    first_half = values[..., :half_width]
    second_half = values[..., half_width:]
    return jnp.concatenate(
        [first_half * cosine - second_half * sine, second_half * cosine + first_half * sine],
        axis=-1,
    )


def body(
    tokens,
    lengths,
    routes,
    attn_gain,
    q_gain,
    k_gain,
    qkv_weight,
    out_weight,
    ffn_gain,
    router_weight,
    expert_in,
    expert_out,
    balance_coef,
    cotangent,
):
    bf16, f32 = jnp.bfloat16, jnp.float32
    n_expert = lax.axis_size("expert")
    group_index = lax.axis_index("dp")
    member = lax.axis_index("expert")
    slot_count = tokens.shape[1]
    seq_count = tokens.shape[2]
    width = tokens.shape[3]
    experts_here = expert_in.shape[0]
    experts_all = experts_here * n_expert
    tok_rows = slot_count * seq_count
    full_len = slot_count * n_expert
    all_rows = tok_rows * n_expert
    heads_here = HEADS // n_expert
    cols = heads_here * HD
    head_shape = (full_len, seq_count, heads_here, HD)
    scale = 1.0 / math.sqrt(HD)

    def gather_rows(rows):
        return lax.all_gather(rows, "expert", axis=0, tiled=True)

    def scatter_rows(rows):
        return lax.psum_scatter(rows, "expert", scatter_dimension=0, tiled=True)

    slot_ids = member * slot_count + jnp.arange(slot_count)
    seq_lens = lengths[group_index]
    valid_mask = (slot_ids[:, None] < seq_lens[None, :]).astype(f32)
    valid_rows = valid_mask.reshape(tok_rows)
    all_slots = jnp.arange(full_len)
    positions = all_slots.astype(f32)
    key_live = all_slots[None, :] < seq_lens[:, None]
    valid_all = (all_slots[:, None] < seq_lens[None, :]).astype(f32).reshape(all_rows)

    picked_ids = routes.reshape(tok_rows, TOPK)
    chosen = jnp.sum(
        (picked_ids[:, :, None] == jnp.arange(experts_all)[None, None, :]).astype(f32), axis=1
    )
    counts = jnp.sum(valid_rows[:, None] * chosen, axis=0)
    count_total = lax.psum(counts, ("dp", "expert"))
    n_valid = jnp.sum(lengths).astype(f32)
    fraction = count_total / (TOPK * n_valid)
    chosen_all = gather_rows(chosen)

    row_count = qkv_weight.shape[0]
    w_cols = lax.all_to_all(
        qkv_weight.reshape(row_count, 3, n_expert, cols),
        "expert",
        split_axis=2,
        concat_axis=0,
        tiled=True,
    ).reshape(n_expert * row_count, 3 * cols)
    w_qkv = lax.all_gather(w_cols, "dp", axis=0, tiled=True)
    w_out = lax.all_gather(
        lax.all_gather(out_weight, "expert", axis=0, tiled=True), "dp", axis=0, tiled=True
    )

    inputs = tokens[0].astype(f32).reshape(tok_rows, width)
    normed, norm_back = jax.vjp(norm_rows, inputs, attn_gain)
    normed_all = gather_rows(normed.astype(bf16))
    project = jnp.dot(normed_all, w_qkv, preferred_element_type=f32)

    def shape_heads(query_proj, key_proj, query_gain, key_gain):
        return (
            rotary(norm_rows(query_proj.reshape(head_shape), query_gain), positions),
            rotary(norm_rows(key_proj.reshape(head_shape), key_gain), positions),
        )

    (query_full, key_full), heads_back = jax.vjp(
        shape_heads, project[:, :cols], project[:, cols : 2 * cols], q_gain, k_gain
    )
    queries = query_full.astype(bf16)
    key_rows = key_full.astype(bf16)
    values = project[:, 2 * cols :].reshape(head_shape).astype(bf16)

    def scores_of():
        raw_scores = (
            jnp.einsum("tshd,ushd->shtu", queries, key_rows, preferred_element_type=f32) * scale
        )
        return jnp.where(key_live[:, None, None, :], raw_scores, -1e30)

    scores = scores_of()
    highest = jnp.max(scores, axis=-1, keepdims=True)
    expo_scores = jnp.exp(scores - highest)
    totals = jnp.sum(expo_scores, axis=-1, keepdims=True)
    log_total = highest + jnp.log(totals)
    probs_low = (expo_scores / totals).astype(bf16)
    attended = jnp.einsum("shtu,ushd->tshd", probs_low, values, preferred_element_type=f32)
    attended_heads = attended.astype(bf16).reshape(n_expert, tok_rows, cols)
    attended_low = (
        lax.all_to_all(attended_heads, "expert", split_axis=0, concat_axis=0, tiled=True)
        .transpose(1, 0, 2)
        .reshape(tok_rows, width)
    )
    residual = inputs + jnp.dot(attended_low, w_out, preferred_element_type=f32)
    ffn_normed, ffn_back = jax.vjp(norm_rows, residual, ffn_gain)
    ffn_low = ffn_normed.astype(bf16)
    ffn_all = gather_rows(ffn_low)
    cot_all = gather_rows(cotangent.reshape(tok_rows, width))

    def route(rows, hits, live):
        logits = jnp.dot(rows, router_weight, preferred_element_type=f32)
        probs = jax.nn.softmax(logits, axis=-1)
        picked = hits * probs
        total = jnp.sum(picked, axis=-1, keepdims=True)
        return probs, picked, total, live[:, None] * picked / total

    router_probs, picked, picked_total, _ = route(ffn_low, chosen, valid_rows)
    gates_all = route(ffn_all, chosen_all, valid_all)[3]
    gates = lax.dynamic_slice_in_dim(gates_all, member * experts_here, experts_here, 1)
    prob_sums = jnp.sum(valid_rows[:, None] * router_probs, axis=0)

    out_grad_all = cot_all.astype(f32) * valid_all[:, None]
    gate_up = jnp.einsum("td,edf->etf", ffn_all, expert_in, preferred_element_type=f32)
    gate_pre = gate_up[..., :FF]
    up_pre = gate_up[..., FF:]
    gate_sigmoid = jax.nn.sigmoid(gate_pre)
    hidden = (gate_pre * gate_sigmoid * up_pre).astype(bf16)
    result = jnp.einsum("etf,efd->etd", hidden, expert_out, preferred_element_type=f32).astype(bf16)
    result_full = result.astype(f32)
    mixture = scatter_rows(
        jnp.sum(gates.T[:, :, None] * result_full, axis=0).astype(bf16)
    ).astype(f32)
    block_out = (residual + mixture).reshape(1, slot_count, seq_count, width)
    gate_grads_here = jnp.sum(result_full * out_grad_all[None], axis=-1).T
    gate_grads = (
        lax.all_to_all(
            gate_grads_here.reshape(n_expert, tok_rows, experts_here),
            "expert",
            split_axis=0,
            concat_axis=0,
            tiled=True,
        )
        .transpose(1, 0, 2)
        .reshape(tok_rows, experts_all)
        * chosen
    )
    pair_grad = (gates.T[:, :, None] * out_grad_all[None]).astype(bf16)
    hidden_grad = jnp.einsum("etd,efd->etf", pair_grad, expert_out, preferred_element_type=f32)
    gate_up_grad = jnp.concatenate(
        [
            hidden_grad * up_pre * gate_sigmoid * (1.0 + gate_pre * (1.0 - gate_sigmoid)),
            hidden_grad * gate_pre * gate_sigmoid,
        ],
        axis=-1,
    ).astype(bf16)
    pair_in = jnp.einsum("etf,edf->td", gate_up_grad, expert_in, preferred_element_type=f32)
    ffn_grad = scatter_rows(pair_in.astype(bf16)).astype(f32)
    in_terms = jnp.einsum("td,etf->edf", ffn_all, gate_up_grad, preferred_element_type=f32)
    out_terms = jnp.einsum("etf,etd->efd", hidden, pair_grad, preferred_element_type=f32)
    grad_expert_in = lax.psum_scatter(
        in_terms.astype(bf16), "dp", scatter_dimension=1, tiled=True
    ).astype(f32)
    grad_expert_out = lax.psum_scatter(
        out_terms.astype(bf16), "dp", scatter_dimension=1, tiled=True
    ).astype(f32)

    live = valid_rows[:, None]
    picked_grad = (
        live
        * chosen
        * (
            gate_grads / picked_total
            - jnp.sum(gate_grads * picked, axis=-1, keepdims=True) / (picked_total * picked_total)
        )
    )
    prob_grad = picked_grad + balance_coef * experts_all * fraction[None, :] / n_valid * live
    logit_grad = router_probs * (
        prob_grad - jnp.sum(router_probs * prob_grad, axis=-1, keepdims=True)
    )
    ffn_grad = ffn_grad + jnp.dot(logit_grad, router_weight.astype(f32).T, precision=PRECISE)
    router_terms = jnp.dot(ffn_low.astype(f32).T, logit_grad, precision=PRECISE)
    residual_norm_grad, ffn_gain_terms = ffn_back(ffn_grad)
    out_grad = cotangent.astype(f32).reshape(tok_rows, width) * live
    residual_grad = out_grad + residual_norm_grad
    branch_grad = residual_grad.astype(bf16)

    attended_grad = (
        lax.all_to_all(
            lax.dot_general(
                branch_grad, w_out, (((1,), (1,)), ((), ())), preferred_element_type=f32
            )
            .astype(bf16)
            .reshape(tok_rows, n_expert, cols),
            "expert",
            split_axis=1,
            concat_axis=0,
            tiled=True,
        )
    ).reshape(head_shape)
    probs_back = jnp.exp(scores_of() - log_total)
    prob_back = jnp.einsum("tshd,ushd->shtu", attended_grad, values, preferred_element_type=f32)
    row_dot = jnp.sum(probs_back * prob_back, axis=-1, keepdims=True)
    score_grad = (probs_back * (prob_back - row_dot)).astype(bf16)
    query_grad = (
        jnp.einsum("shtu,ushd->tshd", score_grad, key_rows, preferred_element_type=f32) * scale
    )
    key_grad = (
        jnp.einsum("shtu,tshd->ushd", score_grad, queries, preferred_element_type=f32) * scale
    )
    value_grad = jnp.einsum(
        "shtu,tshd->ushd", probs_back.astype(bf16), attended_grad, preferred_element_type=f32
    )
    query_proj_grad, key_proj_grad, q_gain_terms, k_gain_terms = heads_back((query_grad, key_grad))
    proj_grad = jnp.concatenate(
        [query_proj_grad, key_proj_grad, value_grad.reshape(all_rows, cols)], axis=1
    ).astype(bf16)
    normed_grad = scatter_rows(
        lax.dot_general(
            proj_grad, w_qkv, (((1,), (1,)), ((), ())), preferred_element_type=f32
        ).astype(bf16)
    ).astype(f32)
    input_norm_grad, attn_gain_terms = norm_back(normed_grad)
    grad_tokens = (residual_grad + input_norm_grad).reshape(1, slot_count, seq_count, width)

    proj_terms = lax.dot_general(
        normed_all, proj_grad, (((0,), (0,)), ((), ())), preferred_element_type=f32
    )
    proj_share = lax.psum_scatter(proj_terms.astype(bf16), "dp", scatter_dimension=0, tiled=True)
    grad_qkv = (
        lax.all_to_all(
            proj_share.reshape(n_expert, row_count, 3, cols),
            "expert",
            split_axis=0,
            concat_axis=0,
            tiled=True,
        )
        .transpose(1, 2, 0, 3)
        .reshape(row_count, 3, width)
        .astype(f32)
    )
    output_terms = lax.dot_general(
        attended_low, branch_grad, (((0,), (0,)), ((), ())), preferred_element_type=f32
    )
    grad_out = lax.psum_scatter(
        lax.psum_scatter(output_terms.astype(bf16), "dp", scatter_dimension=0, tiled=True),
        "expert",
        scatter_dimension=0,
        tiled=True,
    ).astype(f32)
    grad_attn_gain, grad_q_gain, grad_k_gain, grad_ffn_gain, grad_router, prob_total = lax.psum(
        (
            attn_gain_terms,
            q_gain_terms,
            k_gain_terms,
            ffn_gain_terms,
            router_terms,
            prob_sums,
        ),
        ("dp", "expert"),
    )
    balance_loss = balance_coef * experts_all * jnp.sum(fraction * (prob_total / n_valid))
    return (
        block_out,
        balance_loss,
        grad_tokens,
        grad_attn_gain,
        grad_q_gain,
        grad_k_gain,
        grad_qkv,
        grad_out,
        grad_ffn_gain,
        grad_router,
        grad_expert_in,
        grad_expert_out,
    )


def solution(mesh):
    placed = (
        P("dp", "expert", None, None),
        P(),
        P("dp", "expert", None, None),
        P(),
        P(),
        P(),
        P(("dp", "expert"), None, None),
        P(("dp", "expert"), None),
        P(),
        P(),
        P("expert", None, None),
        P("expert", None, None),
        P(),
        P("dp", "expert", None, None),
    )
    return jax.shard_map(
        body,
        mesh=mesh,
        in_specs=placed,
        out_specs=(
            P("dp", "expert", None, None),
            P(),
            P("dp", "expert", None, None),
            P(),
            P(),
            P(),
            P(("dp", "expert"), None, None),
            P(("dp", "expert"), None),
            P(),
            P(),
            P("expert", "dp", None),
            P("expert", "dp", None),
        ),
        check_vma=False,
    )
```

time: 3930 us -> 1710 us (0.44)
  waiting for transfers between devices: 3140 us -> 972 us
  blocking collectives: 97.2 us -> 202 us
  other arithmetic: 164 us -> 77.3 us
  local copies, waits for them, and re-layouts: 180 us -> 102 us
    reduce_scatter x4 -> x8, waiting for transfers between devices: 1560 us -> 498 us  [the longest x3 336 us: scatter_rows(): return lax.psum_scatter(rows, 'expert', scatter_dimension=0, tiled=True)]
    all_to_all x4 -> x3, waiting for transfers between devices: 972 us -> 32.4 us  [the longest x1 25.6 us: body(): lax.all_to_all(lax.dot_general(branch_grad, w_out, (((1,), (1,)), ((), ()...]
    all_gather x4 -> x6, waiting for transfers between devices: 433 us -> 313 us  [the longest x3 269 us: gather_rows(): return lax.all_gather(rows, 'expert', axis=0, tiled=True)]
    all_to_all x0 -> x2, blocking collectives: none -> 91.7 us  [the longest x1 55.9 us: body(): lax.all_to_all(attended_heads, 'expert', split_axis=0, concat_axis=0, til...]
    concatenate x2 -> x0, other arithmetic: 49.1 us -> none  [the longest x1 47.5 us: body(): jnp.concatenate([proj_terms, output_terms[:, None, :]], axis=1)]
    scatter x1 -> x0, local copies, waits for them, and re-layouts: 46.4 us -> none  [body(): dispatch_rows = jnp.zeros((experts_all * capacity, width), jnp.bfloat16)....]
    gather x2 -> x0, local copies, waits for them, and re-layouts: 45.2 us -> none  [the longest x1 22.7 us: body(): returned.reshape(experts_all * capacity, width)[slot_index]]
    unnamed x11 -> x15, waiting for transfers between devices: 42.6 us -> 1.39 us
  transfers between devices with their start and end apart: 14 -> 18, of which waited for: 13 -> 14; matrix products, arithmetic and copies ran while one was open for 10% -> 21% of each run, Pallas kernels for 0% -> 0%
where the time goes in v1:
time: 1710 us
  waiting for transfers between devices  972 us (57%)
  matrix products  324 us (19%)
  blocking collectives  202 us (12%)
  local copies, waits for them, and re-layouts  102 us (6%)
  other arithmetic  77.3 us (5%)
  between operations  18.5 us (1%)
    reduce_scatter x3, waiting for transfers between devices, scatter_rows(): return lax.psum_scatter(rows, 'expert', scatter_dimension=0, tiled=True)  336 us
    all_gather x3, waiting for transfers between devices, gather_rows(): return lax.all_gather(rows, 'expert', axis=0, tiled=True)  269 us
    psum x1, waiting for transfers between devices, body(): lax.psum((attn_gain_terms, q_gain_terms, k_gain_terms, ffn_gain_terms, ro...  127 us
    reduce_scatter x1, waiting for transfers between devices, body(): lax.psum_scatter(in_terms.astype(bf16), 'dp', scatter_dimension=1, tiled=...  122 us
    all_to_all x1, blocking collectives, body(): lax.all_to_all(attended_heads, 'expert', split_axis=0, concat_axis=0, til...  55.9 us
    dot_general x1, matrix products, body(): jnp.einsum('etf,edf->td', gate_up_grad, expert_in, preferred_element_type...  44.1 us
    dot_general x1, matrix products, body(): jnp.einsum('td,etf->edf', ffn_all, gate_up_grad, preferred_element_type=f32)  42.1 us
    dot_general x1, matrix products, body(): jnp.einsum('td,edf->etf', ffn_all, expert_in, preferred_element_type=f32)  41.3 us
  transfers between devices with their start and end apart: 18, of which 14 were waited for; matrix products, arithmetic and copies ran while one was open for 21% of the time, Pallas kernels for 0%

profile of v1, /device:TPU:0, one launch (start us, length us, event | category | flops | bytes accessed | tf_op | source)
XLA Modules:
  0.0 1706.8 jit_solution(4897274375680020941)
XLA Ops:
  9.2 35.8 %all_to_all.45 = bf16[64,3,8,256]{3,0,1,2:T(8,128)(2,1)S(1)} all-to-all(bf16[64,3,8,256]{3,0,1,2:T(8,128)(2,1)S(1)} %bitcast.106), channel_id=1, replica_groups=mesh['dp'=4,'expert'=8] {'expert'}, dimensions={2} | all-to-all | bytes 1572864 | tf_op jit(solution)/shard_map/all_to_all | solution.py:101
  50.9 18.6 %all-gather.11.cloned.1.call-done = bf16[512,2048]{1,0:T(8,128)(2,1)} async-done(((bf16[64,2048]{1,0:T(8,128)(2,1)}), bf16[512,2048]{1,0:T(8,128)(2,1)}) %all-gather.11.cloned.1.call-update) | async-done | bytes 2097168 | tf_op jit(solution)/shard_map/all_gather | solution.py:110
  73.1 26.1 %all-gather.9.cloned.1.call-done = bf16[2048,768]{1,0:T(8,128)(2,1)} async-done(((bf16[512,768]{1,0:T(8,128)(2,1)}), bf16[2048,768]{1,0:T(8,128)(2,1)}) %all-gather.9.cloned.1.call-update) | async-done | bytes 3145744 | tf_op jit(solution)/shard_map/all_gather | solution.py:108
  99.2 127.7 %all-gather.7.cloned.1.call-done = bf16[2048,2048]{1,0:T(8,128)(2,1)} async-done(((bf16[256,2048]{1,0:T(8,128)(2,1)}), bf16[2048,2048]{1,0:T(8,128)(2,1)}) %all-gather.7.cloned.1.call-update) | async-done | bytes 8388624 | tf_op jit(solution)/shard_map/all_gather | solution.py:76
  226.9 10.5 fusion.68
  288.7 55.9 %all_to_all.46 = bf16[8,256,256]{2,1,0:T(8,128)(2,1)} all-to-all(bf16[8,256,256]{2,1,0:T(8,128)(2,1)} %reshape.334), channel_id=1, replica_groups=mesh['dp'=4,'expert'=8] {'expert'}, dimensions={0} | all-to-all | bytes 2097152 | tf_op jit(solution)/shard_map/all_to_all | solution.py:146
  356.2 31.7 %all_gather.25 = f32[2048,16]{0,1:T(8,128)S(1)} all-gather(f32[256,16]{0,1:T(8,128)S(1)} %convert_reduce_fusion), channel_id=1, replica_groups=mesh['dp'=4,'expert'=8] {'expert'}, dimensions={0}, use_global_device_ids=true | all-gather | bytes 147456 | tf_op jit(solution)/shard_map/all_gather | solution.py:76
  387.9 44.7 %all-gather.17.cloned.1.call-done = bf16[2048,2048]{1,0:T(8,128)(2,1)} async-done(((bf16[256,2048]{1,0:T(8,128)(2,1)}), bf16[2048,2048]{1,0:T(8,128)(2,1)}) %all-gather.17.cloned.1.call-update) | async-done | bytes 8388624 | tf_op jit(solution)/shard_map/all_gather | solution.py:76
  432.6 11.1 convert_multiply_fusion.2
  443.7 17.9 %copy.309 = f32[2048,2048]{0,1:T(8,128)} copy(f32[2048,2048]{1,0:T(8,128)} %convert_multiply_fusion.2) | data formatting | bytes 33554432 | tf_op jit(solution)/shard_map/mul | solution.py:168
  461.6 96.2 %all-gather.15.cloned.1.call-done = bf16[2048,2048]{1,0:T(8,128)(2,1)} async-done(((bf16[256,2048]{1,0:T(8,128)(2,1)}), bf16[2048,2048]{1,0:T(8,128)(2,1)}) %all-gather.15.cloned.1.call-update) | async-done | bytes 8388624 | tf_op jit(solution)/shard_map/all_gather | solution.py:76
  563.8 41.3 %convolution_bitcast_fusion = f32[2,2048,2048]{1,2,0:T(8,128)} fusion(bf16[2,2048,2048]{2,1,0:T(8,128)(2,1)} %param.24, bf16[2048,2048]{1,0:T(8,128)(2,1)S(1)} %copy-done.17), kind=kOutput, calls=%fused_computation.26 | convolution fusion | flops 34359738368 | bytes 58720256 | tf_op jit(solution)/shard_map/td,edf->etf/dot_general | solution.py:169
  605.1 35.7 %multiply_convert_fusion.5 = (bf16[2,2048,1024]{1,2,0:T(8,128)(2,1)}, bf16[2,2048,1024]{1,2,0:T(8,128)(2,1)}, bf16[2,2048,1024]{1,2,0:T(8,128)(2,1)}) fusion(f32[2,2048,2048]{1,2,0:T(8,128)} %convolution_bitcast_fusion, bf16[2,1024,2048]{2,1,0:T(8,128)(2,1)} %param.25, f32[2048,2048]{0,1:T(8,128)} %copy.309, f32[2,2048]{1,0:T(2,128)S(1)} %fusion.45), kind=kOutput, calls=%fused_computation.14 | convolution fusion | flops 17263755264 | bytes 83902464 | tf_op jit(solution)/shard_map/etd,efd->etf/dot_general | solution.py:194
  640.8 44.1 %bitcast_convert_fusion = bf16[2048,2048]{1,0:T(8,128)(2,1)} fusion(bf16[2,2048,2048]{2,1,0:T(8,128)(2,1)} %param.24, bf16[2,2048,1024]{1,2,0:T(8,128)(2,1)} %get-tuple-element.134, bf16[2,2048,1024]{1,2,0:T(8,128)(2,1)} %get-tuple-element.133), kind=kOutput, calls=%fused_computation.8 | convolution fusion | flops 34397487104 | bytes 41943040 | tf_op jit(solution)/shard_map/etf,edf->td/dot_general | solution.py:202
  685.0 39.2 %fusion.1 = (f32[2,2048]{1,0:T(2,128)}, bf16[2048,2048]{0,1:T(8,128)(2,1)}) fusion(f32[2048,2048]{0,1:T(8,128)} %copy.309, f32[2,2048]{1,0:T(2,128)S(1)} %fusion.45, bf16[2,2048,1024]{1,2,0:T(8,128)(2,1)} %get-tuple-element.135, bf16[2,1024,2048]{2,1,0:T(8,128)(2,1)} %param.25), kind=kOutput, calls=%fused_computation.3 | convolution fusion | flops 17226002432 | bytes 41975808 | tf_op jit(solution)/shard_map/etf,efd->etd/dot_general | solution.py:174
  724.2 12.1 copy.308
  750.1 38.7 %psum.49 = f32[16]{0:T(128)S(1)} all-reduce(f32[16]{0:T(128)S(1)} %get-tuple-element.122), channel_id=1, replica_groups=mesh['dp'=4,'expert'=8] {'dp','expert'}, use_global_device_ids=true, to_apply=%region_13.14 | all-reduce | flops 16 | bytes 128 | tf_op jit(solution)/shard_map/psum | solution.py:95
  790.0 43.0 %reduce-scatter.11.cloned.1.call-done = bf16[256,2048]{1,0:T(8,128)(2,1)} async-done(((bf16[2048,2048]{1,0:T(8,128)(2,1)}), bf16[256,2048]{1,0:T(8,128)(2,1)}) %reduce-scatter.11.cloned.1.call-update) | async-done | bytes 1048592 | tf_op jit(solution)/shard_map/reduce_scatter | solution.py:79
  837.7 147.4 %reduce-scatter.9.cloned.1.call-done = bf16[256,2048]{1,0:T(8,128)(2,1)} async-done(((bf16[2048,2048]{1,0:T(8,128)(2,1)}), bf16[256,2048]{1,0:T(8,128)(2,1)}) %reduce-scatter.9.cloned.1.call-update) | async-done | bytes 1048592 | tf_op jit(solution)/shard_map/reduce_scatter | solution.py:79
  1008.9 25.6 %all-to-all-done.3 = bf16[256,8,256]{2,0,1:T(8,128)(2,1)S(1)} async-done(((bf16[256,8,256]{2,0,1:T(8,128)(2,1)}), bf16[256,8,256]{2,0,1:T(8,128)(2,1)S(1)}, u32[]{:S(2)}, u32[]{:S(2)}) %all-to-all-start.3) | async-done | bytes 1048608 | tf_op jit(solution)/shard_map/all_to_all | solution.py:234
  1038.2 9.1 fusion.32
  1051.0 9.1 multiply_reduce_fusion
  1060.2 11.9 multiply_convert_fusion.3
  1105.5 24.2 %fusion.19 = bf16[2,1024,2048]{2,1,0:T(8,128)(2,1)} fusion(bf16[2,2048,1024]{1,2,0:T(8,128)(2,1)} %get-tuple-element.135, f32[2048,2048]{0,1:T(8,128)} %copy.309, f32[2,2048]{1,0:T(2,128)S(1)} %fusion.45), kind=kOutput, calls=%fused_computation.39 | convolution fusion | flops 17200840704 | bytes 33570816 | tf_op jit(solution)/shard_map/etf,etd->efd/dot_general | solution.py:205
  1129.8 42.1 %convert_bitcast_fusion = bf16[2,2048,2048]{1,2,0:T(8,128)(2,1)} fusion(bf16[2,2048,1024]{1,2,0:T(8,128)(2,1)} %get-tuple-element.134, bf16[2,2048,1024]{1,2,0:T(8,128)(2,1)} %get-tuple-element.133, bf16[2048,2048]{1,0:T(8,128)(2,1)} %all-gather.15.cloned.1.call-done), kind=kOutput, calls=%fused_computation.9 | convolution fusion | flops 34401681408 | bytes 41943040 | tf_op jit(solution)/shard_map/td,etf->edf/dot_general | solution.py:204
  1173.8 10.8 convolution_convert_fusion.2
  1199.0 17.9 %reduce-scatter.23.cloned.1.call-done = bf16[2,256,2048]{2,1,0:T(8,128)(2,1)} async-done(((bf16[2,1024,2048]{2,1,0:T(8,128)(2,1)}), bf16[2,256,2048]{2,1,0:T(8,128)(2,1)}) %reduce-scatter.23.cloned.1.call-update) | async-done | bytes 2097168 | tf_op jit(solution)/shard_map/reduce_scatter | solution.py:209
  1223.7 122.0 %reduce-scatter.21.cloned.1.call-done = bf16[2,512,2048]{1,2,0:T(8,128)(2,1)} async-done(((bf16[2,2048,2048]{1,2,0:T(8,128)(2,1)}), bf16[2,512,2048]{1,2,0:T(8,128)(2,1)}) %reduce-scatter.21.cloned.1.call-update) | async-done | bytes 4194320 | tf_op jit(solution)/shard_map/reduce_scatter | solution.py:206
  1352.5 145.8 %reduce-scatter.13.cloned.1.call-done = bf16[256,2048]{1,0:T(8,128)(2,1)} async-done(((bf16[2048,2048]{1,0:T(8,128)(2,1)}), bf16[256,2048]{1,0:T(8,128)(2,1)}) %reduce-scatter.13.cloned.1.call-update) | async-done | bytes 1048592 | tf_op jit(solution)/shard_map/reduce_scatter | solution.py:79
  1505.9 40.1 %all-reduce.4 = (f32[16]{0:T(128)S(1)}, f32[2048]{0:T(1024)}, f32[128]{0:T(128)}, f32[128]{0:T(128)}, f32[2048]{0:T(1024)}) all-reduce(f32[16]{0:T(128)S(1)} %copy-done.88, f32[2048]{0:T(1024)S(1)} %get-tuple-element.116, f32[128]{0:T(128)S(1)} %copy-done.91, ...), channel_id=1, replica_groups=mesh['dp'=4,'expert'=8] {'dp','expert'}, use_global_device_ids=true, to_apply=%region_18.19 | all-reduce | flops 4368 | bytes 34944 | tf_op jit(solution)/shard_map/psum | solution.py:296
  1547.3 21.8 %reduce-scatter.19.cloned.1.call-done = bf16[64,2048]{1,0:T(8,128)(2,1)} async-done(((bf16[512,2048]{1,0:T(8,128)(2,1)}), bf16[64,2048]{1,0:T(8,128)(2,1)}) %reduce-scatter.19.cloned.1.call-update) | async-done | bytes 262160 | tf_op jit(solution)/shard_map/reduce_scatter | solution.py:290
  1570.9 126.5 %all-reduce.7.cloned.1.call-done = f32[2048,16]{0,1:T(8,128)} async-done(((f32[2048,16]{0,1:T(8,128)}), f32[2048,16]{0,1:T(8,128)}) %all-reduce.7.cloned.1.call-update) | async-done | bytes 131088 | tf_op jit(solution)/shard_map/psum | solution.py:296
  (324 shorter events, 203.4 us)
Async XLA Ops:
  7.2 550.7 %copy-start = (bf16[2048,16]{0,1:T(8,128)(2,1)S(1)}, bf16[2048,16]{0,1:T(8,128)(2,1)}, u32[]{:S(2)}) copy-start(bf16[2048,16]{0,1:T(8,128)(2,1)} %param.23) | copy-start | bytes 196612
  7.2 62.3 %all-gather.11.cloned.1.call-start = ((), (), s32[]{:S(2)}) async-start(), calls=%async_computation.15 | async-start | bytes 2359296 | tf_op jit(solution)/shard_map/all_gather | solution.py:110
  7.9 91.3 %all-gather.9.cloned.1.call-start = ((), (), s32[]{:S(2)}) async-start(), calls=%async_computation.14 | async-start | bytes 3932160 | tf_op jit(solution)/shard_map/all_gather | solution.py:108
  46.7 180.2 %all-gather.7.cloned.1.call-start = ((), (), s32[]{:S(2)}) async-start(), calls=%async_computation.13 | async-start | bytes 9437184 | tf_op jit(solution)/shard_map/all_gather | solution.py:76
  47.1 299.0 %copy-start.3 = (f32[256,2048]{1,0:T(8,128)}, f32[256,2048]{1,0:T(8,128)S(1)}, u32[]{:S(2)}) copy-start(f32[256,2048]{1,0:T(8,128)S(1)} %reshape.348) | copy-start | bytes 6291460
  50.8 295.4 %all-gather.13.cloned.1.call-start = ((), (), s32[]{:S(2)}) async-start(), calls=%async_computation.16 | async-start | bytes 10485760 | tf_op jit(solution)/shard_map/all_gather | solution.py:109
  69.5 363.1 %all-gather.17.cloned.1.call-start = ((), (), s32[]{:S(2)}) async-start(), calls=%async_computation.19 | async-start | bytes 9437184 | tf_op jit(solution)/shard_map/all_gather | solution.py:76
  70.9 487.0 %all-gather.15.cloned.1.call-start = ((), (), s32[]{:S(2)}) async-start(), calls=%async_computation.17 | async-start | bytes 9437184 | tf_op jit(solution)/shard_map/all_gather | solution.py:76
  71.1 284.1 %copy-start.79 = (s32[2]{0:T(128)}, s32[2]{0:T(128)S(1)}, u32[]{:S(2)}) copy-start(s32[2]{0:T(128)S(1)} %dynamic-slice_reduce_fusion) | copy-start | bytes 28
  71.2 205.3 %copy-start.48 = (pred[2,1024]{1,0:T(4,128)(4,1)}, pred[2,1024]{1,0:T(4,128)(4,1)S(1)}, u32[]{:S(2)}) copy-start(pred[2,1024]{1,0:T(4,128)(4,1)S(1)} %iota_compare_fusion.2) | copy-start | bytes 6148
  354.9 478.1 %reduce-scatter.11.cloned.1.call-start = ((), (), s32[]{:S(2)}) async-start(), calls=%async_computation.20 | async-start | bytes 9437184 | tf_op jit(solution)/shard_map/reduce_scatter | solution.py:79
  684.9 300.2 %reduce-scatter.9.cloned.1.call-start = ((), (), s32[]{:S(2)}) async-start(), calls=%async_computation.18 | async-start | bytes 9437184 | tf_op jit(solution)/shard_map/reduce_scatter | solution.py:79
  739.6 249.6 %copy-start.38 = (f32[256,16]{0,1:T(8,128)}, f32[256,16]{0,1:T(8,128)S(1)}, u32[]{:S(2)}) copy-start(f32[256,16]{0,1:T(8,128)S(1)} %get-tuple-element.161) | copy-start | bytes 49156
  739.6 249.6 %copy-start.64 = (f32[256]{0:T(256)}, f32[256]{0:T(256)S(1)}, u32[]{:S(2)}) copy-start(f32[256]{0:T(256)S(1)} %get-tuple-element.160) | copy-start | bytes 3076
  739.6 245.5 %copy-start.22 = (bf16[256,2048]{1,0:T(8,128)(2,1)S(1)}, bf16[256,2048]{1,0:T(8,128)(2,1)}, u32[]{:S(2)}) copy-start(bf16[256,2048]{1,0:T(8,128)(2,1)} %reshape.337) | copy-start | bytes 3145732
  739.6 10.4 all-to-all-start.2
  743.0 441.7 %reduce-scatter.17.cloned.1.call-start = ((), (), s32[]{:S(2)}) async-start(), calls=%async_computation.23 | async-start | bytes 10485760 | tf_op jit(solution)/shard_map/reduce_scatter | solution.py:291
  743.1 246.1 %copy-start.67 = (f32[256]{0:T(256)}, f32[256]{0:T(256)S(1)}, u32[]{:S(2)}) copy-start(f32[256]{0:T(256)S(1)} %fusion.47) | copy-start | bytes 3076
  790.0 199.1 %copy-start.50 = (f32[256,16]{0,1:T(8,128)}, f32[256,16]{0,1:T(8,128)S(1)}, u32[]{:S(2)}) copy-start(f32[256,16]{0,1:T(8,128)S(1)} %get-tuple-element.128) | copy-start | bytes 49156
  790.0 199.1 %copy-start.77 = (f32[256]{0:T(256)}, f32[256]{0:T(256)S(1)}, u32[]{:S(2)}) copy-start(f32[256]{0:T(256)S(1)} %get-tuple-element.120) | copy-start | bytes 3076
  1005.1 29.4 %all-to-all-start.3 = ((bf16[256,8,256]{2,0,1:T(8,128)(2,1)}), bf16[256,8,256]{2,0,1:T(8,128)(2,1)S(1)}, u32[]{:S(2)}, u32[]{:S(2)}) async-start(bf16[256,8,256]{2,0,1:T(8,128)(2,1)} %bitcast.94), calls=%async_computation.5 | async-start | bytes 2097152 | tf_op jit(solution)/shard_map/all_to_all | solution.py:234
  1008.8 176.6 %reduce-scatter.15.cloned.1.call-start = ((), (), s32[]{:S(2)}) async-start(), calls=%async_computation.22 | async-start | bytes 3932160 | tf_op jit(solution)/shard_map/reduce_scatter | solution.py:274
  1105.5 111.4 %reduce-scatter.23.cloned.1.call-start = ((), (), s32[]{:S(2)}) async-start(), calls=%async_computation.27 | async-start | bytes 10485760 | tf_op jit(solution)/shard_map/reduce_scatter | solution.py:209
  1129.8 215.9 %reduce-scatter.21.cloned.1.call-start = ((), (), s32[]{:S(2)}) async-start(), calls=%async_computation.26 | async-start | bytes 20971520 | tf_op jit(solution)/shard_map/reduce_scatter | solution.py:206
  1172.0 326.3 %reduce-scatter.13.cloned.1.call-start = ((), (), s32[]{:S(2)}) async-start(), calls=%async_computation.21 | async-start | bytes 9437184 | tf_op jit(solution)/shard_map/reduce_scatter | solution.py:79
  1184.7 384.4 %reduce-scatter.19.cloned.1.call-start = ((), (), s32[]{:S(2)}) async-start(), calls=%async_computation.24 | async-start | bytes 2359296 | tf_op jit(solution)/shard_map/reduce_scatter | solution.py:290
  1191.2 29.8 %all-to-all-start.4 = ((bf16[8,64,3,256]{3,1,2,0:T(8,128)(2,1)}), bf16[8,64,3,256]{3,1,2,0:T(8,128)(2,1)}, u32[]{:S(2)}, u32[]{:S(2)}) async-start(bf16[8,64,3,256]{3,1,2,0:T(8,128)(2,1)} %copy.330), calls=%async_computation.8 | async-start | bytes 1572864 | tf_op jit(solution)/shard_map/all_to_all | solution.py:276
  1195.4 502.0 %all-reduce.7.cloned.1.call-start = ((), (), s32[]{:S(2)}) async-start(), calls=%async_computation.25 | async-start | bytes 262144 | tf_op jit(solution)/shard_map/psum | solution.py:296
  1223.7 274.6 %copy-start.4 = (f32[256,2048]{1,0:T(8,128)S(1)}, f32[256,2048]{1,0:T(8,128)}, u32[]{:S(2)}) copy-start(f32[256,2048]{1,0:T(8,128)} %copy-done.3) | copy-start | bytes 6291460
  1223.7 274.6 %copy-start.59 = (f32[2048]{0:T(1024)S(1)}, f32[2048]{0:T(1024)}, u32[]{:S(2)}) copy-start(f32[2048]{0:T(1024)} %param.17) | copy-start | bytes 24580
  1223.7 274.6 %copy-start.70 = (f32[256]{0:T(256)S(1)}, f32[256]{0:T(256)}, u32[]{:S(2)}) copy-start(f32[256]{0:T(256)} %copy-done.69) | copy-start | bytes 3076
  1500.5 198.5 %copy-start.1 = (bf16[2048,16]{0,1:T(8,128)(2,1)S(1)}, bf16[2048,16]{0,1:T(8,128)(2,1)}, u32[]{:S(2)}) copy-start(bf16[2048,16]{0,1:T(8,128)(2,1)} %param.23) | copy-start | bytes 196612
  (80 other events, 1416.9 us)
Sparse Core Ops, SparseCore 0:
  10.2 59.2 all-gather.10
  71.6 27.5 all-gather.8
  102.0 124.9 all-gather.6
  228.3 56.4 all-gather.12
  286.8 145.7 all-gather.16
  434.6 123.2 all-gather.14
  685.1 147.9 reduce-scatter.10
  837.1 147.9 reduce-scatter.8
  996.4 70.7 reduce-scatter.16
  1105.6 36.9 reduce-scatter.14
  1145.1 71.7 reduce-scatter.22
  1219.5 126.1 reduce-scatter.20
  1349.3 148.9 reduce-scatter.12
  1502.1 66.9 reduce-scatter.18
  1576.0 121.3 all-reduce.6

commit v2 on v1

v2 whole, which is shorter than its diff:
```python
import functools
import math

import jax
import jax.numpy as jnp
from jax import lax
from jax.experimental import pallas as pl
from jax.experimental.pallas import tpu as pltpu
from jax.sharding import PartitionSpec as P

HEADS = 16
HD = 128
FF = 1024
TOPK = 8


NORM_EPS = 1e-05
PRECISE = lax.Precision.HIGHEST


def norm_rows(values, scale_gain):
    return (
        values
        * lax.rsqrt(jnp.mean(values * values, axis=-1, keepdims=True) + NORM_EPS)
        * scale_gain
    )


VMEM_BYTES = 56 * 1024 * 1024
TILE = 256
WIDE = 512


def params():
    return pltpu.CompilerParams(vmem_limit_bytes=VMEM_BYTES)


def dot_nn(left, right):
    return jnp.dot(left, right, preferred_element_type=jnp.float32)


def dot_nt(left, right):
    return lax.dot_general(
        left, right, (((1,), (1,)), ((), ())), preferred_element_type=jnp.float32
    )


def dot_tn(left, right):
    return lax.dot_general(
        left, right, (((0,), (0,)), ((), ())), preferred_element_type=jnp.float32
    )


def turn(values, cosine, sine):
    return values * cosine + pltpu.roll(values, HD // 2, 1) * sine


def turn_back(values, cosine, sine):
    return values * cosine + pltpu.roll(values * sine, HD // 2, 1)


def head_norm(proj):
    return lax.rsqrt(jnp.mean(proj * proj, axis=-1, keepdims=True) + NORM_EPS)


def load_heads(proj_ref, cos_ref, sin_ref, gain_ref):
    rows = cos_ref.shape[0]
    proj = proj_ref[...].reshape(rows, 3 * HD)
    cosine, sine = cos_ref[...], sin_ref[...]
    q_proj, k_proj, v_proj = proj[:, :HD], proj[:, HD : 2 * HD], proj[:, 2 * HD :]
    queries = turn(q_proj * head_norm(q_proj) * gain_ref[0:1], cosine, sine).astype(jnp.bfloat16)
    keys = turn(k_proj * head_norm(k_proj) * gain_ref[1:2], cosine, sine).astype(jnp.bfloat16)
    return q_proj, k_proj, queries, keys, v_proj.astype(jnp.bfloat16)


def row_probs(queries, keys, live):
    scores = jnp.where(live, dot_nt(queries, keys), -1e30)
    expo = jnp.exp((scores - jnp.max(scores, axis=-1, keepdims=True)) * (1.0 / math.sqrt(HD)))
    return expo * (1.0 / jnp.sum(expo, axis=-1, keepdims=True))


def attend_kernel(
    owner_ref, proj_ref, cos_ref, sin_ref, live_ref, gain_ref, out_ref, q_scr, o_scr
):
    rows, slots = cos_ref.shape[0], proj_ref.shape[2]
    step = min(TILE, rows)
    _, _, queries, keys, values = load_heads(proj_ref, cos_ref, sin_ref, gain_ref)
    q_scr[...] = queries
    live = live_ref[0] > 0.0

    def chunk(i, carry):
        part = pl.ds(pl.multiple_of(i * step, step), step)
        probs = row_probs(q_scr[part, :], keys, live).astype(jnp.bfloat16)
        o_scr[part, :] = dot_nn(probs, values).astype(jnp.bfloat16)
        return carry

    lax.fori_loop(0, rows // step, chunk, 0, unroll=True)
    for r in range(proj_ref.shape[0]):
        out_ref[owner_ref[r], 0] = o_scr[r * slots : (r + 1) * slots, :]


def attend(owners, proj, cosine, sine, live, gains):
    blocks, seqs, slots, width = proj.shape
    heads, rows = width // (3 * HD), blocks * slots
    return pl.pallas_call(
        attend_kernel,
        grid_spec=pltpu.PrefetchScalarGridSpec(
            num_scalar_prefetch=1,
            grid=(seqs, heads),
            in_specs=[
                pl.BlockSpec((blocks, 1, slots, 3 * HD), lambda s, h, o: (0, s, 0, h)),
                pl.BlockSpec((rows, HD), lambda s, h, o: (0, 0)),
                pl.BlockSpec((rows, HD), lambda s, h, o: (0, 0)),
                pl.BlockSpec((1, 1, rows), lambda s, h, o: (s, 0, 0)),
                pl.BlockSpec((2, HD), lambda s, h, o: (0, 0)),
            ],
            out_specs=pl.BlockSpec((blocks, 1, slots, HD), lambda s, h, o: (0, s, 0, h)),
            scratch_shapes=[pltpu.VMEM((rows, HD), jnp.bfloat16)] * 2,
        ),
        out_shape=jax.ShapeDtypeStruct((blocks, seqs, slots, heads * HD), jnp.bfloat16),
        compiler_params=params(),
        cost_estimate=pl.CostEstimate(
            flops=4 * seqs * heads * rows * rows * HD,
            bytes_accessed=seqs * rows * width * 5,
            transcendentals=seqs * heads * rows * rows,
        ),
        name="attend",
    )(owners, proj, cosine, sine, live, gains)


def attend_back_kernel(
    owner_ref, proj_ref, grad_ref, cos_ref, sin_ref, live_ref, gain_ref, out_ref, gain_out, q_scr, dq, dk, dv
):
    rows, slots = cos_ref.shape[0], proj_ref.shape[2]
    step = min(TILE, rows)
    scale = 1.0 / math.sqrt(HD)
    q_proj, k_proj, queries, keys, values = load_heads(proj_ref, cos_ref, sin_ref, gain_ref)
    q_scr[0] = queries
    for r in range(proj_ref.shape[0]):
        q_scr[1, r * slots : (r + 1) * slots, :] = grad_ref[owner_ref[r], 0]
    dk[...] = jnp.zeros_like(dk)
    dv[...] = jnp.zeros_like(dv)
    live = live_ref[0] > 0.0

    def chunk(i, carry):
        part = pl.ds(pl.multiple_of(i * step, step), step)
        q_part, g_part = q_scr[0, part, :], q_scr[1, part, :]
        probs = row_probs(q_part, keys, live)
        prob_grad = dot_nt(g_part, values)
        row_dot = jnp.sum(probs * prob_grad, axis=-1, keepdims=True)
        score_grad = (probs * (prob_grad - row_dot)).astype(jnp.bfloat16)
        dq[part, :] = dot_nn(score_grad, keys)
        dk[...] += dot_tn(score_grad, q_part)
        dv[...] += dot_tn(probs.astype(jnp.bfloat16), g_part)
        return carry

    lax.fori_loop(0, rows // step, chunk, 0, unroll=True)
    cosine, sine = cos_ref[...], sin_ref[...]
    parts = []
    for i, (proj, grad) in enumerate(((q_proj, dq), (k_proj, dk))):
        gain, inverse = gain_ref[i : i + 1], head_norm(proj)
        back = turn_back(grad[...] * scale, cosine, sine)
        scaled = proj * inverse
        gain_out[0, 0, i : i + 1, :] = jnp.sum(back * scaled, axis=0, keepdims=True)
        back = back * gain
        parts.append(
            inverse * (back - scaled * jnp.mean(scaled * back, axis=-1, keepdims=True))
        )
    grads = jnp.concatenate(parts + [dv[...]], axis=1).astype(jnp.bfloat16)
    out_ref[...] = grads.reshape(out_ref.shape)


def attend_back(owners, proj, grads, cosine, sine, live, gains):
    blocks, seqs, slots, width = proj.shape
    heads, rows = width // (3 * HD), blocks * slots
    return pl.pallas_call(
        attend_back_kernel,
        grid_spec=pltpu.PrefetchScalarGridSpec(
            num_scalar_prefetch=1,
            grid=(seqs, heads),
            in_specs=[
                pl.BlockSpec((blocks, 1, slots, 3 * HD), lambda s, h, o: (0, s, 0, h)),
                pl.BlockSpec((blocks, 1, slots, HD), lambda s, h, o: (0, s, 0, h)),
                pl.BlockSpec((rows, HD), lambda s, h, o: (0, 0)),
                pl.BlockSpec((rows, HD), lambda s, h, o: (0, 0)),
                pl.BlockSpec((1, 1, rows), lambda s, h, o: (s, 0, 0)),
                pl.BlockSpec((2, HD), lambda s, h, o: (0, 0)),
            ],
            out_specs=[
                pl.BlockSpec((blocks, 1, slots, 3 * HD), lambda s, h, o: (0, s, 0, h)),
                pl.BlockSpec((1, 1, 2, HD), lambda s, h, o: (s, h, 0, 0)),
            ],
            scratch_shapes=[pltpu.VMEM((2, rows, HD), jnp.bfloat16)]
            + [pltpu.VMEM((rows, HD), jnp.float32)] * 3,
        ),
        out_shape=[
            jax.ShapeDtypeStruct(proj.shape, jnp.bfloat16),
            jax.ShapeDtypeStruct((seqs, heads, 2, HD), jnp.float32),
        ],
        compiler_params=params(),
        cost_estimate=pl.CostEstimate(
            flops=10 * seqs * heads * rows * rows * HD,
            bytes_accessed=seqs * rows * width * 7,
            transcendentals=seqs * heads * rows * rows,
        ),
        name="attend_back",
    )(owners, proj, grads, cosine, sine, live, gains)


def gate_column(gates_ref, index):
    gates = gates_ref[...]
    out = jnp.zeros((gates.shape[0], 1), jnp.float32)
    for e in range(gates.shape[1]):
        out = out + jnp.where(index == e, gates[:, e : e + 1], 0.0)
    return out


def fill_rows(refs, out_ref):
    base = 0
    for ref in refs:
        out_ref[base : base + ref.shape[0], :] = ref[...]
        base += ref.shape[0]


def experts_kernel(parts, held, tiles, per, count, *refs):
    x_refs, refs = refs[:parts], refs[parts:]
    hits_ref, router_ref, own_ref, gate_w, up_w, down_w = refs[:6]
    rows, gate_out, up_out, gated_out, gates_ref, mix_out, gated = refs[6 + held :]
    i = pl.program_id(0)

    @pl.when(i == 0)
    def _():
        fill_rows(x_refs, rows)
        logits = dot_nn(rows[...], router_ref[...])
        hits = hits_ref[...]
        lane = lax.broadcasted_iota(jnp.int32, logits.shape, 1)
        logits = jnp.where(lane < count, logits, -1e30)
        expo = jnp.exp(logits - jnp.max(logits, axis=1, keepdims=True))
        picked = jnp.where(lane < count, hits * expo / jnp.sum(expo, axis=1, keepdims=True), 0.0)
        live = jnp.sum(jnp.where(lane == count, hits, 0.0), axis=1, keepdims=True)
        gates = live * picked / jnp.sum(picked, axis=1, keepdims=True)
        for e in range(gates_ref.shape[1]):
            gates_ref[:, e : e + 1] = jnp.sum(gates * own_ref[e : e + 1], axis=1, keepdims=True)

    @pl.when(i < tiles)
    def _():
        gate = dot_nn(rows[...], gate_w[0])
        up = dot_nn(rows[...], up_w[0])
        hidden = gate / (1.0 + jnp.exp(-gate)) * up * gate_column(gates_ref, i // per)
        gate_out[...] = gate.astype(jnp.bfloat16)
        up_out[...] = up.astype(jnp.bfloat16)
        low = hidden.astype(jnp.bfloat16)
        gated_out[...] = low
        gated[:, pl.ds(pl.multiple_of(i * WIDE, WIDE), WIDE)] = low

    @pl.when(i >= tiles)
    def _():
        mix_out[...] = dot_nn(gated[...], down_w[...]).astype(jnp.bfloat16)


def experts_forward(xs, hits, router, own, count, w_in, w_down, held, base, total):
    experts, width, _ = w_in.shape
    hidden = w_down.shape[0]
    rows = sum(x.shape[0] for x in xs)
    place = base // rows
    tiles, per, outs = hidden // WIDE, FF // WIDE, width // WIDE
    clamp = lambda i: jnp.minimum(i, tiles - 1)
    later = lambda i: jnp.maximum(i - tiles, 0)
    keep = pl.BlockSpec((rows, WIDE), lambda i: (place, clamp(i)))
    known = len(xs) + 6
    lanes = router.shape[1]
    return pl.pallas_call(
        functools.partial(experts_kernel, len(xs), len(held), tiles, per, count),
        grid=(tiles + outs,),
        in_specs=[pl.BlockSpec(x.shape, lambda i: (0, 0)) for x in xs]
        + [
            pl.BlockSpec((rows, lanes), lambda i: (0, 0)),
            pl.BlockSpec((width, lanes), lambda i: (0, 0)),
            pl.BlockSpec((experts, lanes), lambda i: (0, 0)),
            pl.BlockSpec((1, width, WIDE), lambda i: (clamp(i) // per, 0, clamp(i) % per)),
            pl.BlockSpec((1, width, WIDE), lambda i: (clamp(i) // per, 0, per + clamp(i) % per)),
            pl.BlockSpec((hidden, WIDE), lambda i: (0, later(i))),
        ]
        + [pl.BlockSpec(memory_space=pl.ANY)] * len(held),
        out_specs=[pl.BlockSpec((rows, width), lambda i: (place, 0))]
        + [keep] * 3
        + [
            pl.BlockSpec((rows, experts), lambda i: (0, 0)),
            pl.BlockSpec((rows, WIDE), lambda i: (0, later(i))),
        ],
        out_shape=[jax.ShapeDtypeStruct((total, width), jnp.bfloat16)]
        + [jax.ShapeDtypeStruct((total, hidden), jnp.bfloat16)] * 3
        + [
            jax.ShapeDtypeStruct((rows, experts), jnp.float32),
            jax.ShapeDtypeStruct((rows, width), jnp.bfloat16),
        ],
        scratch_shapes=[pltpu.VMEM((rows, hidden), jnp.bfloat16)],
        input_output_aliases={known + i: i for i in range(len(held))},
        compiler_params=params(),
        cost_estimate=pl.CostEstimate(
            flops=6 * rows * hidden * width,
            bytes_accessed=6 * hidden * width + 10 * rows * width,
            transcendentals=rows * hidden,
        ),
        name="experts_forward",
    )(*xs, hits, router, own, w_in, w_in, w_down, *held)


def experts_back_kernel(parts, held, tiles, per, *refs):
    c_refs, refs = refs[:parts], refs[parts:]
    gates_ref, own_ref, gate_ref, up_ref, down_w, in_w = refs[:6]
    rows, gate_out, up_out, score_out, grad_out, gate_grads, up_grads = refs[6 + held :]
    i = pl.program_id(0)

    @pl.when(i == 0)
    def _():
        fill_rows(c_refs, rows)

    @pl.when(i < tiles)
    def _():
        raw = dot_nt(rows[...], down_w[...])
        gate, up = gate_ref[...].astype(jnp.float32), up_ref[...].astype(jnp.float32)
        sigmoid = 1.0 / (1.0 + jnp.exp(-gate))
        silu = gate * sigmoid
        score = jnp.sum(silu * up * raw, axis=1, keepdims=True)
        own = own_ref[...]
        place = sum(jnp.where(i // per == e, own[e : e + 1], 0.0) for e in range(own.shape[0]))
        mine = score * place
        score_out[...] = jnp.where(i == 0, mine, score_out[...] + mine)
        grad = raw * gate_column(gates_ref, i // per)
        gate_low = (grad * up * (sigmoid + silu * (1.0 - sigmoid))).astype(jnp.bfloat16)
        up_low = (grad * silu).astype(jnp.bfloat16)
        gate_out[...] = gate_low
        up_out[...] = up_low
        part = pl.ds(pl.multiple_of(i * WIDE, WIDE), WIDE)
        gate_grads[:, part] = gate_low
        up_grads[:, part] = up_low

    @pl.when(i >= tiles)
    def _():
        total = 0.0
        for e in range(in_w.shape[0]):
            part = slice(e * FF, (e + 1) * FF)
            total = total + dot_nt(gate_grads[:, part], in_w[e, :, :FF])
            total = total + dot_nt(up_grads[:, part], in_w[e, :, FF:])
        grad_out[...] = total.astype(jnp.bfloat16)


def experts_backward(outs, gates, own, gate, up, w_in, w_down, held, base):
    experts, width, _ = w_in.shape
    hidden, total = w_down.shape[0], gate.shape[0]
    rows = sum(o.shape[0] for o in outs)
    place = base // rows
    tiles, per, last = hidden // WIDE, FF // WIDE, width // WIDE
    clamp = lambda i: jnp.minimum(i, tiles - 1)
    later = lambda i: jnp.maximum(i - tiles, 0)
    keep = pl.BlockSpec((rows, WIDE), lambda i: (place, clamp(i)))
    known, lanes = len(outs) + 6, own.shape[1]
    return pl.pallas_call(
        functools.partial(experts_back_kernel, len(outs), len(held), tiles, per),
        grid=(tiles + last,),
        in_specs=[pl.BlockSpec(o.shape, lambda i: (0, 0)) for o in outs]
        + [
            pl.BlockSpec((rows, experts), lambda i: (0, 0)),
            pl.BlockSpec((experts, lanes), lambda i: (0, 0)),
            keep,
            keep,
            pl.BlockSpec((WIDE, width), lambda i: (clamp(i), 0)),
            pl.BlockSpec((experts, WIDE, 2 * FF), lambda i: (0, later(i), 0)),
        ]
        + [pl.BlockSpec(memory_space=pl.ANY)] * len(held),
        out_specs=[
            pl.BlockSpec((rows, width), lambda i: (place, 0)),
            keep,
            keep,
            pl.BlockSpec((rows, lanes), lambda i: (0, 0)),
            pl.BlockSpec((rows, WIDE), lambda i: (0, later(i))),
        ],
        out_shape=[jax.ShapeDtypeStruct((total, width), jnp.bfloat16)]
        + [jax.ShapeDtypeStruct((total, hidden), jnp.bfloat16)] * 2
        + [
            jax.ShapeDtypeStruct((rows, lanes), jnp.float32),
            jax.ShapeDtypeStruct((rows, width), jnp.bfloat16),
        ],
        scratch_shapes=[pltpu.VMEM((rows, hidden), jnp.bfloat16)] * 2,
        input_output_aliases={known + i: i for i in range(len(held))},
        compiler_params=params(),
        cost_estimate=pl.CostEstimate(
            flops=6 * rows * hidden * width,
            bytes_accessed=6 * hidden * width + 12 * rows * width,
            transcendentals=rows * hidden,
        ),
        name="experts_backward",
    )(*outs, gates, own, gate, up, w_down, w_in, *held)


def ring_order(size):
    return list(range(0, size, 2)) + list(range(size - 1, 0, -2))


def ring_shift(rows, order, step):
    size = len(order)
    pairs = [(order[i], order[(i + step) % size]) for i in range(size)]
    return lax.ppermute(rows, "expert", pairs)


class Gather:
    def __init__(self, rows, order):
        self.order, self.half, self.done = order, len(order) // 2, 0
        self.blocks = {0: rows}

    def step(self, *waits):
        self.done = s = self.done + 1
        ahead, back = self.blocks[1 - s], self.blocks[s - 1]
        if s == self.half:
            cut = ahead.shape[0] // 2
            ahead, back = ahead[:cut], back[cut:]
        if waits:
            ahead, back = lax.optimization_barrier((ahead, back, *waits))[:2]
        ahead, back = ring_shift(ahead, self.order, 1), ring_shift(back, self.order, -1)
        if s == self.half:
            self.blocks[s] = jnp.concatenate([ahead, back], axis=0)
        else:
            self.blocks[-s], self.blocks[s] = ahead, back


class Scatter:
    def __init__(self, far, order, *waits):
        self.order, self.cut, self.first = order, far.shape[0] // 2, True
        self.send(far[: self.cut], far[self.cut :], waits)

    def send(self, ahead, back, waits):
        ahead, back = ahead.astype(jnp.bfloat16), back.astype(jnp.bfloat16)
        if waits:
            ahead, back = lax.optimization_barrier((ahead, back, *waits))[:2]
        self.ahead = ring_shift(ahead, self.order, 1).astype(jnp.float32)
        self.back = ring_shift(back, self.order, -1).astype(jnp.float32)

    def step(self, mine, other, *waits):
        mine, other = mine.astype(jnp.float32), other.astype(jnp.float32)
        if self.first:
            cut, self.first = self.cut, False
            mine = jnp.concatenate([mine[:cut] + self.ahead, mine[cut:]], axis=0)
            other = jnp.concatenate([other[:cut], other[cut:] + self.back], axis=0)
        else:
            mine, other = mine + self.ahead, other + self.back
        self.send(mine, other, waits)

    def finish(self, own):
        return own.astype(jnp.float32) + self.ahead + self.back


def offsets_of(size):
    half = size // 2
    out = [0]
    for step in range(1, half):
        out += [-step, step]
    return out + [half]


def sum_over(values, axis):
    size, step = lax.axis_size(axis), 1
    while step < size:
        values = values + lax.ppermute(values, axis, [(i, i ^ step) for i in range(size)])
        step *= 2
    return values


def gather_small(rows, axis):
    size, step, me = lax.axis_size(axis), 1, lax.axis_index(axis)
    while step < size:
        other = lax.ppermute(rows, axis, [(i, i ^ step) for i in range(size)])
        upper = (me // step) % 2 == 1
        rows = jnp.concatenate(
            [jnp.where(upper, other, rows), jnp.where(upper, rows, other)], axis=0
        )
        step *= 2
    return rows


def after(values, *others):
    return lax.optimization_barrier((values, *others))[0]


def weight_kernel(parts, adds, index_ref, *refs):
    left_refs, right_ref, refs = refs[:parts], refs[parts], refs[parts + 1 :]
    add_refs, out_ref, left = refs[: adds * parts], refs[-2], refs[-1]
    tile = left_refs[0].shape[1]

    @pl.when(pl.program_id(0) == 0)
    def _():
        for p, ref in enumerate(left_refs):
            left[p * tile : (p + 1) * tile, :] = ref[...].T

    total = dot_nn(left[...], right_ref[...])
    for p in range(parts):
        part = total[p * tile : (p + 1) * tile]
        for a in range(adds):
            part = part + add_refs[a * parts + p][...].astype(jnp.float32)
        out_ref[p * tile : (p + 1) * tile, :] = part.astype(out_ref.dtype)


def weight_part(left, right, tile, columns, adds, dtype, name):
    rows, width, wide = left.shape[0], right.shape[1], WIDE
    parts = len(columns)
    places = list(columns) + [t for _, tiles in adds for t in tiles]
    in_specs = [
        pl.BlockSpec((rows, tile), lambda j, at, p=p: (0, at[p])) for p in range(parts)
    ] + [pl.BlockSpec((rows, wide), lambda j, at: (0, j))]
    in_specs += [
        pl.BlockSpec((tile, wide), lambda j, at, p=p: (at[p], j))
        for p in range(parts, len(places))
    ]
    return pl.pallas_call(
        functools.partial(weight_kernel, parts, len(adds)),
        grid_spec=pltpu.PrefetchScalarGridSpec(
            num_scalar_prefetch=1,
            grid=(width // wide,),
            in_specs=in_specs,
            out_specs=pl.BlockSpec((parts * tile, wide), lambda j, at: (0, j)),
            scratch_shapes=[pltpu.VMEM((parts * tile, rows), jnp.bfloat16)],
        ),
        out_shape=jax.ShapeDtypeStruct((parts * tile, width), dtype),
        compiler_params=params(),
        cost_estimate=pl.CostEstimate(
            flops=2 * rows * parts * tile * width,
            bytes_accessed=2 * rows * (parts * tile + width) + 4 * parts * tile * width,
            transcendentals=0,
        ),
        name=name,
    )(
        jnp.stack([jnp.asarray(p, jnp.int32) for p in places]),
        *[left] * parts,
        right,
        *[a for a, tiles in adds for _ in tiles],
    )


class GroupSum:
    def __init__(self, left, right, outer, name):
        self.left, self.right, self.outer, self.name = left, right, outer, name
        self.size = lax.axis_size("dp")
        me = lax.axis_index("dp")
        self.core, self.pair = me % 2, me // 2
        self.tile = left.shape[1] // outer // self.size

    def tiles(self, core, pairs):
        return [4 * o + 2 * pair + core for o in range(self.outer) for pair in pairs]

    def part(self, columns, adds, dtype, waits):
        left = after(self.left, *waits) if waits else self.left
        return weight_part(left, self.right, self.tile, columns, adds, dtype, self.name)

    def first(self, *waits):
        if self.size != 4:
            left = after(self.left, *waits) if waits else self.left
            terms = dot_tn(left, self.right).astype(jnp.bfloat16)
            terms = terms.reshape(self.outer, -1, terms.shape[1])
            self.far = lax.psum_scatter(terms, "dp", scatter_dimension=1, tiled=True)
            return
        columns = self.tiles(1 - self.core, (0, 1))
        self.far = self.part(columns, [], jnp.bfloat16, waits)
        self.got = lax.ppermute(self.far, "dp", [(i, i ^ 1) for i in range(4)])

    def halves(self, pair):
        return [2 * o + pair for o in range(self.outer)]

    def second(self, *waits):
        if self.size != 4:
            return
        other = 1 - self.pair
        terms = self.part(
            self.tiles(self.core, (other,)),
            [(self.got, self.halves(other))],
            jnp.bfloat16,
            waits,
        )
        self.near = lax.ppermute(terms, "dp", [(i, i ^ 2) for i in range(4)])

    def third(self, *waits):
        if self.size != 4:
            return self.far.reshape(-1, self.far.shape[-1]).astype(jnp.float32)
        return self.part(
            self.tiles(self.core, (self.pair,)),
            [(self.got, self.halves(self.pair)), (self.near, range(self.outer))],
            jnp.float32,
            waits,
        )


def body(
    tokens,
    lengths,
    routes,
    attn_gain,
    q_gain,
    k_gain,
    qkv_weight,
    out_weight,
    ffn_gain,
    router_weight,
    expert_in,
    expert_out,
    balance_coef,
    cotangent,
):
    bf16, f32 = jnp.bfloat16, jnp.float32
    n_expert = lax.axis_size("expert")
    group_index = lax.axis_index("dp")
    member = lax.axis_index("expert")
    slot_count = tokens.shape[1]
    seq_count = tokens.shape[2]
    width = tokens.shape[3]
    experts_here = expert_in.shape[0]
    experts_all = experts_here * n_expert
    tok_rows = slot_count * seq_count
    full_len = slot_count * n_expert
    heads_here = HEADS // n_expert
    cols = heads_here * HD

    order = ring_order(n_expert)
    offsets = offsets_of(n_expert)
    half = n_expert // 2
    table = [[order[(order.index(m) + r) % n_expert] for r in offsets] for m in range(n_expert)]
    owners = lax.dynamic_index_in_dim(jnp.array(table, jnp.int32), member, 0, False)
    owner = {r: owners[i] for i, r in enumerate(offsets)}

    def blockwise(blocks, axis=0):
        return jnp.concatenate([blocks[r] for r in offsets], axis=axis)

    def to_rows(values):
        return jnp.swapaxes(values[0], 0, 1).reshape(tok_rows, values.shape[3])

    def from_rows(rows):
        return jnp.swapaxes(rows.reshape(seq_count, slot_count, width), 0, 1)[None]

    seq_lens = lengths[group_index]
    slot_ids = member * slot_count + jnp.arange(slot_count)
    valid_rows = (slot_ids[None, :] < seq_lens[:, None]).astype(f32).reshape(tok_rows)
    all_slots = (owners[:, None] * slot_count + jnp.arange(slot_count)[None, :]).reshape(full_len)
    key_live = (all_slots[None, :] < seq_lens[:, None]).astype(f32)[:, None, :]
    inv_freq = jnp.exp(
        jnp.arange(HD // 2, dtype=f32) * (-2.0 * math.log(10000.0) / HD)
    )
    angles = all_slots.astype(f32)[:, None] * inv_freq[None, :]
    cosine, sine = jnp.cos(angles), jnp.sin(angles)
    cosine = jnp.concatenate([cosine, cosine], axis=1)
    sine = jnp.concatenate([-sine, sine], axis=1)
    head_gains = jnp.stack([q_gain, k_gain])

    inputs = to_rows(tokens).astype(f32)
    normed = norm_rows(inputs, attn_gain)
    normed_ring = Gather(normed.astype(bf16), order)
    normed_ring.step()

    row_count = qkv_weight.shape[0]
    w_cols = qkv_weight.reshape(row_count, 3, n_expert, heads_here, HD).transpose(2, 0, 3, 1, 4)
    w_cols = lax.all_to_all(
        after(w_cols.reshape(n_expert, row_count, 3 * cols), normed_ring.blocks[1]),
        "expert",
        split_axis=0,
        concat_axis=0,
        tiled=True,
    )
    w_qkv = lax.all_gather(w_cols.reshape(-1, 3 * cols), "dp", axis=0, tiled=True)
    w_out = lax.all_gather(out_weight, "expert", axis=0, tiled=True)
    for _ in range(half - 1):
        normed_ring.step()
    normed_all = blockwise(normed_ring.blocks)
    w_out = lax.all_gather(after(w_out, normed_all), "dp", axis=0, tiled=True)
    cot_rows = to_rows(cotangent)
    cot_ring = Gather(cot_rows, order)
    cot_ring.step(normed_all)

    picked_ids = to_rows(routes)
    chosen = jnp.sum(
        (picked_ids[:, :, None] == jnp.arange(experts_all)[None, None, :]).astype(f32), axis=1
    )
    lanes = 128
    hits = jnp.concatenate([chosen, valid_rows[:, None]], axis=1).T
    hits = jnp.pad(hits, ((0, -hits.shape[0] % 16), (0, 0))).astype(bf16)
    hits_all = gather_small(hits[None], "expert")
    hits_of = {
        r: jnp.pad(
            lax.dynamic_index_in_dim(hits_all, owner[r], 0, False).T.astype(f32),
            ((0, 0), (0, lanes - hits.shape[0])),
        )
        for r in offsets
    }
    router_pad = jnp.pad(router_weight, ((0, 0), (0, lanes - experts_all)))
    own_ids = member * experts_here + jnp.arange(experts_here)
    own_rows = (own_ids[:, None] == jnp.arange(lanes)[None, :]).astype(f32)
    n_valid = jnp.sum(lengths).astype(f32)
    count_total = sum_over(
        sum_over(jnp.sum(valid_rows[:, None] * chosen, axis=0), "expert"), "dp"
    )
    fraction = count_total / (TOPK * n_valid)

    project = dot_nn(normed_all, w_qkv).reshape(n_expert, seq_count, slot_count, 3 * cols)
    cot_ring.step(project)
    attended = attend(owners, project, cosine, sine, key_live, head_gains)
    attended_low = lax.all_to_all(
        attended.reshape(n_expert, tok_rows, cols), "expert", split_axis=0, concat_axis=0, tiled=True
    )
    attended_low = jnp.swapaxes(attended_low, 0, 1).reshape(tok_rows, width)
    for _ in range(half - 3):
        cot_ring.step(attended_low)
    residual = inputs + dot_nn(attended_low, w_out)
    ffn_normed, ffn_back = jax.vjp(norm_rows, residual, ffn_gain)
    ffn_low = ffn_normed.astype(bf16)
    ffn_ring = Gather(ffn_low, order)
    ffn_ring.step()

    live = valid_rows[:, None]
    router_probs = jax.nn.softmax(dot_nn(ffn_low, router_weight), axis=-1)
    picked = chosen * router_probs
    picked_total = jnp.sum(picked, axis=-1, keepdims=True)
    prob_sums = jnp.sum(live * router_probs, axis=0)
    groups = [[0]] + [[-s, s] for s in range(1, half)] + [[half]]
    bases = [(n_expert - 2) * tok_rows]
    bases += [2 * s * tok_rows for s in range(half - 1)] + [(n_expert - 1) * tok_rows]
    w_down = expert_out.reshape(experts_here * FF, width)
    all_rows = n_expert * tok_rows

    def split(rows, group):
        return {r: rows[i * tok_rows : (i + 1) * tok_rows] for i, r in enumerate(group)}

    held, mix_blocks, group_gates = [], {}, []
    for i, g in enumerate(groups):
        *held, gates, mixed = experts_forward(
            [ffn_ring.blocks[r] for r in g],
            jnp.concatenate([hits_of[r] for r in g], axis=0),
            router_pad,
            own_rows,
            experts_all,
            expert_in,
            w_down,
            held,
            bases[i],
            all_rows,
        )
        group_gates.append(gates)
        mix_blocks.update(split(mixed, g))
        if i < half - 1:
            ffn_ring.step(mixed)
        if i == 1:
            cot_ring.step(mixed)
    x_all, gate_all, up_all, gated_all = held
    held, ffn_sum = [], None
    for i in reversed(range(len(groups))):
        g = groups[i]
        *held, scores, grads = experts_backward(
            [cot_ring.blocks[r] for r in g],
            group_gates[i],
            own_rows,
            gate_all,
            up_all,
            expert_in,
            w_down,
            held,
            bases[i],
        )
        grads = jnp.concatenate([grads, scores.astype(bf16)], axis=1)
        if i == half:
            ffn_sum = Scatter(grads, order)
        elif i > 0:
            ffn_sum.step(grads[tok_rows:], grads[:tok_rows])
    out_all, gate_grad_all, up_grad_all = held
    ffn_grad = ffn_sum.finish(grads)
    gate_grads = ffn_grad[:, width : width + experts_all] * chosen
    ffn_grad = ffn_grad[:, :width]
    mix_sum = Scatter(mix_blocks[half], order, ffn_grad)
    picked_grad = (
        live
        * chosen
        * (
            gate_grads / picked_total
            - jnp.sum(gate_grads * picked, axis=-1, keepdims=True) / (picked_total * picked_total)
        )
    )
    prob_grad = picked_grad + balance_coef * experts_all * fraction[None, :] / n_valid * live
    logit_grad = router_probs * (
        prob_grad - jnp.sum(router_probs * prob_grad, axis=-1, keepdims=True)
    )
    ffn_grad = ffn_grad + jnp.dot(logit_grad, router_weight.astype(f32).T, precision=PRECISE)
    router_terms = jnp.dot(ffn_low.astype(f32).T, logit_grad, precision=PRECISE)
    residual_norm_grad, ffn_gain_terms = ffn_back(ffn_grad)
    residual_grad = cot_rows.astype(f32) * live + residual_norm_grad
    branch_grad = residual_grad.astype(bf16)

    attended_grad = dot_nt(branch_grad, w_out).astype(bf16)
    mix_sum.step(mix_blocks[half - 1], mix_blocks[1 - half], attended_grad)
    attended_grad = lax.all_to_all(
        jnp.swapaxes(attended_grad.reshape(tok_rows, n_expert, cols), 0, 1),
        "expert",
        split_axis=0,
        concat_axis=0,
        tiled=True,
    ).reshape(attended.shape)

    output_terms = dot_tn(attended_low, branch_grad).astype(bf16)
    grad_out = lax.psum_scatter(
        lax.psum_scatter(output_terms, "dp", scatter_dimension=0, tiled=True),
        "expert",
        scatter_dimension=0,
        tiled=True,
    ).astype(f32)
    sums = [
        GroupSum(gated_all, out_all, experts_here, "weights_out"),
        GroupSum(x_all, gate_grad_all, 1, "weights_gate"),
        GroupSum(x_all, up_grad_all, 1, "weights_up"),
    ]
    sums[0].first(branch_grad)
    attended_grad = after(attended_grad, sums[0].far)

    proj_grad, gain_parts = attend_back(
        owners, project, attended_grad, cosine, sine, key_live, head_gains
    )
    for s in range(half - 2, 0, -1):
        mix_sum.step(mix_blocks[s], mix_blocks[-s], proj_grad if s == 1 else attended_grad)
    proj_grad = proj_grad.reshape(all_rows, 3 * cols)
    normed_terms = dot_nt(proj_grad, w_qkv).astype(bf16)
    normed_parts = {
        r: normed_terms[i * tok_rows : (i + 1) * tok_rows] for i, r in enumerate(offsets)
    }
    normed_sum = Scatter(normed_parts[half], order)
    proj_terms = dot_tn(after(normed_all, normed_terms), proj_grad).astype(bf16)
    proj_share = lax.psum_scatter(proj_terms, "dp", scatter_dimension=0, tiled=True)
    sums[0].second(proj_terms)
    sums[1].first(proj_terms)
    for s in range(half - 1, 0, -1):
        normed_sum.step(normed_parts[s], normed_parts[-s])
        if s == half - 1:
            sums[2].first(normed_sum.ahead, sums[1].far)
            sums[1].second(sums[2].far)
        if s == half - 2:
            sums[2].second(normed_sum.ahead)
    normed_grad = normed_sum.finish(normed_parts[0])
    (input_norm_grad,) = jax.vjp(lambda v: norm_rows(v, attn_gain), inputs)[1](normed_grad)
    grad_tokens = from_rows(residual_grad + input_norm_grad)
    block_out = from_rows(residual + mix_sum.finish(mix_blocks[0]))
    grad_expert_out = sums[0].third(normed_sum.ahead).reshape(experts_here, -1, width)
    shares = [sums[1].third(normed_sum.ahead), sums[2].third(normed_sum.ahead)]
    grad_expert_in = jnp.stack(
        [
            jnp.concatenate([s[:, e * FF : (e + 1) * FF] for s in shares], axis=1)
            for e in range(experts_here)
        ]
    )

    grad_qkv = lax.all_to_all(
        proj_share.reshape(n_expert, row_count, 3 * cols),
        "expert",
        split_axis=0,
        concat_axis=0,
        tiled=True,
    ).reshape(n_expert, row_count, heads_here, 3, HD)
    grad_qkv = grad_qkv.transpose(1, 3, 0, 2, 4).reshape(row_count, 3, width).astype(f32)

    early = jnp.concatenate([router_terms.reshape(-1), ffn_gain_terms, prob_sums])
    early = sum_over(sum_over(early, "expert"), "dp")
    grad_router = early[: width * experts_all].reshape(width, experts_all)
    grad_ffn_gain = early[width * experts_all : width * experts_all + width]
    prob_total = early[width * experts_all + width :]
    head_gain_grads = jnp.sum(gain_parts, axis=(0, 1)).reshape(-1)
    attn_gain_terms = (
        jnp.sum(normed_terms.astype(f32) * normed_all.astype(f32), axis=0) / attn_gain
    )
    late = jnp.concatenate([attn_gain_terms, head_gain_grads])
    late = sum_over(sum_over(late, "expert"), "dp")
    balance_loss = balance_coef * experts_all * jnp.sum(fraction * (prob_total / n_valid))
    return (
        block_out,
        balance_loss,
        grad_tokens,
        late[:width],
        late[width : width + HD],
        late[width + HD :],
        grad_qkv,
        grad_out,
        grad_ffn_gain,
        grad_router,
        grad_expert_in,
        grad_expert_out,
    )


def solution(mesh):
    placed = (
        P("dp", "expert", None, None),
        P(),
        P("dp", "expert", None, None),
        P(),
        P(),
        P(),
        P(("dp", "expert"), None, None),
        P(("dp", "expert"), None),
        P(),
        P(),
        P("expert", None, None),
        P("expert", None, None),
        P(),
        P("dp", "expert", None, None),
    )
    return jax.shard_map(
        body,
        mesh=mesh,
        in_specs=placed,
        out_specs=(
            P("dp", "expert", None, None),
            P(),
            P("dp", "expert", None, None),
            P(),
            P(),
            P(),
            P(("dp", "expert"), None, None),
            P(("dp", "expert"), None),
            P(),
            P(),
            P("expert", "dp", None),
            P("expert", "dp", None),
        ),
        check_vma=False,
    )
```

time: 1710 us -> 1040 us (0.61)
  waiting for transfers between devices: 972 us -> 294 us
  Pallas kernels: 0 us -> 374 us
  matrix products: 324 us -> 58 us
  blocking collectives: 202 us -> 28.9 us
  starting transfers between devices: 11.9 us -> 97.6 us
  local copies, waits for them, and re-layouts: 102 us -> 67.2 us
    reduce_scatter x8 -> x3, waiting for transfers between devices: 498 us -> 0.01 us  [the longest x1 0.01 us: body(): lax.psum_scatter(output_terms, 'dp', scatter_dimension=0, tiled=True)]
    pallas_call x0 -> x21, Pallas kernels: none -> 374 us  [the longest x9 111 us: weight_part(): pl.pallas_call(functools.partial(weight_kernel, parts, len(adds)), grid_s...]
    all_gather x6 -> x3, waiting for transfers between devices: 313 us -> 0.01 us  [the longest x1 0.01 us: body(): lax.all_gather(w_cols.reshape(-1, 3 * cols), 'dp', axis=0, tiled=True)]
    ppermute x0 -> x72, waiting for transfers between devices: none -> 293 us  [the longest x48 192 us: ring_shift(): return lax.ppermute(rows, 'expert', pairs)]
    dot_general x20 -> x7, matrix products: 318 us -> 52.4 us  [the longest x3 19 us: dot_nn(): return jnp.dot(left, right, preferred_element_type=jnp.float32)]
    psum x1 -> x0, waiting for transfers between devices: 127 us -> none  [body(): lax.psum((attn_gain_terms, q_gain_terms, k_gain_terms, ffn_gain_terms, ro...]
    ppermute x0 -> x72, starting transfers between devices: none -> 82.9 us  [the longest x48 60.9 us: ring_shift(): return lax.ppermute(rows, 'expert', pairs)]
    psum x2 -> x0, blocking collectives: 78.9 us -> none  [the longest x1 40.1 us: body(): lax.psum((attn_gain_terms, q_gain_terms, k_gain_terms, ffn_gain_terms, ro...]
  transfers between devices with their start and end apart: 18 -> 81, of which waited for: 14 -> 33; matrix products, arithmetic and copies ran while one was open for 21% -> 16% of each run, Pallas kernels for 0% -> 33%
where the time goes in v2:
time: 1040 us; the launch traced here: 1030 us
  Pallas kernels  374 us (36%)
  waiting for transfers between devices  294 us (28%)
  starting transfers between devices  97.6 us (9%)
  other arithmetic  81.7 us (8%)
  local copies, waits for them, and re-layouts  67.2 us (6%)
  matrix products  58 us (6%)
  between operations  34 us (3%)
  blocking collectives  28.9 us (3%)
    ppermute x48, waiting for transfers between devices, ring_shift(): return lax.ppermute(rows, 'expert', pairs)  192 us
    pallas_call x9, Pallas kernels, weight_part(): pl.pallas_call(functools.partial(weight_kernel, parts, len(adds)), grid_s...  111 us
    pallas_call x5, Pallas kernels, experts_forward(): pl.pallas_call(functools.partial(experts_kernel, len(xs), len(held), tile...  107 us
    pallas_call x5, Pallas kernels, experts_backward(): pl.pallas_call(functools.partial(experts_back_kernel, len(outs), len(held...  106 us
    ppermute x48, starting transfers between devices, ring_shift(): return lax.ppermute(rows, 'expert', pairs)  60.9 us
    ppermute x3, waiting for transfers between devices, second(): self.near = lax.ppermute(terms, 'dp', [(i, i ^ 2) for i in range(4)])  51.7 us
    ppermute x15, waiting for transfers between devices, sum_over(): lax.ppermute(values, axis, [(i, i ^ step) for i in range(size)])  33.7 us
    pallas_call x1, Pallas kernels, attend_back(): pl.pallas_call(attend_back_kernel, grid_spec=pltpu.PrefetchScalarGridSpec...  31.8 us
  transfers between devices with their start and end apart: 81, of which 33 were waited for; matrix products, arithmetic and copies ran while one was open for 16% of the time, Pallas kernels for 33%

profile of v2, /device:TPU:0, one launch (start us, length us, event | category | flops | bytes accessed | tf_op | source)
XLA Modules:
  0.0 1034.6 jit_solution(14015542480853079811)
XLA Ops:
  23.2 33.2 %collective-permute-done.1 = bf16[256,2048]{1,0:T(8,128)(2,1)} collective-permute-done((bf16[256,2048]{1,0:T(8,128)(2,1)}, bf16[256,2048]{1,0:T(8,128)(2,1)}, u32[]{:S(2)}, u32[]{:S(2)}) %collective-permute-start.1) | collective-permute-done | bytes 1048608 | tf_op jit(solution)/shard_map/ppermute | solution.py:404
  56.4 28.9 %all_to_all.20 = bf16[8,64,768]{2,1,0:T(8,128)(2,1)} all-to-all(bf16[8,64,768]{2,1,0:T(8,128)(2,1)} %reshape.327), channel_id=1, replica_groups=mesh['dp'=4,'expert'=8] {'expert'}, dimensions={0} | all-to-all | bytes 1572864 | tf_op jit(solution)/shard_map/all_to_all | solution.py:658
  85.4 24.1 %collective-permute-done = bf16[256,2048]{1,0:T(8,128)(2,1)S(1)} collective-permute-done((bf16[256,2048]{1,0:T(8,128)(2,1)}, bf16[256,2048]{1,0:T(8,128)(2,1)S(1)}, u32[]{:S(2)}, u32[]{:S(2)}) %collective-permute-start) | collective-permute-done | bytes 1048608 | tf_op jit(solution)/shard_map/ppermute | solution.py:404
  111.5 21.3 %collective-permute-done.2 = bf16[256,2048]{1,0:T(8,128)(2,1)S(1)} collective-permute-done((bf16[256,2048]{1,0:T(8,128)(2,1)S(1)}, bf16[256,2048]{1,0:T(8,128)(2,1)S(1)}, u32[]{:S(2)}, u32[]{:S(2)}) %collective-permute-start.2) | collective-permute-done | bytes 1048608 | tf_op jit(solution)/shard_map/ppermute | solution.py:404
  139.3 16.7 %collective-permute-done.4 = bf16[256,2048]{1,0:T(8,128)(2,1)S(1)} collective-permute-done((bf16[256,2048]{1,0:T(8,128)(2,1)S(1)}, bf16[256,2048]{1,0:T(8,128)(2,1)S(1)}, u32[]{:S(2)}, u32[]{:S(2)}) %collective-permute-start.4) | collective-permute-done | bytes 1048608 | tf_op jit(solution)/shard_map/ppermute | solution.py:404
  178.1 12.8 %fusion.58 = f32[2048,768]{1,0:T(8,128)} fusion(bf16[2048,2048]{1,0:T(8,128)(2,1)} %constant_dynamic-update-slice_fusion, bf16[2048,768]{1,0:T(8,128)(2,1)} %all-gather.4.cloned.1.call-done), kind=kOutput, calls=%fused_computation.208 | convolution fusion | flops 6442450944 | bytes 17825792 | tf_op jit(solution)/shard_map/dot_general | solution.py:39
  190.9 18.5 %attend.1 = bf16[8,2,128,256]{3,2,1,0:T(8,128)(2,1)} custom-call(s32[8]{0:T(128)} %get-tuple-element.318.owner_ref, f32[8,2,128,768]{3,2,1,0:T(8,128)} %bitcast.183, f32[1024,128]{1,0:T(8,128)} %get-tuple-element.340.cos_ref, f32[1024,128]{1,0:T(8,128)} %get-tuple-element.341.sin_ref, f32[2,1,1024]{2,1,0:T(1,128)} %compare_convert_fusion.live_ref, ...), custom_call_target="tpu_custom_call" | custom-call | flops 2147483648 | bytes 7864320 | tf_op jit(solution)/shard_map/attend/pallas_call | solution.py:105
  240.4 13.2 %collective-permute-done.9 = bf16[2,32,256]{2,1,0:T(8,128)(2,1)S(1)} collective-permute-done((bf16[2,32,256]{2,1,0:T(8,128)(2,1)S(1)}, bf16[2,32,256]{2,1,0:T(8,128)(2,1)S(1)}, u32[]{:S(2)}, u32[]{:S(2)}) %collective-permute-start.9) | collective-permute-done | bytes 32800 | tf_op jit(solution)/shard_map/ppermute | solution.py:472
  274.8 12.1 %collective-permute-done.23.refs_0_ = bf16[256,2048]{1,0:T(8,128)(2,1)} collective-permute-done((bf16[256,2048]{1,0:T(8,128)(2,1)}, bf16[256,2048]{1,0:T(8,128)(2,1)}, u32[]{:S(2)}, u32[]{:S(2)}) %collective-permute-start.23) | collective-permute-done | bytes 1048608 | tf_op jit(solution)/shard_map/ppermute | solution.py:404
  291.3 17.8 %experts_forward.5 = (bf16[2048,2048]{1,0:T(8,128)(2,1)}, bf16[2048,2048]{1,0:T(8,128)(2,1)}, bf16[2048,2048]{1,0:T(8,128)(2,1)}, bf16[2048,2048]{1,0:T(8,128)(2...) custom-call(bf16[256,2048]{1,0:T(8,128)(2,1)} %copy-done.4, f32[256,128]{1,0:T(8,128)} %pad_convert_fusion.1.refs_1_, ...), custom_call_target="tpu_custom_call" | custom-call | flops 6442450944 | bytes 30408704 | tf_op jit(solution)/shard_map/experts_forward/pallas_call | solution.py:272
  311.2 23.6 %experts_forward.6 = (bf16[2048,2048]{1,0:T(8,128)(2,1)}, bf16[2048,2048]{1,0:T(8,128)(2,1)}, bf16[2048,2048]{1,0:T(8,128)(2,1)}, bf16[2048,2048]{1,0:T(8,128)(2...) custom-call(bf16[256,2048]{1,0:T(8,128)(2,1)} %copy-done.26, ...), custom_call_target="tpu_custom_call", output_to_operand_aliasing={{0}: (8, {}), {1}: (9, {}), {2}: (10, {}), {3}: (11, {})} | custom-call | flops 12884901888 | bytes 35651584 | tf_op jit(solution)/shard_map/experts_forward/pallas_call | solution.py:272
  356.1 23.7 %experts_forward.7 = (bf16[2048,2048]{1,0:T(8,128)(2,1)}, bf16[2048,2048]{1,0:T(8,128)(2,1)}, bf16[2048,2048]{1,0:T(8,128)(2,1)}, bf16[2048,2048]{1,0:T(8,128)(2...) custom-call(bf16[256,2048]{1,0:T(8,128)(2,1)} %collective-permute-do, ...), custom_call_target="tpu_custom_call", output_to_operand_aliasing={{0}: (8, {}), {1}: (9, {}), {2}: (10, {}), {3}: (11, {})} | custom-call | flops 12884901888 | bytes 35651584 | tf_op jit(solution)/shard_map/experts_forward/pallas_call | solution.py:272
  382.1 23.7 %experts_forward.8 = (bf16[2048,2048]{1,0:T(8,128)(2,1)}, bf16[2048,2048]{1,0:T(8,128)(2,1)}, bf16[2048,2048]{1,0:T(8,128)(2,1)}, bf16[2048,2048]{1,0:T(8,128)(2...) custom-call(bf16[256,2048]{1,0:T(8,128)(2,1)} %copy-done.14, ...), custom_call_target="tpu_custom_call", output_to_operand_aliasing={{0}: (8, {}), {1}: (9, {}), {2}: (10, {}), {3}: (11, {})} | custom-call | flops 12884901888 | bytes 35651584 | tf_op jit(solution)/shard_map/experts_forward/pallas_call | solution.py:272
  406.9 17.8 %experts_forward.9 = (bf16[2048,2048]{1,0:T(8,128)(2,1)}, bf16[2048,2048]{1,0:T(8,128)(2,1)}, bf16[2048,2048]{1,0:T(8,128)(2,1)}, bf16[2048,2048]{1,0:T(8,128)(2...) custom-call(bf16[256,2048]{1,0:T(8,128)(2,1)} %pad_maximum_fusion.5., ...), custom_call_target="tpu_custom_call", output_to_operand_aliasing={{0}: (7, {}), {1}: (8, {}), {2}: (9, {}), {3}: (10, {})} | custom-call | flops 6442450944 | bytes 30408704 | tf_op jit(solution)/shard_map/experts_forward/pallas_call | solution.py:272
  424.7 17.2 %experts_backward.5 = (bf16[2048,2048]{1,0:T(8,128)(2,1)}, bf16[2048,2048]{1,0:T(8,128)(2,1)}, bf16[2048,2048]{1,0:T(8,128)(2,1)}, f32[256,128]{1,0:T(8,128)}, bf16[256,2048]{1,0:T(8,128)(2,1)}) custom-call(bf16[256,2048]{1,0:T(8,128)(2,1)} %pad_maximum_fusion.6.refs_0_, f32[256,2]{1,0:T(8,128)} %get-tuple-element.146.refs_1_, ...), custom_call_target="tpu_custom_call" | custom-call | flops 6442450944 | bytes 31457280 | tf_op jit(solution)/shard_map/experts_backward/pallas_call | solution.py:359
  446.2 23.8 %experts_backward.6 = (bf16[2048,2048]{1,0:T(8,128)(2,1)}, bf16[2048,2048]{1,0:T(8,128)(2,1)}, bf16[2048,2048]{1,0:T(8,128)(2,1)}, f32[512,128]{1,0:T(8,128)}, bf16[512,2048]{1,0:T(8,128)(2,1)}) custom-call(bf16[256,2048]{1,0:T(8,128)(2,1)} %collective-permute-done.23.refs_0_, ...), custom_call_target="tpu_custom_call", output_to_operand_aliasing={{0}: (8, {}), {1}: (9, {}), {2}: (10, {})} | custom-call | flops 12884901888 | bytes 37748736 | tf_op jit(solution)/shard_map/experts_backward/pallas_call | solution.py:359
  475.3 23.8 %experts_backward.7 = (bf16[2048,2048]{1,0:T(8,128)(2,1)}, bf16[2048,2048]{1,0:T(8,128)(2,1)}, bf16[2048,2048]{1,0:T(8,128)(2,1)}, f32[512,128]{1,0:T(8,128)}, bf16[512,2048]{1,0:T(8,128)(2,1)}) custom-call(bf16[256,2048]{1,0:T(8,128)(2,1)} %collective-permute-done.21.refs_0_, ...), custom_call_target="tpu_custom_call", output_to_operand_aliasing={{0}: (8, {}), {1}: (9, {}), {2}: (10, {})} | custom-call | flops 12884901888 | bytes 37748736 | tf_op jit(solution)/shard_map/experts_backward/pallas_call | solution.py:359
  504.2 23.8 %experts_backward.8 = (bf16[2048,2048]{1,0:T(8,128)(2,1)}, bf16[2048,2048]{1,0:T(8,128)(2,1)}, bf16[2048,2048]{1,0:T(8,128)(2,1)}, f32[512,128]{1,0:T(8,128)}, bf16[512,2048]{1,0:T(8,128)(2,1)}) custom-call(bf16[256,2048]{1,0:T(8,128)(2,1)} %collective-permute-done.19.refs_0_, ...), custom_call_target="tpu_custom_call", output_to_operand_aliasing={{0}: (8, {}), {1}: (9, {}), {2}: (10, {})} | custom-call | flops 12884901888 | bytes 37748736 | tf_op jit(solution)/shard_map/experts_backward/pallas_call | solution.py:359
  536.0 17.2 %experts_backward.9 = (bf16[2048,2048]{1,0:T(8,128)(2,1)}, bf16[2048,2048]{1,0:T(8,128)(2,1)}, bf16[2048,2048]{1,0:T(8,128)(2,1)}, f32[256,128]{1,0:T(8,128)}, bf16[256,2048]{1,0:T(8,128)(2,1)}) custom-call(bf16[256,2048]{1,0:T(8,128)(2,1)} %bitcast.47.refs_0_, ...), custom_call_target="tpu_custom_call", output_to_operand_aliasing={{0}: (7, {}), {1}: (8, {}), {2}: (9, {})} | custom-call | flops 6442450944 | bytes 31457280 | tf_op jit(solution)/shard_map/experts_backward/pallas_call | solution.py:359
  629.3 13.7 %collective-permute-done.49 = f32[34832]{0:T(1024)S(1)} collective-permute-done((f32[34832]{0:T(1024)S(1)}, f32[34832]{0:T(1024)S(1)}, u32[]{:S(2)}, u32[]{:S(2)}) %collective-permute-start.49) | collective-permute-done | bytes 139360 | tf_op jit(solution)/shard_map/ppermute | solution.py:464
  657.2 15.2 %weights_out.3 = bf16[1024,2048]{1,0:T(8,128)(2,1)} custom-call(s32[4]{0:T(128)} %pad_add_fusion.index_ref, bf16[2048,2048]{1,0:T(8,128)(2,1)} %get-tuple-element.193.refs_0_.refs_1_.refs_2_.refs_3_, bf16[2048,2048]{1,0:T(8,128)(2,1)} %get-tuple-element.193.refs_0_.refs_1_.refs_2_.refs_3_, ...), custom_call_target="tpu_custom_call" | custom-call | flops 8589934592 | bytes 20971520 | tf_op jit(solution)/shard_map/weights_out/pallas_call | solution.py:514
  673.0 31.8 %attend_back.1 = (bf16[8,2,128,768]{3,2,1,0:T(8,128)(2,1)}, f32[2,2,2,128]{3,2,1,0:T(2,128)}) custom-call(s32[8]{0:T(128)} %get-tuple-element.318.owner_ref, f32[8,2,128,768]{3,2,1,0:T(8,128)} %bitcast.184, bf16[8,2,128,256]{3,2,1,0:T(8,128)(2,1)} %bitcast.52.grad_ref, f32[1024,128]{1,0:T(8,128)} %get-tuple-element.340.cos_ref, ...), custom_call_target="tpu_custom_call" | custom-call | flops 5368709120 | bytes 11010048 | tf_op jit(solution)/shard_map/attend_back/pallas_call | solution.py:176
  722.1 11.4 %convolution_convert_fusion.2 = bf16[2048,768]{1,0:T(8,128)(2,1)} fusion(bf16[2048,2048]{1,0:T(8,128)(2,1)} %constant_dynamic-update-slice_fusion, bf16[2048,768]{1,0:T(8,128)(2,1)} %bitcast.209), kind=kOutput, calls=%fused_computation.9 | convolution fusion | flops 6444023808 | bytes 14680064 | tf_op jit(solution)/shard_map/dot_general | solution.py:49
  733.9 15.2 %weights_gate.3 = bf16[1024,2048]{1,0:T(8,128)(2,1)} custom-call(s32[2]{0:T(128)} %pad_add_fusion.2.index_ref, bf16[2048,2048]{1,0:T(8,128)(2,1)} %get-tuple-element.190.refs_0_.refs_1_, bf16[2048,2048]{1,0:T(8,128)(2,1)} %get-tuple-element.190.refs_0_.refs_1_, bf16[2048,2048]{1,0:T(8,128)(2,1)} %get-tuple-element.186.refs_2_.refs_1_), custom_call_target="tpu_custom_call" | custom-call | flops 8589934592 | bytes 20971520 | tf_op jit(solution)/shard_map/weights_gate/pallas_call | solution.py:514
  754.8 15.3 %weights_up.3 = bf16[1024,2048]{1,0:T(8,128)(2,1)} custom-call(s32[2]{0:T(128)} %pad_add_fusion.2.index_ref, bf16[2048,2048]{1,0:T(8,128)(2,1)} %get-tuple-element.190.refs_0_.refs_1_, bf16[2048,2048]{1,0:T(8,128)(2,1)} %get-tuple-element.190.refs_0_.refs_1_, bf16[2048,2048]{1,0:T(8,128)(2,1)} %get-tuple-element.189.refs_2_.refs_1_), custom_call_target="tpu_custom_call" | custom-call | flops 8589934592 | bytes 20971520 | tf_op jit(solution)/shard_map/weights_up/pallas_call | solution.py:514
  783.6 18.8 %collective-permute-done.42 = bf16[256,2048]{1,0:T(8,128)(2,1)S(1)} collective-permute-done((bf16[256,2048]{1,0:T(8,128)(2,1)S(1)}, bf16[256,2048]{1,0:T(8,128)(2,1)S(1)}, u32[]{:S(2)}, u32[]{:S(2)}) %collective-permute-start.42) | collective-permute-done | bytes 1048608 | tf_op jit(solution)/shard_map/ppermute | solution.py:404
  811.0 11.3 %collective-permute-done.55 = bf16[256,2048]{1,0:T(8,128)(2,1)S(1)} collective-permute-done((bf16[256,2048]{1,0:T(8,128)(2,1)S(1)}, bf16[256,2048]{1,0:T(8,128)(2,1)S(1)}, u32[]{:S(2)}, u32[]{:S(2)}) %collective-permute-start.55) | collective-permute-done | bytes 1048608 | tf_op jit(solution)/shard_map/ppermute | solution.py:404
  912.6 11.4 %weights_out.5 = f32[512,2048]{1,0:T(8,128)} custom-call(s32[6]{0:T(128)} %stack.107.index_ref, bf16[2048,2048]{1,0:T(8,128)(2,1)} %get-tuple-element.193.refs_0_.refs_1_.refs_2_.refs_3_, bf16[2048,2048]{1,0:T(8,128)(2,1)} %get-tuple-element.193.refs_0_.refs_1_.refs_2_.refs_3_, bf16[2048,2048]{1,0:T(8,128)(2,1)} %get-tuple-element.175.refs_4_.refs_2_, ...), custom_call_target="tpu_custom_call" | custom-call | flops 4294967296 | bytes 14680064 | tf_op jit(solution)/shard_map/weights_out/pallas_call | solution.py:514
  937.4 20.2 %collective-permute-done.69.refs_3_ = bf16[512,2048]{1,0:T(8,128)(2,1)} collective-permute-done((bf16[512,2048]{1,0:T(8,128)(2,1)}, bf16[512,2048]{1,0:T(8,128)(2,1)}, u32[]{:S(2)}, u32[]{:S(2)}) %collective-permute-start.69) | collective-permute-done | bytes 2097184 | tf_op jit(solution)/shard_map/ppermute | solution.py:578
  957.6 11.4 %weights_up.5 = f32[512,2048]{1,0:T(8,128)} custom-call(s32[3]{0:T(128)} %pad_add_fusion.1.index_ref, bf16[2048,2048]{1,0:T(8,128)(2,1)} %get-tuple-element.190.refs_0_.refs_1_, bf16[2048,2048]{1,0:T(8,128)(2,1)} %get-tuple-element.189.refs_2_.refs_1_, bf16[1024,2048]{1,0:T(8,128)(2,1)} %collective-permute-done.68.refs_2_, ...), custom_call_target="tpu_custom_call" | custom-call | flops 4294967296 | bytes 14680064 | tf_op jit(solution)/shard_map/weights_up/pallas_call | solution.py:514
  971.8 26.8 %collective-permute-done.67.refs_3_ = bf16[512,2048]{1,0:T(8,128)(2,1)S(1)} collective-permute-done((bf16[512,2048]{1,0:T(8,128)(2,1)}, bf16[512,2048]{1,0:T(8,128)(2,1)S(1)}, u32[]{:S(2)}, u32[]{:S(2)}) %collective-permute-start.67) | collective-permute-done | bytes 2097184 | tf_op jit(solution)/shard_map/ppermute | solution.py:578
  999.9 11.3 %weights_gate.5 = f32[512,2048]{1,0:T(8,128)} custom-call(s32[3]{0:T(128)} %pad_add_fusion.1.index_ref, bf16[2048,2048]{1,0:T(8,128)(2,1)} %get-tuple-element.190.refs_0_.refs_1_, bf16[2048,2048]{1,0:T(8,128)(2,1)} %get-tuple-element.186.refs_2_.refs_1_, bf16[1024,2048]{1,0:T(8,128)(2,1)} %collective-permute-done.66.refs_2_, bf16[512,2048]{1,0:T(8,128)(2,1)} %copy-done.17), custom_call_target="tpu_custom_call" | custom-call | flops 4294967296 | bytes 14680064 | tf_op jit(solution)/shard_map/weights_gate/pallas_call | solution.py:514
  (443 shorter events, 394.0 us)
Async XLA Ops:
  7.2 160.7 %all-gather.6.cloned.1.call-start = ((), (), s32[]{:S(2)}) async-start(), calls=%async_computation.8 | async-start | bytes 2359296 | tf_op jit(solution)/shard_map/all_gather | solution.py:666
  7.9 170.2 %all-gather.4.cloned.1.call-start = ((), (), s32[]{:S(2)}) async-start(), calls=%async_computation.7 | async-start | bytes 3932160 | tf_op jit(solution)/shard_map/all_gather | solution.py:665
  15.1 41.3 %collective-permute-start.1 = (bf16[256,2048]{1,0:T(8,128)(2,1)}, bf16[256,2048]{1,0:T(8,128)(2,1)}, u32[]{:S(2)}, u32[]{:S(2)}) collective-permute-start(bf16[256,2048]{1,0:T(8,128)(2,1)} %get-tuple-element.332), channel_id=1, source_target_pairs={{0,1},{2,0},{4,2},{6,4},{7,6},{5,7},{3,5},{1,3},{8,9},{10,8},{12,1... | collective-permute-start | bytes 3145736 | tf_op jit(solution)/shard_map/ppermute | solution.py:404
  85.3 177.7 %all-gather.8.cloned.1.call-start = ((), (), s32[]{:S(2)}) async-start(), calls=%async_computation.9 | async-start | bytes 10485760 | tf_op jit(solution)/shard_map/all_gather | solution.py:670
  175.9 44.1 %collective-permute-start.19 = (bf16[256,2048]{1,0:T(8,128)(2,1)}, bf16[256,2048]{1,0:T(8,128)(2,1)}, u32[]{:S(2)}, u32[]{:S(2)}) collective-permute-start(bf16[256,2048]{1,0:T(8,128)(2,1)} %bitcast.47.refs_0_), channel_id=1, source_target_pairs={{0,2},{2,4},{4,6},{6,7},{7,5},{5,3},{3,1},{1,0},{8,10},{10,12},{12... | collective-permute-start | bytes 3145736 | tf_op jit(solution)/shard_map/ppermute | solution.py:404
  177.4 42.6 %collective-permute-start.20 = (bf16[256,2048]{1,0:T(8,128)(2,1)}, bf16[256,2048]{1,0:T(8,128)(2,1)}, u32[]{:S(2)}, u32[]{:S(2)}) collective-permute-start(bf16[256,2048]{1,0:T(8,128)(2,1)} %bitcast.47.refs_0_), channel_id=1, source_target_pairs={{0,1},{2,0},{4,2},{6,4},{7,6},{5,7},{3,5},{1,3},{8,9},{10,8},{12,1... | collective-permute-start | bytes 3145736 | tf_op jit(solution)/shard_map/ppermute | solution.py:404
  211.7 44.7 %all-to-all-start.1 = ((bf16[8,256,256]{1,2,0:T(8,128)(2,1)}), bf16[8,256,256]{1,2,0:T(8,128)(2,1)S(1)}, u32[]{:S(2)}, u32[]{:S(2)}) async-start(bf16[8,256,256]{1,2,0:T(8,128)(2,1)} %copy.140), calls=%async_computation.1 | async-start | bytes 2097152 | tf_op jit(solution)/shard_map/all_to_all | solution.py:702
  216.6 691.3 %reduce-scatter.6.cloned.1.call-start = ((), (), s32[]{:S(2)}) async-start(), calls=%async_computation.11 | async-start | bytes 10485760 | tf_op jit(solution)/shard_map/reduce_scatter | solution.py:803
  220.0 36.3 %collective-permute-start.21 = (bf16[256,2048]{1,0:T(8,128)(2,1)}, bf16[256,2048]{1,0:T(8,128)(2,1)}, u32[]{:S(2)}, u32[]{:S(2)}) collective-permute-start(bf16[256,2048]{1,0:T(8,128)(2,1)} %collective-permute-done.19.refs_0_), channel_id=1, source_target_pairs={{0,2},{2,4},{4,6},{6,7},{7,5},{5,3},{3,1},{1,0},{8,10},{10,12},{12... | collective-permute-start | bytes 3145736 | tf_op jit(solution)/shard_map/ppermute | solution.py:404
  221.5 34.9 %collective-permute-start.22 = (bf16[256,2048]{1,0:T(8,128)(2,1)}, bf16[256,2048]{1,0:T(8,128)(2,1)}, u32[]{:S(2)}, u32[]{:S(2)}) collective-permute-start(bf16[256,2048]{1,0:T(8,128)(2,1)} %collective-permute-done.20.refs_1_), channel_id=1, source_target_pairs={{0,1},{2,0},{4,2},{6,4},{7,6},{5,7},{3,5},{1,3},{8,9},{10,8},{12,1... | collective-permute-start | bytes 3145736 | tf_op jit(solution)/shard_map/ppermute | solution.py:404
  270.4 38.7 %collective-permute-start.11 = (bf16[256,2048]{1,0:T(8,128)(2,1)S(1)}, bf16[256,2048]{1,0:T(8,128)(2,1)S(1)}, u32[]{:S(2)}, u32[]{:S(2)}) collective-permute-start(bf16[256,2048]{1,0:T(8,128)(2,1)S(1)} %multiply_convert_fusion.refs_0_), channel_id=1, source_target_pairs={{0,2},{2,4},{4,6},{6,7},{7,5},{5,3},{3,1},{1,0},{8,10},{10,12},{12... | collective-permute-start | bytes 3145736 | tf_op jit(solution)/shard_map/ppermute | solution.py:404
  272.5 36.6 %collective-permute-start.12 = (bf16[256,2048]{1,0:T(8,128)(2,1)S(1)}, bf16[256,2048]{1,0:T(8,128)(2,1)S(1)}, u32[]{:S(2)}, u32[]{:S(2)}) collective-permute-start(bf16[256,2048]{1,0:T(8,128)(2,1)S(1)} %multiply_convert_fusion.refs_0_), channel_id=1, source_target_pairs={{0,1},{2,0},{4,2},{6,4},{7,6},{5,7},{3,5},{1,3},{8,9},{10,8},{12,1... | collective-permute-start | bytes 3145736 | tf_op jit(solution)/shard_map/ppermute | solution.py:404
  309.1 44.9 %collective-permute-start.13 = (bf16[256,2048]{1,0:T(8,128)(2,1)S(1)}, bf16[256,2048]{1,0:T(8,128)(2,1)}, u32[]{:S(2)}, u32[]{:S(2)}) collective-permute-start(bf16[256,2048]{1,0:T(8,128)(2,1)S(1)} %collective-permute-done.11.refs_0_), channel_id=1, source_target_pairs={{0,2},{2,4},{4,6},{6,7},{7,5},{5,3},{3,1},{1,0},{8,10},{10,12},{12... | collective-permute-start | bytes 3145736 | tf_op jit(solution)/shard_map/ppermute | solution.py:404
  311.1 42.9 %collective-permute-start.14 = (bf16[256,2048]{1,0:T(8,128)(2,1)S(1)}, bf16[256,2048]{1,0:T(8,128)(2,1)S(1)}, u32[]{:S(2)}, u32[]{:S(2)}) collective-permute-start(bf16[256,2048]{1,0:T(8,128)(2,1)S(1)} %collective-permute-done.12.refs_1_), channel_id=1, source_target_pairs={{0,1},{2,0},{4,2},{6,4},{7,6},{5,7},{3,5},{1,3},{8,9},{10,8},{12,1... | collective-permute-start | bytes 3145736 | tf_op jit(solution)/shard_map/ppermute | solution.py:404
  619.6 53.4 %all-to-all-start.2 = ((bf16[8,256,256]{2,1,0:T(8,128)(2,1)}), bf16[8,256,256]{2,1,0:T(8,128)(2,1)}, u32[]{:S(2)}, u32[]{:S(2)}) async-start(bf16[8,256,256]{2,1,0:T(8,128)(2,1)} %bitcast.164), calls=%async_computation.2 | async-start | bytes 2097152 | tf_op jit(solution)/shard_map/all_to_all | solution.py:793
  624.0 308.2 %reduce-scatter.4.cloned.1.call-start = ((), (), s32[]{:S(2)}) async-start(), calls=%async_computation.10 | async-start | bytes 3932160 | tf_op jit(solution)/shard_map/reduce_scatter | solution.py:828
  649.4 122.2 %collective-permute-start.43 = (bf16[256,2048]{1,0:T(8,128)(2,1)}, bf16[256,2048]{1,0:T(8,128)(2,1)}, u32[]{:S(2)}, u32[]{:S(2)}) collective-permute-start(bf16[256,2048]{1,0:T(8,128)(2,1)} %pad_maximum_fusion.8), channel_id=1, source_target_pairs={{0,1},{2,0},{4,2},{6,4},{7,6},{5,7},{3,5},{1,3},{8,9},{10,8},{12,1... | collective-permute-start | bytes 3145736 | tf_op jit(solution)/shard_map/ppermute | solution.py:404
  672.4 180.6 %collective-permute-start.70 = (bf16[1024,2048]{1,0:T(8,128)(2,1)}, bf16[1024,2048]{1,0:T(8,128)(2,1)}, u32[]{:S(2)}, u32[]{:S(2)}) collective-permute-start(bf16[1024,2048]{1,0:T(8,128)(2,1)} %weights_out.3), channel_id=1, source_target_pairs={{0,8},{8,0},{16,24},{24,16},{1,9},{9,1},{17,25},{25,17},{2,10},{10... | collective-permute-start | bytes 12582920 | tf_op jit(solution)/shard_map/ppermute | solution.py:563
  719.5 32.2 %collective-permute-start.57 = (bf16[128,2048]{1,0:T(8,128)(2,1)}, bf16[128,2048]{1,0:T(8,128)(2,1)}, u32[]{:S(2)}, u32[]{:S(2)}) collective-permute-start(bf16[128,2048]{1,0:T(8,128)(2,1)} %get-tuple-element.271), channel_id=1, source_target_pairs={{0,1},{2,0},{4,2},{6,4},{7,6},{5,7},{3,5},{1,3},{8,9},{10,8},{12,1... | collective-permute-start | bytes 1572872 | tf_op jit(solution)/shard_map/ppermute | solution.py:404
  733.5 291.1 %reduce-scatter.8.cloned.1.call-start = ((), (), s32[]{:S(2)}) async-start(), calls=%async_computation.12 | async-start | bytes 2359296 | tf_op jit(solution)/shard_map/reduce_scatter | solution.py:802
  770.0 94.2 %collective-permute-start.68 = (bf16[1024,2048]{1,0:T(8,128)(2,1)}, bf16[1024,2048]{1,0:T(8,128)(2,1)}, u32[]{:S(2)}, u32[]{:S(2)}) collective-permute-start(bf16[1024,2048]{1,0:T(8,128)(2,1)} %weights_up.3), channel_id=1, source_target_pairs={{0,8},{8,0},{16,24},{24,16},{1,9},{9,1},{17,25},{25,17},{2,10},{10... | collective-permute-start | bytes 12582920 | tf_op jit(solution)/shard_map/ppermute | solution.py:563
  770.1 32.3 %collective-permute-start.42 = (bf16[256,2048]{1,0:T(8,128)(2,1)S(1)}, bf16[256,2048]{1,0:T(8,128)(2,1)S(1)}, u32[]{:S(2)}, u32[]{:S(2)}) collective-permute-start(bf16[256,2048]{1,0:T(8,128)(2,1)S(1)} %copy-done.23), channel_id=1, source_target_pairs={{0,2},{2,4},{4,6},{6,7},{7,5},{5,3},{3,1},{1,0},{8,10},{10,12},{12... | collective-permute-start | bytes 3145736 | tf_op jit(solution)/shard_map/ppermute | solution.py:404
  783.1 39.2 %collective-permute-start.55 = (bf16[256,2048]{1,0:T(8,128)(2,1)S(1)}, bf16[256,2048]{1,0:T(8,128)(2,1)S(1)}, u32[]{:S(2)}, u32[]{:S(2)}) collective-permute-start(bf16[256,2048]{1,0:T(8,128)(2,1)S(1)} %add_convert_fusion.7), channel_id=1, source_target_pairs={{0,2},{2,4},{4,6},{6,7},{7,5},{5,3},{3,1},{1,0},{8,10},{10,12},{12... | collective-permute-start | bytes 3145736 | tf_op jit(solution)/shard_map/ppermute | solution.py:404
  806.0 91.5 %collective-permute-start.66 = (bf16[1024,2048]{1,0:T(8,128)(2,1)}, bf16[1024,2048]{1,0:T(8,128)(2,1)}, u32[]{:S(2)}, u32[]{:S(2)}) collective-permute-start(bf16[1024,2048]{1,0:T(8,128)(2,1)} %weights_gate.3), channel_id=1, source_target_pairs={{0,8},{8,0},{16,24},{24,16},{1,9},{9,1},{17,25},{25,17},{2,10},{10... | collective-permute-start | bytes 12582920 | tf_op jit(solution)/shard_map/ppermute | solution.py:563
  851.3 31.7 %collective-permute-start.47 = (bf16[256,2048]{1,0:T(8,128)(2,1)}, bf16[256,2048]{1,0:T(8,128)(2,1)S(1)}, u32[]{:S(2)}, u32[]{:S(2)}) collective-permute-start(bf16[256,2048]{1,0:T(8,128)(2,1)} %get-tuple-element.181), channel_id=1, source_target_pairs={{0,1},{2,0},{4,2},{6,4},{7,6},{5,7},{3,5},{1,3},{8,9},{10,8},{12,1... | collective-permute-start | bytes 3145736 | tf_op jit(solution)/shard_map/ppermute | solution.py:404
  853.0 31.5 %collective-permute-start.46 = (bf16[256,2048]{1,0:T(8,128)(2,1)}, bf16[256,2048]{1,0:T(8,128)(2,1)S(1)}, u32[]{:S(2)}, u32[]{:S(2)}) collective-permute-start(bf16[256,2048]{1,0:T(8,128)(2,1)} %get-tuple-element.180), channel_id=1, source_target_pairs={{0,2},{2,4},{4,6},{6,7},{7,5},{5,3},{3,1},{1,0},{8,10},{10,12},{12... | collective-permute-start | bytes 3145736 | tf_op jit(solution)/shard_map/ppermute | solution.py:404
  863.8 48.9 %collective-permute-start.71 = (bf16[512,2048]{1,0:T(8,128)(2,1)}, bf16[512,2048]{1,0:T(8,128)(2,1)}, u32[]{:S(2)}, u32[]{:S(2)}) collective-permute-start(bf16[512,2048]{1,0:T(8,128)(2,1)} %weights_out.4), channel_id=1, source_target_pairs={{0,16},{8,24},{16,0},{24,8},{1,17},{9,25},{17,1},{25,9},{2,18},{10... | collective-permute-start | bytes 6291464 | tf_op jit(solution)/shard_map/ppermute | solution.py:578
  864.3 33.2 %collective-permute-start.56 = (bf16[256,2048]{1,0:T(8,128)(2,1)S(1)}, bf16[256,2048]{1,0:T(8,128)(2,1)S(1)}, u32[]{:S(2)}, u32[]{:S(2)}) collective-permute-start(bf16[256,2048]{1,0:T(8,128)(2,1)S(1)} %copy-done.25), channel_id=1, source_target_pairs={{0,2},{2,4},{4,6},{6,7},{7,5},{5,3},{3,1},{1,0},{8,10},{10,12},{12... | collective-permute-start | bytes 3145736 | tf_op jit(solution)/shard_map/ppermute | solution.py:404
  882.9 41.1 %collective-permute-start.60 = (bf16[256,2048]{1,0:T(8,128)(2,1)}, bf16[256,2048]{1,0:T(8,128)(2,1)}, u32[]{:S(2)}, u32[]{:S(2)}) collective-permute-start(bf16[256,2048]{1,0:T(8,128)(2,1)} %add_convert_fusion.4), channel_id=1, source_target_pairs={{0,1},{2,0},{4,2},{6,4},{7,6},{5,7},{3,5},{1,3},{8,9},{10,8},{12,1... | collective-permute-start | bytes 3145736 | tf_op jit(solution)/shard_map/ppermute | solution.py:404
  884.5 73.1 %collective-permute-start.69 = (bf16[512,2048]{1,0:T(8,128)(2,1)}, bf16[512,2048]{1,0:T(8,128)(2,1)}, u32[]{:S(2)}, u32[]{:S(2)}) collective-permute-start(bf16[512,2048]{1,0:T(8,128)(2,1)} %weights_up.4), channel_id=1, source_target_pairs={{0,16},{8,24},{16,0},{24,8},{1,17},{9,25},{17,1},{25,9},{2,18},{10... | collective-permute-start | bytes 6291464 | tf_op jit(solution)/shard_map/ppermute | solution.py:578
  907.9 90.6 %collective-permute-start.67 = (bf16[512,2048]{1,0:T(8,128)(2,1)}, bf16[512,2048]{1,0:T(8,128)(2,1)S(1)}, u32[]{:S(2)}, u32[]{:S(2)}) collective-permute-start(bf16[512,2048]{1,0:T(8,128)(2,1)} %weights_gate.4), channel_id=1, source_target_pairs={{0,16},{8,24},{16,0},{24,8},{1,17},{9,25},{17,1},{25,9},{2,18},{10... | collective-permute-start | bytes 6291464 | tf_op jit(solution)/shard_map/ppermute | solution.py:578
  932.2 86.3 %all-to-all-start.3 = ((bf16[8,64,768]{2,1,0:T(8,128)(2,1)}), bf16[8,64,768]{2,1,0:T(8,128)(2,1)S(1)}, u32[]{:S(2)}, u32[]{:S(2)}) async-start(bf16[8,64,768]{2,1,0:T(8,128)(2,1)} %bitcast.193), calls=%async_computation.4 | async-start | bytes 1572864 | tf_op jit(solution)/shard_map/all_to_all | solution.py:851
  (109 other events, 1651.5 us)
Sparse Core Ops, SparseCore 0:
  10.1 61.4 all-gather.5
  85.4 28.3 all-gather.3
  168.0 58.2 all-gather.7
  590.1 70.3 reduce-scatter.5
  733.6 38.3 reduce-scatter.3
  908.1 74.7 reduce-scatter.7

commit v3 on v2

--- a/solution.py
+++ b/solution.py
@@ -232,7 +232,7 @@
     def _():
         fill_rows(x_refs, rows)
         logits = dot_nn(rows[...], router_ref[...])
-        hits = hits_ref[...]
+        hits = hits_ref[...].astype(jnp.float32)
         lane = lax.broadcasted_iota(jnp.int32, logits.shape, 1)
         logits = jnp.where(lane < count, logits, -1e30)
         expo = jnp.exp(logits - jnp.max(logits, axis=1, keepdims=True))
@@ -405,8 +405,8 @@
 
 
 class Gather:
-    def __init__(self, rows, order):
-        self.order, self.half, self.done = order, len(order) // 2, 0
+    def __init__(self, rows, order, name):
+        self.order, self.half, self.done, self.name = order, len(order) // 2, 0, name
         self.blocks = {0: rows}
 
     def step(self, *waits):
@@ -417,24 +417,32 @@
             ahead, back = ahead[:cut], back[cut:]
         if waits:
             ahead, back = lax.optimization_barrier((ahead, back, *waits))[:2]
-        ahead, back = ring_shift(ahead, self.order, 1), ring_shift(back, self.order, -1)
+        with jax.named_scope(self.name):
+            ahead, back = ring_shift(ahead, self.order, 1), ring_shift(back, self.order, -1)
         if s == self.half:
-            self.blocks[s] = jnp.concatenate([ahead, back], axis=0)
+            self.parts = ahead, back
         else:
             self.blocks[-s], self.blocks[s] = ahead, back
 
 
+    def join(self, *waits):
+        parts = lax.optimization_barrier((*self.parts, *waits))[:2] if waits else self.parts
+        self.blocks[self.half] = jnp.concatenate(parts, axis=0)
+
+
 class Scatter:
-    def __init__(self, far, order, *waits):
-        self.order, self.cut, self.first = order, far.shape[0] // 2, True
+    def __init__(self, far, order, name, *waits):
+        self.order, self.cut, self.first, self.name = order, far.shape[0] // 2, True, name
         self.send(far[: self.cut], far[self.cut :], waits)
 
     def send(self, ahead, back, waits):
         ahead, back = ahead.astype(jnp.bfloat16), back.astype(jnp.bfloat16)
         if waits:
             ahead, back = lax.optimization_barrier((ahead, back, *waits))[:2]
-        self.ahead = ring_shift(ahead, self.order, 1).astype(jnp.float32)
-        self.back = ring_shift(back, self.order, -1).astype(jnp.float32)
+        self.sent = (ahead, back)
+        with jax.named_scope(self.name):
+            self.ahead = ring_shift(ahead, self.order, 1).astype(jnp.float32)
+            self.back = ring_shift(back, self.order, -1).astype(jnp.float32)
 
     def step(self, mine, other, *waits):
         mine, other = mine.astype(jnp.float32), other.astype(jnp.float32)
@@ -466,25 +474,37 @@
     return values
 
 
-def gather_small(rows, axis):
-    size, step, me = lax.axis_size(axis), 1, lax.axis_index(axis)
-    while step < size:
-        other = lax.ppermute(rows, axis, [(i, i ^ step) for i in range(size)])
-        upper = (me // step) % 2 == 1
-        rows = jnp.concatenate(
-            [jnp.where(upper, other, rows), jnp.where(upper, rows, other)], axis=0
-        )
-        step *= 2
-    return rows
+class Sum:
+    def __init__(self, values):
+        self.values = values
+        self.left = [
+            (axis, 1 << b)
+            for axis in ("expert", "dp")
+            for b in range(lax.axis_size(axis).bit_length() - 1)
+        ]
+
+    def step(self, *waits):
+        if not self.left:
+            return
+        axis, bit = self.left.pop(0)
+        values = after(self.values, *waits) if waits else self.values
+        with jax.named_scope("sum_small"):
+            other = lax.ppermute(values, axis, [(i, i ^ bit) for i in range(lax.axis_size(axis))])
+        self.values = values + other
+
+    def finish(self):
+        while self.left:
+            self.step()
+        return self.values
 
 
 def after(values, *others):
     return lax.optimization_barrier((values, *others))[0]
 
 
-def weight_kernel(parts, adds, index_ref, *refs):
+def weight_kernel(parts, adds, outs, index_ref, *refs):
     left_refs, right_ref, refs = refs[:parts], refs[parts], refs[parts + 1 :]
-    add_refs, out_ref, left = refs[: adds * parts], refs[-2], refs[-1]
+    add_refs, out_refs, left = refs[:adds], refs[adds : adds + outs], refs[-1]
     tile = left_refs[0].shape[1]
 
     @pl.when(pl.program_id(0) == 0)
@@ -493,17 +513,21 @@
             left[p * tile : (p + 1) * tile, :] = ref[...].T
 
     total = dot_nn(left[...], right_ref[...])
-    for p in range(parts):
-        part = total[p * tile : (p + 1) * tile]
-        for a in range(adds):
-            part = part + add_refs[a * parts + p][...].astype(jnp.float32)
-        out_ref[p * tile : (p + 1) * tile, :] = part.astype(out_ref.dtype)
-
-
-def weight_part(left, right, tile, columns, adds, dtype, name):
+    height = parts * tile // outs
+    for o, out_ref in enumerate(out_refs):
+        for p in range(parts // outs):
+            at = o * height + p * tile
+            part = total[at : at + tile]
+            if adds:
+                part = part + add_refs[at // tile][...].astype(jnp.float32)
+            out_ref[p * tile : (p + 1) * tile, :] = part.astype(out_ref.dtype)
+
+
+def weight_part(left, right, tile, columns, add, add_rows, types, name):
     rows, width, wide = left.shape[0], right.shape[1], WIDE
-    parts = len(columns)
-    places = list(columns) + [t for _, tiles in adds for t in tiles]
+    parts, adds, outs = len(columns), len(add_rows), len(types)
+    places = list(columns) + list(add_rows)
+    height = parts * tile // outs
     in_specs = [
         pl.BlockSpec((rows, tile), lambda j, at, p=p: (0, at[p])) for p in range(parts)
     ] + [pl.BlockSpec((rows, wide), lambda j, at: (0, j))]
@@ -512,15 +536,15 @@
         for p in range(parts, len(places))
     ]
     return pl.pallas_call(
-        functools.partial(weight_kernel, parts, len(adds)),
+        functools.partial(weight_kernel, parts, adds, outs),
         grid_spec=pltpu.PrefetchScalarGridSpec(
             num_scalar_prefetch=1,
             grid=(width // wide,),
             in_specs=in_specs,
-            out_specs=pl.BlockSpec((parts * tile, wide), lambda j, at: (0, j)),
+            out_specs=[pl.BlockSpec((height, wide), lambda j, at: (0, j))] * outs,
             scratch_shapes=[pltpu.VMEM((parts * tile, rows), jnp.bfloat16)],
         ),
-        out_shape=jax.ShapeDtypeStruct((parts * tile, width), dtype),
+        out_shape=[jax.ShapeDtypeStruct((height, width), t) for t in types],
         compiler_params=params(),
         cost_estimate=pl.CostEstimate(
             flops=2 * rows * parts * tile * width,
@@ -528,12 +552,7 @@
             transcendentals=0,
         ),
         name=name,
-    )(
-        jnp.stack([jnp.asarray(p, jnp.int32) for p in places]),
-        *[left] * parts,
-        right,
-        *[a for a, tiles in adds for _ in tiles],
-    )
+    )(jnp.stack([jnp.asarray(p, jnp.int32) for p in places]), *[left] * parts, right, *[add] * adds)
 
 
 class GroupSum:
@@ -545,47 +564,44 @@
         self.tile = left.shape[1] // outer // self.size
 
     def tiles(self, core, pairs):
-        return [4 * o + 2 * pair + core for o in range(self.outer) for pair in pairs]
-
-    def part(self, columns, adds, dtype, waits):
+        return [4 * o + 2 * pair + core for pair in pairs for o in range(self.outer)]
+
+    def first(self, *waits):
         left = after(self.left, *waits) if waits else self.left
-        return weight_part(left, self.right, self.tile, columns, adds, dtype, self.name)
-
-    def first(self, *waits):
         if self.size != 4:
-            left = after(self.left, *waits) if waits else self.left
             terms = dot_tn(left, self.right).astype(jnp.bfloat16)
             terms = terms.reshape(self.outer, -1, terms.shape[1])
-            self.far = lax.psum_scatter(terms, "dp", scatter_dimension=1, tiled=True)
+            self.far = self.near = lax.psum_scatter(terms, "dp", scatter_dimension=1, tiled=True)
             return
         columns = self.tiles(1 - self.core, (0, 1))
-        self.far = self.part(columns, [], jnp.bfloat16, waits)
-        self.got = lax.ppermute(self.far, "dp", [(i, i ^ 1) for i in range(4)])
-
-    def halves(self, pair):
-        return [2 * o + pair for o in range(self.outer)]
+        (self.far,) = weight_part(
+            left, self.right, self.tile, columns, None, [], [jnp.bfloat16], self.name
+        )
+        with jax.named_scope(self.name + "_cores"):
+            self.got = lax.ppermute(self.far, "dp", [(i, i ^ 1) for i in range(4)])
 
     def second(self, *waits):
         if self.size != 4:
             return
-        other = 1 - self.pair
-        terms = self.part(
-            self.tiles(self.core, (other,)),
-            [(self.got, self.halves(other))],
-            jnp.bfloat16,
-            waits,
+        left = after(self.left, *waits) if waits else self.left
+        pairs = (1 - self.pair, self.pair)
+        self.near, self.own = weight_part(
+            left,
+            self.right,
+            self.tile,
+            self.tiles(self.core, pairs),
+            self.got,
+            [pair * self.outer + o for pair in pairs for o in range(self.outer)],
+            [jnp.bfloat16, jnp.float32],
+            self.name,
         )
-        self.near = lax.ppermute(terms, "dp", [(i, i ^ 2) for i in range(4)])
-
-    def third(self, *waits):
+        with jax.named_scope(self.name + "_groups"):
+            self.back = lax.ppermute(self.near, "dp", [(i, i ^ 2) for i in range(4)])
+
+    def total(self):
         if self.size != 4:
             return self.far.reshape(-1, self.far.shape[-1]).astype(jnp.float32)
-        return self.part(
-            self.tiles(self.core, (self.pair,)),
-            [(self.got, self.halves(self.pair)), (self.near, range(self.outer))],
-            jnp.float32,
-            waits,
-        )
+        return self.own + self.back.astype(jnp.float32)
 
 
 def body(
@@ -650,65 +666,73 @@
 
     inputs = to_rows(tokens).astype(f32)
     normed = norm_rows(inputs, attn_gain)
-    normed_ring = Gather(normed.astype(bf16), order)
+
+    lanes = 128
+    picked_ids = to_rows(routes)
+    chosen = jnp.sum(
+        (picked_ids[:, :, None] == jnp.arange(experts_all)[None, None, :]).astype(f32), axis=1
+    )
+    hits = jnp.concatenate([chosen, valid_rows[:, None]], axis=1)
+    hits = jnp.pad(hits, ((0, 0), (0, lanes - experts_all - 1)))
+    normed_ring = Gather(
+        jnp.concatenate([normed.astype(bf16), hits.astype(bf16)], axis=1), order, "ring_normed"
+    )
     normed_ring.step()
 
     row_count = qkv_weight.shape[0]
     w_cols = qkv_weight.reshape(row_count, 3, n_expert, heads_here, HD).transpose(2, 0, 3, 1, 4)
     w_cols = lax.all_to_all(
-        after(w_cols.reshape(n_expert, row_count, 3 * cols), normed_ring.blocks[1]),
+        after(
+            w_cols.reshape(n_expert, row_count, 3 * cols),
+            normed_ring.blocks[1],
+            normed_ring.blocks[-1],
+        ),
         "expert",
         split_axis=0,
         concat_axis=0,
         tiled=True,
     )
     w_qkv = lax.all_gather(w_cols.reshape(-1, 3 * cols), "dp", axis=0, tiled=True)
-    w_out = lax.all_gather(out_weight, "expert", axis=0, tiled=True)
-    for _ in range(half - 1):
-        normed_ring.step()
-    normed_all = blockwise(normed_ring.blocks)
-    w_out = lax.all_gather(after(w_out, normed_all), "dp", axis=0, tiled=True)
-    cot_rows = to_rows(cotangent)
-    cot_ring = Gather(cot_rows, order)
-    cot_ring.step(normed_all)
-
-    picked_ids = to_rows(routes)
-    chosen = jnp.sum(
-        (picked_ids[:, :, None] == jnp.arange(experts_all)[None, None, :]).astype(f32), axis=1
-    )
-    lanes = 128
-    hits = jnp.concatenate([chosen, valid_rows[:, None]], axis=1).T
-    hits = jnp.pad(hits, ((0, -hits.shape[0] % 16), (0, 0))).astype(bf16)
-    hits_all = gather_small(hits[None], "expert")
-    hits_of = {
-        r: jnp.pad(
-            lax.dynamic_index_in_dim(hits_all, owner[r], 0, False).T.astype(f32),
-            ((0, 0), (0, lanes - hits.shape[0])),
-        )
-        for r in offsets
-    }
     router_pad = jnp.pad(router_weight, ((0, 0), (0, lanes - experts_all)))
     own_ids = member * experts_here + jnp.arange(experts_here)
     own_rows = (own_ids[:, None] == jnp.arange(lanes)[None, :]).astype(f32)
+
+    for _ in range(half - 2):
+        normed_ring.step()
+    w_out = lax.all_gather(
+        after(out_weight, normed_ring.blocks[half - 1], normed_ring.blocks[1 - half]),
+        "expert",
+        axis=0,
+        tiled=True,
+    )
+    normed_ring.step()
+    normed_ring.join()
+    hits_of = {r: normed_ring.blocks[r][:, width:] for r in offsets}
+    normed_all = blockwise({r: normed_ring.blocks[r][:, :width] for r in offsets})
+    hits_all = blockwise(hits_of).astype(f32)
+    counts = jnp.sum(hits_all[:, experts_all : experts_all + 1] * hits_all, axis=0)
+    count_total = sum_over(counts[:experts_all], "dp")
     n_valid = jnp.sum(lengths).astype(f32)
-    count_total = sum_over(
-        sum_over(jnp.sum(valid_rows[:, None] * chosen, axis=0), "expert"), "dp"
-    )
     fraction = count_total / (TOPK * n_valid)
+    cot_rows = to_rows(cotangent)
+    cot_ring = Gather(cot_rows, order, "ring_cotangent")
+    cot_ring.step(normed_all)
 
     project = dot_nn(normed_all, w_qkv).reshape(n_expert, seq_count, slot_count, 3 * cols)
-    cot_ring.step(project)
     attended = attend(owners, project, cosine, sine, key_live, head_gains)
+    w_out = lax.all_gather(after(w_out, attended), "dp", axis=0, tiled=True)
+    attended = after(attended, cot_ring.blocks[1], cot_ring.blocks[-1])
+    cot_ring.step(attended)
     attended_low = lax.all_to_all(
         attended.reshape(n_expert, tok_rows, cols), "expert", split_axis=0, concat_axis=0, tiled=True
     )
     attended_low = jnp.swapaxes(attended_low, 0, 1).reshape(tok_rows, width)
-    for _ in range(half - 3):
-        cot_ring.step(attended_low)
     residual = inputs + dot_nn(attended_low, w_out)
     ffn_normed, ffn_back = jax.vjp(norm_rows, residual, ffn_gain)
     ffn_low = ffn_normed.astype(bf16)
-    ffn_ring = Gather(ffn_low, order)
+    for _ in range(half - 3):
+        cot_ring.step(residual)
+    ffn_ring = Gather(ffn_low, order, "ring_ffn")
     ffn_ring.step()
 
     live = valid_rows[:, None]
@@ -728,7 +752,12 @@
     held, mix_blocks, group_gates = [], {}, []
     for i, g in enumerate(groups):
         *held, gates, mixed = experts_forward(
-            [ffn_ring.blocks[r] for r in g],
+            [
+                after(ffn_ring.blocks[r], cot_ring.blocks[half - 1], cot_ring.blocks[1 - half])
+                if i == 2
+                else ffn_ring.blocks[r]
+                for r in g
+            ],
             jnp.concatenate([hits_of[r] for r in g], axis=0),
             router_pad,
             own_rows,
@@ -743,15 +772,20 @@
         mix_blocks.update(split(mixed, g))
         if i < half - 1:
             ffn_ring.step(mixed)
+        if i == half - 1:
+            ffn_ring.join()
         if i == 1:
             cot_ring.step(mixed)
+    cot_ring.join(gates)
     x_all, gate_all, up_all, gated_all = held
     held, ffn_sum = [], None
+    mix_sum = Scatter(mix_blocks[half], order, "ring_mixture")
+    ready = ()
     for i in reversed(range(len(groups))):
         g = groups[i]
         *held, scores, grads = experts_backward(
             [cot_ring.blocks[r] for r in g],
-            group_gates[i],
+            after(group_gates[i], *ready) if ready else group_gates[i],
             own_rows,
             gate_all,
             up_all,
@@ -762,14 +796,23 @@
         )
         grads = jnp.concatenate([grads, scores.astype(bf16)], axis=1)
         if i == half:
-            ffn_sum = Scatter(grads, order)
+            ffn_sum = Scatter(grads, order, "ring_ffn_grad")
         elif i > 0:
             ffn_sum.step(grads[tok_rows:], grads[:tok_rows])
+        if 1 < i < half:
+            mix_sum.step(mix_blocks[i], mix_blocks[-i], grads)
+        ready = (*mix_sum.sent, *ffn_sum.sent)
     out_all, gate_grad_all, up_grad_all = held
-    ffn_grad = ffn_sum.finish(grads)
+    sums = [
+        GroupSum(gated_all, out_all, experts_here, "weights_out"),
+        GroupSum(x_all, gate_grad_all, 1, "weights_gate"),
+        GroupSum(x_all, up_grad_all, 1, "weights_up"),
+    ]
+    sums[0].first()
+    ffn_grad = ffn_sum.finish(after(grads, sums[0].far))
     gate_grads = ffn_grad[:, width : width + experts_all] * chosen
     ffn_grad = ffn_grad[:, :width]
-    mix_sum = Scatter(mix_blocks[half], order, ffn_grad)
+    mix_sum.step(mix_blocks[1], mix_blocks[-1], ffn_grad)
     picked_grad = (
         live
         * chosen
@@ -789,7 +832,6 @@
     branch_grad = residual_grad.astype(bf16)
 
     attended_grad = dot_nt(branch_grad, w_out).astype(bf16)
-    mix_sum.step(mix_blocks[half - 1], mix_blocks[1 - half], attended_grad)
     attended_grad = lax.all_to_all(
         jnp.swapaxes(attended_grad.reshape(tok_rows, n_expert, cols), 0, 1),
         "expert",
@@ -799,48 +841,60 @@
     ).reshape(attended.shape)
 
     output_terms = dot_tn(attended_low, branch_grad).astype(bf16)
-    grad_out = lax.psum_scatter(
-        lax.psum_scatter(output_terms, "dp", scatter_dimension=0, tiled=True),
-        "expert",
-        scatter_dimension=0,
-        tiled=True,
-    ).astype(f32)
-    sums = [
-        GroupSum(gated_all, out_all, experts_here, "weights_out"),
-        GroupSum(x_all, gate_grad_all, 1, "weights_gate"),
-        GroupSum(x_all, up_grad_all, 1, "weights_up"),
-    ]
-    sums[0].first(branch_grad)
-    attended_grad = after(attended_grad, sums[0].far)
-
+    out_share = lax.psum_scatter(output_terms, "dp", scatter_dimension=0, tiled=True)
+    sums[0].second(branch_grad)
+    attended_grad = after(attended_grad, sums[0].near, output_terms)
+
+    block_rows = residual + mix_sum.finish(mix_blocks[0])
+    attended_grad = after(attended_grad, block_rows)
     proj_grad, gain_parts = attend_back(
         owners, project, attended_grad, cosine, sine, key_live, head_gains
     )
-    for s in range(half - 2, 0, -1):
-        mix_sum.step(mix_blocks[s], mix_blocks[-s], proj_grad if s == 1 else attended_grad)
     proj_grad = proj_grad.reshape(all_rows, 3 * cols)
     normed_terms = dot_nt(proj_grad, w_qkv).astype(bf16)
     normed_parts = {
         r: normed_terms[i * tok_rows : (i + 1) * tok_rows] for i, r in enumerate(offsets)
     }
-    normed_sum = Scatter(normed_parts[half], order)
-    proj_terms = dot_tn(after(normed_all, normed_terms), proj_grad).astype(bf16)
+    normed_sum = Scatter(normed_parts[half], order, "ring_normed_grad")
+    attn_gain_terms = (
+        jnp.sum(normed_terms.astype(f32) * normed_all.astype(f32), axis=0) / attn_gain
+    )
+    head_gain_grads = jnp.sum(gain_parts, axis=(0, 1)).reshape(-1)
+    small = Sum(
+        jnp.concatenate(
+            [
+                router_terms.reshape(-1),
+                ffn_gain_terms,
+                attn_gain_terms,
+                head_gain_grads,
+                prob_sums,
+            ]
+        )
+    )
+    sums[1].first(normed_terms)
+    waits = [sums[1].far]
+    for s in range(half - 1, 0, -1):
+        normed_sum.step(normed_parts[s], normed_parts[-s], *waits)
+        waits = []
+        if s == half - 1:
+            sums[1].second(normed_terms)
+            proj_terms = dot_tn(after(normed_all, sums[1].near), proj_grad).astype(bf16)
+            waits = [sums[1].near, proj_terms]
+        if s == half - 2:
+            sums[2].first(proj_terms)
+            waits = [sums[2].far]
+        if s == half - 3:
+            sums[2].second(proj_terms)
     proj_share = lax.psum_scatter(proj_terms, "dp", scatter_dimension=0, tiled=True)
-    sums[0].second(proj_terms)
-    sums[1].first(proj_terms)
-    for s in range(half - 1, 0, -1):
-        normed_sum.step(normed_parts[s], normed_parts[-s])
-        if s == half - 1:
-            sums[2].first(normed_sum.ahead, sums[1].far)
-            sums[1].second(sums[2].far)
-        if s == half - 2:
-            sums[2].second(normed_sum.ahead)
-    normed_grad = normed_sum.finish(normed_parts[0])
+    normed_grad = normed_sum.finish(after(normed_parts[0], sums[2].near))
+    grad_out = lax.psum_scatter(
+        out_share, "expert", scatter_dimension=0, tiled=True
+    ).astype(f32)
     (input_norm_grad,) = jax.vjp(lambda v: norm_rows(v, attn_gain), inputs)[1](normed_grad)
     grad_tokens = from_rows(residual_grad + input_norm_grad)
-    block_out = from_rows(residual + mix_sum.finish(mix_blocks[0]))
-    grad_expert_out = sums[0].third(normed_sum.ahead).reshape(experts_here, -1, width)
-    shares = [sums[1].third(normed_sum.ahead), sums[2].third(normed_sum.ahead)]
+    block_out = from_rows(block_rows)
+    grad_expert_out = sums[0].total().reshape(experts_here, -1, width)
+    shares = [sums[1].total(), sums[2].total()]
     grad_expert_in = jnp.stack(
         [
             jnp.concatenate([s[:, e * FF : (e + 1) * FF] for s in shares], axis=1)
@@ -857,29 +911,28 @@
     ).reshape(n_expert, row_count, heads_here, 3, HD)
     grad_qkv = grad_qkv.transpose(1, 3, 0, 2, 4).reshape(row_count, 3, width).astype(f32)
 
-    early = jnp.concatenate([router_terms.reshape(-1), ffn_gain_terms, prob_sums])
-    early = sum_over(sum_over(early, "expert"), "dp")
-    grad_router = early[: width * experts_all].reshape(width, experts_all)
-    grad_ffn_gain = early[width * experts_all : width * experts_all + width]
-    prob_total = early[width * experts_all + width :]
-    head_gain_grads = jnp.sum(gain_parts, axis=(0, 1)).reshape(-1)
-    attn_gain_terms = (
-        jnp.sum(normed_terms.astype(f32) * normed_all.astype(f32), axis=0) / attn_gain
-    )
-    late = jnp.concatenate([attn_gain_terms, head_gain_grads])
-    late = sum_over(sum_over(late, "expert"), "dp")
+    small.step(normed_grad)
+    for _ in range(n_expert.bit_length() - 2):
+        small.step()
+    small.step(grad_qkv)
+    small = small.finish()
+    places, pieces = 0, []
+    for size in (width * experts_all, width, width, HD, HD, experts_all):
+        pieces.append(small[places : places + size])
+        places += size
+    grad_router, grad_ffn_gain, grad_attn_gain, grad_q_gain, grad_k_gain, prob_total = pieces
     balance_loss = balance_coef * experts_all * jnp.sum(fraction * (prob_total / n_valid))
     return (
         block_out,
         balance_loss,
         grad_tokens,
-        late[:width],
-        late[width : width + HD],
-        late[width + HD :],
+        grad_attn_gain,
+        grad_q_gain,
+        grad_k_gain,
         grad_qkv,
         grad_out,
         grad_ffn_gain,
-        grad_router,
+        grad_router.reshape(width, experts_all),
         grad_expert_in,
         grad_expert_out,
     )

time: 1040 us -> 951 us (0.914)
  waiting for transfers between devices: 294 us -> 229 us
  Pallas kernels: 374 us -> 359 us
  between operations: 34 us -> 19 us
  local copies, waits for them, and re-layouts: 67.2 us -> 79.6 us
    ppermute x6 -> x8, waiting for transfers between devices: 67.2 us -> 20.1 us  [the longest x5 20.1 us: step(): lax.ppermute(values, axis, [(i, i ^ bit) for i in range(lax.axis_size(axi...]
    ppermute x15 -> x2, waiting for transfers between devices: 33.7 us -> 0.46 us  [sum_over(): lax.ppermute(values, axis, [(i, i ^ step) for i in range(size)])]
    pallas_call x9 -> x6, Pallas kernels: 111 us -> 95.3 us  [weight_part(): pl.pallas_call(functools.partial(weight_kernel, parts, adds, outs), grid_...]
    ppermute x48, waiting for transfers between devices: 192 us -> 177 us  [ring_shift(): return lax.ppermute(rows, 'expert', pairs)]
    ppermute x15 -> x2, starting transfers between devices: 16 us -> 1.53 us  [sum_over(): lax.ppermute(values, axis, [(i, i ^ step) for i in range(size)])]
    all_to_all x1, waiting for transfers between devices: 0.01 us -> 12.1 us  [body(): lax.all_to_all(attended.reshape(n_expert, tok_rows, cols), 'expert', spli...]
    unnamed x130 -> x162, local copies, waits for them, and re-layouts: 21 us -> 29.8 us
    convert_element_type x7 -> x6, other arithmetic: 21.6 us -> 15.2 us  [send(): ahead, back = (ahead.astype(jnp.bfloat16), back.astype(jnp.bfloat16))]
  transfers between devices with their start and end apart: 81 -> 70, of which waited for: 33 -> 33; matrix products, arithmetic and copies ran while one was open for 16% -> 20% of each run, Pallas kernels for 33% -> 38%
where the time goes in v3:
time: 951 us; the launch traced here: 942 us
  Pallas kernels  359 us (38%)
  waiting for transfers between devices  229 us (24%)
  starting transfers between devices  91 us (10%)
  other arithmetic  84.2 us (9%)
  local copies, waits for them, and re-layouts  79.6 us (8%)
  matrix products  56.8 us (6%)
  blocking collectives  24 us (3%)
  between operations  19 us (2%)
    ppermute x48, waiting for transfers between devices, ring_shift(): return lax.ppermute(rows, 'expert', pairs)  177 us
    pallas_call x5, Pallas kernels, experts_forward(): pl.pallas_call(functools.partial(experts_kernel, len(xs), len(held), tile...  107 us
    pallas_call x5, Pallas kernels, experts_backward(): pl.pallas_call(functools.partial(experts_back_kernel, len(outs), len(held...  106 us
    pallas_call x6, Pallas kernels, weight_part(): pl.pallas_call(functools.partial(weight_kernel, parts, adds, outs), grid_...  95.3 us
    ppermute x48, starting transfers between devices, ring_shift(): return lax.ppermute(rows, 'expert', pairs)  58 us
    pallas_call x1, Pallas kernels, attend_back(): pl.pallas_call(attend_back_kernel, grid_spec=pltpu.PrefetchScalarGridSpec...  31.8 us
    unnamed x162, local copies, waits for them, and re-layouts  29.8 us
    all_to_all x1, blocking collectives, body(): lax.all_to_all(after(w_cols.reshape(n_expert, row_count, 3 * cols), norme...  24 us
  transfers between devices with their start and end apart: 70, of which 33 were waited for; matrix products, arithmetic and copies ran while one was open for 20% of the time, Pallas kernels for 38%

profile of v3, /device:TPU:0, one launch (start us, length us, event | category | flops | bytes accessed | tf_op | source)
XLA Modules:
  0.0 942.1 jit_solution(13174011362849267936)
XLA Ops:
  29.3 19.7 %collective-permute-done.1 = bf16[256,2176]{1,0:T(8,128)(2,1)} collective-permute-done((bf16[256,2176]{1,0:T(8,128)(2,1)}, bf16[256,2176]{1,0:T(8,128)(2,1)}, u32[]{:S(2)}, u32[]{:S(2)}) %collective-permute-start.1) | collective-permute-done | bytes 1114144 | tf_op jit(solution)/shard_map/ring_normed/ppermute | solution.py:404
  50.4 24.0 %all_to_all.20 = bf16[8,64,768]{2,1,0:T(8,128)(2,1)} all-to-all(bf16[8,64,768]{2,1,0:T(8,128)(2,1)} %reshape.295), channel_id=1, replica_groups=mesh['dp'=4,'expert'=8] {'expert'}, dimensions={0} | all-to-all | bytes 1572864 | tf_op jit(solution)/shard_map/all_to_all | solution.py:684
  85.3 16.9 %collective-permute-done.3 = bf16[256,2176]{1,0:T(8,128)(2,1)S(1)} collective-permute-done((bf16[256,2176]{1,0:T(8,128)(2,1)}, bf16[256,2176]{1,0:T(8,128)(2,1)S(1)}, u32[]{:S(2)}, u32[]{:S(2)}) %collective-permute-start.3) | collective-permute-done | bytes 1114144 | tf_op jit(solution)/shard_map/ring_normed/ppermute | solution.py:404
  108.7 17.6 %collective-permute-done.5 = bf16[256,2176]{1,0:T(8,128)(2,1)S(1)} collective-permute-done((bf16[256,2176]{1,0:T(8,128)(2,1)S(1)}, bf16[256,2176]{1,0:T(8,128)(2,1)S(1)}, u32[]{:S(2)}, u32[]{:S(2)}) %collective-permute-start.5) | collective-permute-done | bytes 1114144 | tf_op jit(solution)/shard_map/ring_normed/ppermute | solution.py:404
  146.0 11.7 %fusion.36 = f32[2048,768]{1,0:T(8,128)} fusion(bf16[2048,2048]{1,0:T(8,128)(2,1)} %slice_dynamic-update-slice_fusion, bf16[2048,768]{1,0:T(8,128)(2,1)} %all-gather.4.cloned.1.call-done), kind=kOutput, calls=%fused_computation.182 | convolution fusion | flops 6442450944 | bytes 17825792 | tf_op jit(solution)/shard_map/dot_general | solution.py:39
  157.7 18.5 %attend.1 = bf16[8,2,128,256]{3,2,1,0:T(8,128)(2,1)} custom-call(s32[8]{0:T(128)} %dynamic-slice_bitcast_fusion.owner_ref, f32[8,2,128,768]{3,2,1,0:T(8,128)} %bitcast.151, f32[1024,128]{1,0:T(8,128)} %get-tuple-element.380.cos_ref, f32[1024,128]{1,0:T(8,128)} %get-tuple-element.381.sin_ref, f32[2,1,1024]{2,1,0:T(1,128)} %compare_convert_fusion.live_ref, ...), custom_call_target="tpu_custom_call" | custom-call | flops 2147483648 | bytes 7864320 | tf_op jit(solution)/shard_map/attend/pallas_call | solution.py:105
  196.4 10.5 %collective-permute-done.8.refs_1_ = bf16[256,2048]{1,0:T(8,128)(2,1)} collective-permute-done((bf16[256,2048]{1,0:T(8,128)(2,1)S(1)}, bf16[256,2048]{1,0:T(8,128)(2,1)}, u32[]{:S(2)}, u32[]{:S(2)}) %collective-permute-start.8) | collective-permute-done | bytes 1048608 | tf_op jit(solution)/shard_map/ring_cotangent/ppermute | solution.py:404
  229.5 12.1 %all-to-all-done.1 = bf16[8,256,256]{1,2,0:T(8,128)(2,1)S(1)} async-done(((bf16[8,256,256]{1,2,0:T(8,128)(2,1)}), bf16[8,256,256]{1,2,0:T(8,128)(2,1)S(1)}, u32[]{:S(2)}, u32[]{:S(2)}) %all-to-all-start.1) | async-done | bytes 1048608 | tf_op jit(solution)/shard_map/all_to_all | solution.py:726
  266.8 17.7 %experts_forward.5 = (bf16[2048,2048]{1,0:T(8,128)(2,1)}, bf16[2048,2048]{1,0:T(8,128)(2,1)}, bf16[2048,2048]{1,0:T(8,128)(2,1)}, bf16[2048,2048]{1,0:T(8,128)(2...) custom-call(bf16[256,2048]{1,0:T(8,128)(2,1)} %copy-done.5, bf16[256,128]{1,0:T(8,128)(2,1)} %copy-done.44, ...), custom_call_target="tpu_custom_call" | custom-call | flops 6442450944 | bytes 30408704 | tf_op jit(solution)/shard_map/experts_forward/pallas_call | solution.py:272
  287.2 17.5 %collective-permute-done.15.refs_1_ = bf16[256,2048]{1,0:T(8,128)(2,1)S(1)} collective-permute-done((bf16[256,2048]{1,0:T(8,128)(2,1)}, bf16[256,2048]{1,0:T(8,128)(2,1)S(1)}, u32[]{:S(2)}, u32[]{:S(2)}) %collective-permute-start.15) | collective-permute-done | bytes 1048608 | tf_op jit(solution)/shard_map/ring_cotangent/ppermute | solution.py:404
  304.8 24.2 %experts_forward.6 = (bf16[2048,2048]{1,0:T(8,128)(2,1)}, bf16[2048,2048]{1,0:T(8,128)(2,1)}, bf16[2048,2048]{1,0:T(8,128)(2,1)}, bf16[2048,2048]{1,0:T(8,128)(2...) custom-call(bf16[256,2048]{1,0:T(8,128)(2,1)} %collective-permute-do, ...), custom_call_target="tpu_custom_call", output_to_operand_aliasing={{0}: (8, {}), {1}: (9, {}), {2}: (10, {}), {3}: (11, {})} | custom-call | flops 12884901888 | bytes 35651584 | tf_op jit(solution)/shard_map/experts_forward/pallas_call | solution.py:272
  336.1 23.6 %experts_forward.7 = (bf16[2048,2048]{1,0:T(8,128)(2,1)}, bf16[2048,2048]{1,0:T(8,128)(2,1)}, bf16[2048,2048]{1,0:T(8,128)(2,1)}, bf16[2048,2048]{1,0:T(8,128)(2...) custom-call(bf16[256,2048]{1,0:T(8,128)(2,1)} %copy-done.40, ...), custom_call_target="tpu_custom_call", output_to_operand_aliasing={{0}: (8, {}), {1}: (9, {}), {2}: (10, {}), {3}: (11, {})} | custom-call | flops 12884901888 | bytes 35651584 | tf_op jit(solution)/shard_map/experts_forward/pallas_call | solution.py:272
  369.3 23.6 %experts_forward.8 = (bf16[2048,2048]{1,0:T(8,128)(2,1)}, bf16[2048,2048]{1,0:T(8,128)(2,1)}, bf16[2048,2048]{1,0:T(8,128)(2,1)}, bf16[2048,2048]{1,0:T(8,128)(2...) custom-call(bf16[256,2048]{1,0:T(8,128)(2,1)} %copy-done.27, ...), custom_call_target="tpu_custom_call", output_to_operand_aliasing={{0}: (8, {}), {1}: (9, {}), {2}: (10, {}), {3}: (11, {})} | custom-call | flops 12884901888 | bytes 35651584 | tf_op jit(solution)/shard_map/experts_forward/pallas_call | solution.py:272
  395.3 17.8 %experts_forward.9 = (bf16[2048,2048]{1,0:T(8,128)(2,1)}, bf16[2048,2048]{1,0:T(8,128)(2,1)}, bf16[2048,2048]{1,0:T(8,128)(2,1)}, bf16[2048,2048]{1,0:T(8,128)(2...) custom-call(bf16[256,2048]{1,0:T(8,128)(2,1)} %pad_maximum_fusion.8., ...), custom_call_target="tpu_custom_call", output_to_operand_aliasing={{0}: (7, {}), {1}: (8, {}), {2}: (9, {}), {3}: (10, {})} | custom-call | flops 6442450944 | bytes 30408704 | tf_op jit(solution)/shard_map/experts_forward/pallas_call | solution.py:272
  417.7 17.2 %experts_backward.5 = (bf16[2048,2048]{1,0:T(8,128)(2,1)}, bf16[2048,2048]{1,0:T(8,128)(2,1)}, bf16[2048,2048]{1,0:T(8,128)(2,1)}, f32[256,128]{1,0:T(8,128)}, bf16[256,2048]{1,0:T(8,128)(2,1)}) custom-call(bf16[256,2048]{1,0:T(8,128)(2,1)} %pad_maximum_fusion.11.refs_0_, f32[256,2]{1,0:T(8,128)} %get-tuple-element.165.refs_1_, ...), custom_call_target="tpu_custom_call" | custom-call | flops 6442450944 | bytes 31457280 | tf_op jit(solution)/shard_map/experts_backward/pallas_call | solution.py:359
  439.5 24.0 %experts_backward.6 = (bf16[2048,2048]{1,0:T(8,128)(2,1)}, bf16[2048,2048]{1,0:T(8,128)(2,1)}, bf16[2048,2048]{1,0:T(8,128)(2,1)}, f32[512,128]{1,0:T(8,128)}, bf16[512,2048]{1,0:T(8,128)(2,1)}) custom-call(bf16[256,2048]{1,0:T(8,128)(2,1)} %copy-done.26, bf16[256,2048]{1,0:T(8,128)(2,1)} %copy-done.25, ...), custom_call_target="tpu_custom_call", output_to_operand_aliasing={{0}: (8, {}), {1}: (9, {}), {2}: (10, {})} | custom-call | flops 12884901888 | bytes 37748736 | tf_op jit(solution)/shard_map/experts_backward/pallas_call | solution.py:359
  472.2 23.9 %experts_backward.7 = (bf16[2048,2048]{1,0:T(8,128)(2,1)}, bf16[2048,2048]{1,0:T(8,128)(2,1)}, bf16[2048,2048]{1,0:T(8,128)(2,1)}, f32[512,128]{1,0:T(8,128)}, bf16[512,2048]{1,0:T(8,128)(2,1)}) custom-call(bf16[256,2048]{1,0:T(8,128)(2,1)} %collective-permute-done.13.refs_0_, ...), custom_call_target="tpu_custom_call", output_to_operand_aliasing={{0}: (8, {}), {1}: (9, {}), {2}: (10, {})} | custom-call | flops 12884901888 | bytes 37748736 | tf_op jit(solution)/shard_map/experts_backward/pallas_call | solution.py:359
  502.8 15.3 %collective-permute-done.33 = bf16[256,2176]{1,0:T(8,128)(2,1)S(1)} collective-permute-done((bf16[256,2176]{1,0:T(8,128)(2,1)S(1)}, bf16[256,2176]{1,0:T(8,128)(2,1)S(1)}, u32[]{:S(2)}, u32[]{:S(2)}) %collective-permute-start.33) | collective-permute-done | bytes 1114144 | tf_op jit(solution)/shard_map/ring_ffn_grad/ppermute | solution.py:404
  520.9 23.9 %experts_backward.8 = (bf16[2048,2048]{1,0:T(8,128)(2,1)}, bf16[2048,2048]{1,0:T(8,128)(2,1)}, bf16[2048,2048]{1,0:T(8,128)(2,1)}, f32[512,128]{1,0:T(8,128)}, bf16[512,2048]{1,0:T(8,128)(2,1)}) custom-call(bf16[256,2048]{1,0:T(8,128)(2,1)} %collective-permute-done.9.refs_0_, ...), custom_call_target="tpu_custom_call", output_to_operand_aliasing={{0}: (8, {}), {1}: (9, {}), {2}: (10, {})} | custom-call | flops 12884901888 | bytes 37748736 | tf_op jit(solution)/shard_map/experts_backward/pallas_call | solution.py:359
  551.8 12.3 %collective-permute-done.34 = bf16[256,2176]{1,0:T(8,128)(2,1)S(1)} collective-permute-done((bf16[256,2176]{1,0:T(8,128)(2,1)S(1)}, bf16[256,2176]{1,0:T(8,128)(2,1)S(1)}, u32[]{:S(2)}, u32[]{:S(2)}) %collective-permute-start.34) | collective-permute-done | bytes 1114144 | tf_op jit(solution)/shard_map/ring_ffn_grad/ppermute | solution.py:404
  567.1 17.2 %experts_backward.9 = (bf16[2048,2048]{1,0:T(8,128)(2,1)}, bf16[2048,2048]{1,0:T(8,128)(2,1)}, bf16[2048,2048]{1,0:T(8,128)(2,1)}, f32[256,128]{1,0:T(8,128)}, bf16[256,2048]{1,0:T(8,128)(2,1)}) custom-call(bf16[256,2048]{1,0:T(8,128)(2,1)} %bitcast.147, ...), custom_call_target="tpu_custom_call", output_to_operand_aliasing={{0}: (7, {}), {1}: (8, {}), {2}: (9, {})} | custom-call | flops 6442450944 | bytes 31457280 | tf_op jit(solution)/shard_map/experts_backward/pallas_call | solution.py:359
  586.5 15.3 %weights_out.2 = bf16[1024,2048]{1,0:T(8,128)(2,1)} custom-call(s32[4]{0:T(128)} %pad_add_fusion.index_ref, bf16[2048,2048]{1,0:T(8,128)(2,1)} %get-tuple-element.208.refs_0_.refs_1_.refs_2_.refs_3_, bf16[2048,2048]{1,0:T(8,128)(2,1)} %get-tuple-element.208.refs_0_.refs_1_.refs_2_.refs_3_, ...), custom_call_target="tpu_custom_call" | custom-call | flops 8589934592 | bytes 20971520 | tf_op jit(solution)/shard_map/weights_out/pallas_call | solution.py:538
  631.6 17.3 %weights_out.3 = (bf16[512,2048]{1,0:T(8,128)(2,1)}, f32[512,2048]{1,0:T(8,128)}) custom-call(s32[8]{0:T(128)} %stack.100.index_ref, bf16[2048,2048]{1,0:T(8,128)(2,1)} %get-tuple-element.208.refs_0_.refs_1_.refs_2_.refs_3_, bf16[2048,2048]{1,0:T(8,128)(2,1)} %get-tuple-element.208.refs_0_.refs_1_.refs_2_.refs_3_, ...), custom_call_target="tpu_custom_call" | custom-call | flops 8589934592 | bytes 20971520 | tf_op jit(solution)/shard_map/weights_out/pallas_call | solution.py:538
  657.8 31.8 %attend_back.1 = (bf16[8,2,128,768]{3,2,1,0:T(8,128)(2,1)}, f32[2,2,2,128]{3,2,1,0:T(2,128)}) custom-call(s32[8]{0:T(128)} %dynamic-slice_bitcast_fusion.owner_ref, f32[8,2,128,768]{3,2,1,0:T(8,128)} %bitcast.152, bf16[8,2,128,256]{3,2,1,0:T(8,128)(2,1)} %bitcast.160, f32[1024,128]{1,0:T(8,128)} %get-tuple-element.380.cos_ref, ...), custom_call_target="tpu_custom_call" | custom-call | flops 5368709120 | bytes 11010048 | tf_op jit(solution)/shard_map/attend_back/pallas_call | solution.py:176
  689.6 12.5 %multiply_reduce_fusion = (f32[2048]{0:T(1024)S(1)}, bf16[2048,2048]{1,0:T(8,128)(2,1)}) fusion(bf16[2048,2048]{1,0:T(8,128)(2,1)} %slice_dynamic-update-slice_fusion, bf16[2048,768]{1,0:T(8,128)(2,1)} %bitcast.168, bf16[2048,768]{1,0:T(8,128)(2,1)S(1)} %copy-done.70), kind=kOutput, calls=%fused_computation | convolution fusion | flops 6463420416 | bytes 23076864 | tf_op jit(solution)/shard_map/dot_general | solution.py:43
  702.1 15.3 %weights_gate.2 = bf16[1024,2048]{1,0:T(8,128)(2,1)} custom-call(s32[2]{0:T(128)} %pad_add_fusion.2.index_ref, bf16[2048,2048]{1,0:T(8,128)(2,1)} %get-tuple-element.219.refs_0_.refs_1_, bf16[2048,2048]{1,0:T(8,128)(2,1)} %get-tuple-element.219.refs_0_.refs_1_, bf16[2048,2048]{1,0:T(8,128)(2,1)} %get-tuple-element.216.refs_2_), custom_call_target="tpu_custom_call" | custom-call | flops 8589934592 | bytes 20971520 | tf_op jit(solution)/shard_map/weights_gate/pallas_call | solution.py:538
  726.8 15.9 %weights_gate.3 = (bf16[512,2048]{1,0:T(8,128)(2,1)}, f32[512,2048]{1,0:T(8,128)}) custom-call(s32[4]{0:T(128)} %pad_add_fusion.1.index_ref, bf16[2048,2048]{1,0:T(8,128)(2,1)} %get-tuple-element.219.refs_0_.refs_1_, bf16[2048,2048]{1,0:T(8,128)(2,1)} %get-tuple-element.219.refs_0_.refs_1_, bf16[2048,2048]{1,0:T(8,128)(2,1)} %get-tuple-element.216.refs_2_, ...), custom_call_target="tpu_custom_call" | custom-call | flops 8589934592 | bytes 20971520 | tf_op jit(solution)/shard_map/weights_gate/pallas_call | solution.py:538
  742.7 11.4 %convolution_convert_fusion.2 = bf16[2048,768]{1,0:T(8,128)(2,1)} fusion(bf16[2048,2048]{1,0:T(8,128)(2,1)} %slice_dynamic-update-slice_fusion, bf16[2048,768]{1,0:T(8,128)(2,1)} %bitcast.169), kind=kOutput, calls=%fused_computation.17 | convolution fusion | flops 6444023808 | bytes 14680064 | tf_op jit(solution)/shard_map/dot_general | solution.py:49
  754.2 15.2 %weights_up.2 = bf16[1024,2048]{1,0:T(8,128)(2,1)} custom-call(s32[2]{0:T(128)} %pad_add_fusion.2.index_ref, bf16[2048,2048]{1,0:T(8,128)(2,1)} %get-tuple-element.219.refs_0_.refs_1_, bf16[2048,2048]{1,0:T(8,128)(2,1)} %get-tuple-element.219.refs_0_.refs_1_, bf16[2048,2048]{1,0:T(8,128)(2,1)} %get-tuple-element.220.refs_2_), custom_call_target="tpu_custom_call" | custom-call | flops 8589934592 | bytes 20971520 | tf_op jit(solution)/shard_map/weights_up/pallas_call | solution.py:538
  781.9 17.5 %collective-permute-done.47 = bf16[256,2048]{1,0:T(8,128)(2,1)} collective-permute-done((bf16[256,2048]{1,0:T(8,128)(2,1)}, bf16[256,2048]{1,0:T(8,128)(2,1)}, u32[]{:S(2)}, u32[]{:S(2)}) %collective-permute-start.47) | collective-permute-done | bytes 1048608 | tf_op jit(solution)/shard_map/ring_normed_grad/ppermute | solution.py:404
  810.3 16.9 %collective-permute-done.49 = bf16[256,2048]{1,0:T(8,128)(2,1)S(1)} collective-permute-done((bf16[256,2048]{1,0:T(8,128)(2,1)S(1)}, bf16[256,2048]{1,0:T(8,128)(2,1)S(1)}, u32[]{:S(2)}, u32[]{:S(2)}) %collective-permute-start.49) | collective-permute-done | bytes 1048608 | tf_op jit(solution)/shard_map/ring_normed_grad/ppermute | solution.py:404
  834.4 16.3 %weights_up.3 = (bf16[512,2048]{1,0:T(8,128)(2,1)}, f32[512,2048]{1,0:T(8,128)}) custom-call(s32[4]{0:T(128)} %pad_add_fusion.1.index_ref, bf16[2048,2048]{1,0:T(8,128)(2,1)} %get-tuple-element.219.refs_0_.refs_1_, bf16[2048,2048]{1,0:T(8,128)(2,1)} %get-tuple-element.219.refs_0_.refs_1_, bf16[2048,2048]{1,0:T(8,128)(2,1)} %get-tuple-element.220.refs_2_, ...), custom_call_target="tpu_custom_call" | custom-call | flops 8589934592 | bytes 20971520 | tf_op jit(solution)/shard_map/weights_up/pallas_call | solution.py:538
  (430 shorter events, 348.4 us)
Async XLA Ops:
  7.2 138.8 %all-gather.4.cloned.1.call-start = ((), (), s32[]{:S(2)}) async-start(), calls=%async_computation.7 | async-start | bytes 3932160 | tf_op jit(solution)/shard_map/all_gather | solution.py:695
  74.4 106.9 %all-gather.6.cloned.1.call-start = ((), (), s32[]{:S(2)}) async-start(), calls=%async_computation.8 | async-start | bytes 2359296 | tf_op jit(solution)/shard_map/all_gather | solution.py:702
  131.1 110.5 %all-gather.8.cloned.1.call-start = ((), (), s32[]{:S(2)}) async-start(), calls=%async_computation.9 | async-start | bytes 10485760 | tf_op jit(solution)/shard_map/all_gather | solution.py:723
  214.5 640.3 %reduce-scatter.6.cloned.1.call-start = ((), (), s32[]{:S(2)}) async-start(), calls=%async_computation.11 | async-start | bytes 10485760 | tf_op jit(solution)/shard_map/reduce_scatter | solution.py:844
  226.0 38.9 %collective-permute-start.41 = (f32[16]{0:T(128)S(1)}, f32[16]{0:T(128)S(1)}, u32[]{:S(2)}, u32[]{:S(2)}) collective-permute-start(f32[16]{0:T(128)S(1)} %slice_add_fusion), channel_id=1, source_target_pairs={{0,16},{8,24},{16,0},{24,8},{1,17},{9,25},{17,1},{25,9},{2,18},{10... | collective-permute-start | bytes 200 | tf_op jit(solution)/shard_map/ppermute | solution.py:472
  248.1 36.4 %collective-permute-start.11 = (bf16[256,2048]{1,0:T(8,128)(2,1)S(1)}, bf16[256,2048]{1,0:T(8,128)(2,1)}, u32[]{:S(2)}, u32[]{:S(2)}) collective-permute-start(bf16[256,2048]{1,0:T(8,128)(2,1)S(1)} %multiply_convert_fusion.refs_0_), channel_id=1, source_target_pairs={{0,1},{2,0},{4,2},{6,4},{7,6},{5,7},{3,5},{1,3},{8,9},{10,8},{12,1... | collective-permute-start | bytes 3145736 | tf_op jit(solution)/shard_map/ring_ffn/ppermute | solution.py:404
  259.8 44.8 %collective-permute-start.15 = (bf16[256,2048]{1,0:T(8,128)(2,1)}, bf16[256,2048]{1,0:T(8,128)(2,1)S(1)}, u32[]{:S(2)}, u32[]{:S(2)}) collective-permute-start(bf16[256,2048]{1,0:T(8,128)(2,1)} %collective-permute-done.14.refs_1_), channel_id=1, source_target_pairs={{0,1},{2,0},{4,2},{6,4},{7,6},{5,7},{3,5},{1,3},{8,9},{10,8},{12,1... | collective-permute-start | bytes 3145736 | tf_op jit(solution)/shard_map/ring_cotangent/ppermute | solution.py:404
  260.0 44.7 %collective-permute-start.16 = (bf16[256,2048]{1,0:T(8,128)(2,1)}, bf16[256,2048]{1,0:T(8,128)(2,1)S(1)}, u32[]{:S(2)}, u32[]{:S(2)}) collective-permute-start(bf16[256,2048]{1,0:T(8,128)(2,1)} %collective-permute-done.13.refs_0_), channel_id=1, source_target_pairs={{0,2},{2,4},{4,6},{6,7},{7,5},{5,3},{3,1},{1,0},{8,10},{10,12},{12... | collective-permute-start | bytes 3145736 | tf_op jit(solution)/shard_map/ring_cotangent/ppermute | solution.py:404
  284.5 49.4 %collective-permute-start.12 = (bf16[256,2048]{1,0:T(8,128)(2,1)}, bf16[256,2048]{1,0:T(8,128)(2,1)S(1)}, u32[]{:S(2)}, u32[]{:S(2)}) collective-permute-start(bf16[256,2048]{1,0:T(8,128)(2,1)} %collective-permute-done.10.refs_0_), channel_id=1, source_target_pairs={{0,2},{2,4},{4,6},{6,7},{7,5},{5,3},{3,1},{1,0},{8,10},{10,12},{12... | collective-permute-start | bytes 3145736 | tf_op jit(solution)/shard_map/ring_ffn/ppermute | solution.py:404
  287.2 46.8 %collective-permute-start.17 = (bf16[256,2048]{1,0:T(8,128)(2,1)}, bf16[256,2048]{1,0:T(8,128)(2,1)S(1)}, u32[]{:S(2)}, u32[]{:S(2)}) collective-permute-start(bf16[256,2048]{1,0:T(8,128)(2,1)} %collective-permute-done.11.refs_1_), channel_id=1, source_target_pairs={{0,1},{2,0},{4,2},{6,4},{7,6},{5,7},{3,5},{1,3},{8,9},{10,8},{12,1... | collective-permute-start | bytes 3145736 | tf_op jit(solution)/shard_map/ring_ffn/ppermute | solution.py:404
  329.0 85.5 %collective-permute-start.24 = (bf16[128,2048]{1,0:T(8,128)(2,1)S(1)}, bf16[128,2048]{1,0:T(8,128)(2,1)S(1)}, u32[]{:S(2)}, u32[]{:S(2)}) collective-permute-start(bf16[128,2048]{1,0:T(8,128)(2,1)S(1)} %slice.340), channel_id=1, source_target_pairs={{0,2},{2,4},{4,6},{6,7},{7,5},{5,3},{3,1},{1,0},{8,10},{10,12},{12... | collective-permute-start | bytes 1572872 | tf_op jit(solution)/shard_map/ring_cotangent/ppermute | solution.py:404
  333.9 80.5 %collective-permute-start.25 = (bf16[128,2048]{1,0:T(8,128)(2,1)S(1)}, bf16[128,2048]{1,0:T(8,128)(2,1)S(1)}, u32[]{:S(2)}, u32[]{:S(2)}) collective-permute-start(bf16[128,2048]{1,0:T(8,128)(2,1)S(1)} %slice.341), channel_id=1, source_target_pairs={{0,1},{2,0},{4,2},{6,4},{7,6},{5,7},{3,5},{1,3},{8,9},{10,8},{12,1... | collective-permute-start | bytes 1572872 | tf_op jit(solution)/shard_map/ring_cotangent/ppermute | solution.py:404
  414.5 51.5 %collective-permute-start.23 = (bf16[128,2048]{1,0:T(8,128)(2,1)S(1)}, bf16[128,2048]{1,0:T(8,128)(2,1)S(1)}, u32[]{:S(2)}, u32[]{:S(2)}) collective-permute-start(bf16[128,2048]{1,0:T(8,128)(2,1)S(1)} %get-tuple-element.354), channel_id=1, source_target_pairs={{0,1},{2,0},{4,2},{6,4},{7,6},{5,7},{3,5},{1,3},{8,9},{10,8},{12,1... | collective-permute-start | bytes 1572872 | tf_op jit(solution)/shard_map/ring_mixture/ppermute | solution.py:404
  414.6 51.4 %collective-permute-start.22 = (bf16[128,2048]{1,0:T(8,128)(2,1)S(1)}, bf16[128,2048]{1,0:T(8,128)(2,1)S(1)}, u32[]{:S(2)}, u32[]{:S(2)}) collective-permute-start(bf16[128,2048]{1,0:T(8,128)(2,1)S(1)} %get-tuple-element.355), channel_id=1, source_target_pairs={{0,2},{2,4},{4,6},{6,7},{7,5},{5,3},{3,1},{1,0},{8,10},{10,12},{12... | collective-permute-start | bytes 1572872 | tf_op jit(solution)/shard_map/ring_mixture/ppermute | solution.py:404
  470.0 48.1 %collective-permute-start.33 = (bf16[256,2176]{1,0:T(8,128)(2,1)S(1)}, bf16[256,2176]{1,0:T(8,128)(2,1)S(1)}, u32[]{:S(2)}, u32[]{:S(2)}) collective-permute-start(bf16[256,2176]{1,0:T(8,128)(2,1)S(1)} %pad_maximum_fusion.6), channel_id=1, source_target_pairs={{0,1},{2,0},{4,2},{6,4},{7,6},{5,7},{3,5},{1,3},{8,9},{10,8},{12,1... | collective-permute-start | bytes 3342344 | tf_op jit(solution)/shard_map/ring_ffn_grad/ppermute | solution.py:404
  470.2 47.9 %collective-permute-start.32 = (bf16[256,2176]{1,0:T(8,128)(2,1)S(1)}, bf16[256,2176]{1,0:T(8,128)(2,1)S(1)}, u32[]{:S(2)}, u32[]{:S(2)}) collective-permute-start(bf16[256,2176]{1,0:T(8,128)(2,1)S(1)} %pad_maximum_fusion.5), channel_id=1, source_target_pairs={{0,2},{2,4},{4,6},{6,7},{7,5},{5,3},{3,1},{1,0},{8,10},{10,12},{12... | collective-permute-start | bytes 3342344 | tf_op jit(solution)/shard_map/ring_ffn_grad/ppermute | solution.py:404
  500.7 45.1 %collective-permute-start.30 = (bf16[256,2048]{1,0:T(8,128)(2,1)}, bf16[256,2048]{1,0:T(8,128)(2,1)}, u32[]{:S(2)}, u32[]{:S(2)}) collective-permute-start(bf16[256,2048]{1,0:T(8,128)(2,1)} %get-tuple-element.187), channel_id=1, source_target_pairs={{0,2},{2,4},{4,6},{6,7},{7,5},{5,3},{3,1},{1,0},{8,10},{10,12},{12... | collective-permute-start | bytes 3145736 | tf_op jit(solution)/shard_map/ring_mixture/ppermute | solution.py:404
  501.3 44.5 %collective-permute-start.31 = (bf16[256,2048]{1,0:T(8,128)(2,1)S(1)}, bf16[256,2048]{1,0:T(8,128)(2,1)}, u32[]{:S(2)}, u32[]{:S(2)}) collective-permute-start(bf16[256,2048]{1,0:T(8,128)(2,1)S(1)} %get-tuple-element.188), channel_id=1, source_target_pairs={{0,1},{2,0},{4,2},{6,4},{7,6},{5,7},{3,5},{1,3},{8,9},{10,8},{12,1... | collective-permute-start | bytes 3145736 | tf_op jit(solution)/shard_map/ring_mixture/ppermute | solution.py:404
  518.7 45.4 %collective-permute-start.34 = (bf16[256,2176]{1,0:T(8,128)(2,1)S(1)}, bf16[256,2176]{1,0:T(8,128)(2,1)S(1)}, u32[]{:S(2)}, u32[]{:S(2)}) collective-permute-start(bf16[256,2176]{1,0:T(8,128)(2,1)S(1)} %get-tuple-element.323), channel_id=1, source_target_pairs={{0,2},{2,4},{4,6},{6,7},{7,5},{5,3},{3,1},{1,0},{8,10},{10,12},{12... | collective-permute-start | bytes 3342344 | tf_op jit(solution)/shard_map/ring_ffn_grad/ppermute | solution.py:404
  519.0 45.4 %collective-permute-start.35 = (bf16[256,2176]{1,0:T(8,128)(2,1)S(1)}, bf16[256,2176]{1,0:T(8,128)(2,1)S(1)}, u32[]{:S(2)}, u32[]{:S(2)}) collective-permute-start(bf16[256,2176]{1,0:T(8,128)(2,1)S(1)} %get-tuple-element.324), channel_id=1, source_target_pairs={{0,1},{2,0},{4,2},{6,4},{7,6},{5,7},{3,5},{1,3},{8,9},{10,8},{12,1... | collective-permute-start | bytes 3342344 | tf_op jit(solution)/shard_map/ring_ffn_grad/ppermute | solution.py:404
  549.8 58.8 %collective-permute-start.38 = (bf16[256,2048]{1,0:T(8,128)(2,1)}, bf16[256,2048]{1,0:T(8,128)(2,1)}, u32[]{:S(2)}, u32[]{:S(2)}) collective-permute-start(bf16[256,2048]{1,0:T(8,128)(2,1)} %get-tuple-element.206), channel_id=1, source_target_pairs={{0,2},{2,4},{4,6},{6,7},{7,5},{5,3},{3,1},{1,0},{8,10},{10,12},{12... | collective-permute-start | bytes 3145736 | tf_op jit(solution)/shard_map/ring_mixture/ppermute | solution.py:404
  550.0 58.6 %collective-permute-start.39 = (bf16[256,2048]{1,0:T(8,128)(2,1)}, bf16[256,2048]{1,0:T(8,128)(2,1)}, u32[]{:S(2)}, u32[]{:S(2)}) collective-permute-start(bf16[256,2048]{1,0:T(8,128)(2,1)} %get-tuple-element.207), channel_id=1, source_target_pairs={{0,1},{2,0},{4,2},{6,4},{7,6},{5,7},{3,5},{1,3},{8,9},{10,8},{12,1... | collective-permute-start | bytes 3145736 | tf_op jit(solution)/shard_map/ring_mixture/ppermute | solution.py:404
  565.0 39.6 %collective-permute-start.36 = (bf16[256,2176]{1,0:T(8,128)(2,1)S(1)}, bf16[256,2176]{1,0:T(8,128)(2,1)S(1)}, u32[]{:S(2)}, u32[]{:S(2)}) collective-permute-start(bf16[256,2176]{1,0:T(8,128)(2,1)S(1)} %get-tuple-element.321), channel_id=1, source_target_pairs={{0,2},{2,4},{4,6},{6,7},{7,5},{5,3},{3,1},{1,0},{8,10},{10,12},{12... | collective-permute-start | bytes 3342344 | tf_op jit(solution)/shard_map/ring_ffn_grad/ppermute | solution.py:404
  565.4 40.4 %collective-permute-start.37 = (bf16[256,2176]{1,0:T(8,128)(2,1)S(1)}, bf16[256,2176]{1,0:T(8,128)(2,1)S(1)}, u32[]{:S(2)}, u32[]{:S(2)}) collective-permute-start(bf16[256,2176]{1,0:T(8,128)(2,1)S(1)} %get-tuple-element.322), channel_id=1, source_target_pairs={{0,1},{2,0},{4,2},{6,4},{7,6},{5,7},{3,5},{1,3},{8,9},{10,8},{12,1... | collective-permute-start | bytes 3342344 | tf_op jit(solution)/shard_map/ring_ffn_grad/ppermute | solution.py:404
  630.4 260.0 %reduce-scatter.4.cloned.1.call-start = ((), (), s32[]{:S(2)}) async-start(), calls=%async_computation.10 | async-start | bytes 3932160 | tf_op jit(solution)/shard_map/reduce_scatter | solution.py:888
  718.0 88.0 %collective-permute-start.60 = (bf16[512,2048]{1,0:T(8,128)(2,1)}, bf16[512,2048]{1,0:T(8,128)(2,1)}, u32[]{:S(2)}, u32[]{:S(2)}) collective-permute-start(bf16[512,2048]{1,0:T(8,128)(2,1)} %get-tuple-element.209), channel_id=1, source_target_pairs={{0,16},{8,24},{16,0},{24,8},{1,17},{9,25},{17,1},{25,9},{2,18},{10... | collective-permute-start | bytes 6291464 | tf_op jit(solution)/shard_map/weights_out_groups/ppermute | solution.py:599
  722.0 47.5 %collective-permute-start.46 = (bf16[128,2048]{1,0:T(8,128)(2,1)}, bf16[128,2048]{1,0:T(8,128)(2,1)}, u32[]{:S(2)}, u32[]{:S(2)}) collective-permute-start(bf16[128,2048]{1,0:T(8,128)(2,1)} %get-tuple-element.312), channel_id=1, source_target_pairs={{0,1},{2,0},{4,2},{6,4},{7,6},{5,7},{3,5},{1,3},{8,9},{10,8},{12,1... | collective-permute-start | bytes 1572872 | tf_op jit(solution)/shard_map/ring_normed_grad/ppermute | solution.py:404
  723.5 46.1 %collective-permute-start.45 = (bf16[128,2048]{1,0:T(8,128)(2,1)}, bf16[128,2048]{1,0:T(8,128)(2,1)}, u32[]{:S(2)}, u32[]{:S(2)}) collective-permute-start(bf16[128,2048]{1,0:T(8,128)(2,1)} %get-tuple-element.314), channel_id=1, source_target_pairs={{0,2},{2,4},{4,6},{6,7},{7,5},{5,3},{3,1},{1,0},{8,10},{10,12},{12... | collective-permute-start | bytes 1572872 | tf_op jit(solution)/shard_map/ring_normed_grad/ppermute | solution.py:404
  754.2 177.6 %reduce-scatter.8.cloned.1.call-start = ((), (), s32[]{:S(2)}) async-start(), calls=%async_computation.12 | async-start | bytes 2359296 | tf_op jit(solution)/shard_map/reduce_scatter | solution.py:890
  769.4 65.0 %collective-permute-start.44 = (bf16[1024,2048]{1,0:T(8,128)(2,1)}, bf16[1024,2048]{1,0:T(8,128)(2,1)}, u32[]{:S(2)}, u32[]{:S(2)}) collective-permute-start(bf16[1024,2048]{1,0:T(8,128)(2,1)} %weights_up.2), channel_id=1, source_target_pairs={{0,8},{8,0},{16,24},{24,16},{1,9},{9,1},{17,25},{25,17},{2,10},{10... | collective-permute-start | bytes 12582920 | tf_op jit(solution)/shard_map/weights_up_cores/ppermute | solution.py:581
  804.6 47.3 %collective-permute-start.58 = (bf16[512,2048]{1,0:T(8,128)(2,1)}, bf16[512,2048]{1,0:T(8,128)(2,1)S(1)}, u32[]{:S(2)}, u32[]{:S(2)}) collective-permute-start(bf16[512,2048]{1,0:T(8,128)(2,1)} %get-tuple-element.217), channel_id=1, source_target_pairs={{0,16},{8,24},{16,0},{24,8},{1,17},{9,25},{17,1},{25,9},{2,18},{10... | collective-permute-start | bytes 6291464 | tf_op jit(solution)/shard_map/weights_gate_groups/ppermute | solution.py:599
  850.7 49.2 %collective-permute-start.59 = (bf16[512,2048]{1,0:T(8,128)(2,1)}, bf16[512,2048]{1,0:T(8,128)(2,1)}, u32[]{:S(2)}, u32[]{:S(2)}) collective-permute-start(bf16[512,2048]{1,0:T(8,128)(2,1)} %get-tuple-element.221), channel_id=1, source_target_pairs={{0,16},{8,24},{16,0},{24,8},{1,17},{9,25},{17,1},{25,9},{2,18},{10... | collective-permute-start | bytes 6291464 | tf_op jit(solution)/shard_map/weights_up_groups/ppermute | solution.py:599
  (109 other events, 1739.1 us)
Sparse Core Ops, SparseCore 0:
  74.5 27.5 all-gather.3
  131.2 50.0 all-gather.5
  182.9 56.7 all-gather.7
  618.6 72.4 reduce-scatter.5
  754.3 37.1 reduce-scatter.3
  855.0 76.1 reduce-scatter.7

commit v4 on v3

--- a/solution.py
+++ b/solution.py
@@ -799,7 +799,7 @@
             ffn_sum = Scatter(grads, order, "ring_ffn_grad")
         elif i > 0:
             ffn_sum.step(grads[tok_rows:], grads[:tok_rows])
-        if 1 < i < half:
+        if 2 < i < half:
             mix_sum.step(mix_blocks[i], mix_blocks[-i], grads)
         ready = (*mix_sum.sent, *ffn_sum.sent)
     out_all, gate_grad_all, up_grad_all = held
@@ -808,11 +808,11 @@
         GroupSum(x_all, gate_grad_all, 1, "weights_gate"),
         GroupSum(x_all, up_grad_all, 1, "weights_up"),
     ]
-    sums[0].first()
+    mix_sum.step(mix_blocks[2], mix_blocks[-2], grads)
+    sums[0].first(*mix_sum.sent)
     ffn_grad = ffn_sum.finish(after(grads, sums[0].far))
     gate_grads = ffn_grad[:, width : width + experts_all] * chosen
     ffn_grad = ffn_grad[:, :width]
-    mix_sum.step(mix_blocks[1], mix_blocks[-1], ffn_grad)
     picked_grad = (
         live
         * chosen
@@ -845,13 +845,15 @@
     sums[0].second(branch_grad)
     attended_grad = after(attended_grad, sums[0].near, output_terms)
 
-    block_rows = residual + mix_sum.finish(mix_blocks[0])
-    attended_grad = after(attended_grad, block_rows)
+    mix_sum.step(mix_blocks[1], mix_blocks[-1], attended_grad)
+    attended_grad = after(attended_grad, *mix_sum.sent)
     proj_grad, gain_parts = attend_back(
         owners, project, attended_grad, cosine, sine, key_live, head_gains
     )
     proj_grad = proj_grad.reshape(all_rows, 3 * cols)
     normed_terms = dot_nt(proj_grad, w_qkv).astype(bf16)
+    block_rows = residual + mix_sum.finish(mix_blocks[0])
+    normed_terms = after(normed_terms, block_rows)
     normed_parts = {
         r: normed_terms[i * tok_rows : (i + 1) * tok_rows] for i, r in enumerate(offsets)
     }
@@ -912,8 +914,6 @@
     grad_qkv = grad_qkv.transpose(1, 3, 0, 2, 4).reshape(row_count, 3, width).astype(f32)
 
     small.step(normed_grad)
-    for _ in range(n_expert.bit_length() - 2):
-        small.step()
     small.step(grad_qkv)
     small = small.finish()
     places, pieces = 0, []

time: 951 us -> 944 us (level)
  other arithmetic: 84.2 us -> 95.3 us
  waiting for transfers between devices: 229 us -> 219 us
    ppermute x3, waiting for transfers between devices: 0.01 us -> 17.3 us  [second(): self.back = lax.ppermute(self.near, 'dp', [(i, i ^ 2) for i in range(4)])]
    ppermute x48, waiting for transfers between devices: 177 us -> 165 us  [ring_shift(): return lax.ppermute(rows, 'expert', pairs)]
    unnamed x162 -> x158, local copies, waits for them, and re-layouts: 29.8 us -> 29.1 us
  transfers between devices with their start and end apart: 70 -> 70, of which waited for: 33 -> 30; matrix products, arithmetic and copies ran while one was open for 20% -> 21% of each run, Pallas kernels for 38% -> 38%
where the time goes in v4:
time: 944 us; the launch traced here: 934 us
  Pallas kernels  357 us (38%)
  waiting for transfers between devices  219 us (23%)
  other arithmetic  95.3 us (10%)
  starting transfers between devices  84.4 us (9%)
  local copies, waits for them, and re-layouts  80.9 us (9%)
  matrix products  54.6 us (6%)
  blocking collectives  24 us (3%)
  between operations  18.6 us (2%)
    ppermute x48, waiting for transfers between devices, ring_shift(): return lax.ppermute(rows, 'expert', pairs)  165 us
    pallas_call x5, Pallas kernels, experts_forward(): pl.pallas_call(functools.partial(experts_kernel, len(xs), len(held), tile...  107 us
    pallas_call x5, Pallas kernels, experts_backward(): pl.pallas_call(functools.partial(experts_back_kernel, len(outs), len(held...  106 us
    pallas_call x6, Pallas kernels, weight_part(): pl.pallas_call(functools.partial(weight_kernel, parts, adds, outs), grid_...  94.3 us
    ppermute x48, starting transfers between devices, ring_shift(): return lax.ppermute(rows, 'expert', pairs)  57.9 us
    pallas_call x1, Pallas kernels, attend_back(): pl.pallas_call(attend_back_kernel, grid_spec=pltpu.PrefetchScalarGridSpec...  31.6 us
    unnamed x158, local copies, waits for them, and re-layouts  29.1 us
    all_to_all x1, blocking collectives, body(): lax.all_to_all(after(w_cols.reshape(n_expert, row_count, 3 * cols), norme...  24 us
  transfers between devices with their start and end apart: 70, of which 30 were waited for; matrix products, arithmetic and copies ran while one was open for 21% of the time, Pallas kernels for 38%

profile of v4, /device:TPU:0, one launch (start us, length us, event | category | flops | bytes accessed | tf_op | source)
XLA Modules:
  0.0 934.3 jit_solution(16948090915065839024)
XLA Ops:
  29.4 19.7 %collective-permute-done.1 = bf16[256,2176]{1,0:T(8,128)(2,1)} collective-permute-done((bf16[256,2176]{1,0:T(8,128)(2,1)}, bf16[256,2176]{1,0:T(8,128)(2,1)}, u32[]{:S(2)}, u32[]{:S(2)}) %collective-permute-start.1) | collective-permute-done | bytes 1114144 | tf_op jit(solution)/shard_map/ring_normed/ppermute | solution.py:404
  50.5 24.0 %all_to_all.20 = bf16[8,64,768]{2,1,0:T(8,128)(2,1)} all-to-all(bf16[8,64,768]{2,1,0:T(8,128)(2,1)} %reshape.295), channel_id=1, replica_groups=mesh['dp'=4,'expert'=8] {'expert'}, dimensions={0} | all-to-all | bytes 1572864 | tf_op jit(solution)/shard_map/all_to_all | solution.py:684
  85.4 16.9 %collective-permute-done.3 = bf16[256,2176]{1,0:T(8,128)(2,1)S(1)} collective-permute-done((bf16[256,2176]{1,0:T(8,128)(2,1)}, bf16[256,2176]{1,0:T(8,128)(2,1)S(1)}, u32[]{:S(2)}, u32[]{:S(2)}) %collective-permute-start.3) | collective-permute-done | bytes 1114144 | tf_op jit(solution)/shard_map/ring_normed/ppermute | solution.py:404
  108.8 17.6 %collective-permute-done.5 = bf16[256,2176]{1,0:T(8,128)(2,1)S(1)} collective-permute-done((bf16[256,2176]{1,0:T(8,128)(2,1)S(1)}, bf16[256,2176]{1,0:T(8,128)(2,1)S(1)}, u32[]{:S(2)}, u32[]{:S(2)}) %collective-permute-start.5) | collective-permute-done | bytes 1114144 | tf_op jit(solution)/shard_map/ring_normed/ppermute | solution.py:404
  146.1 11.7 %fusion.36 = f32[2048,768]{1,0:T(8,128)} fusion(bf16[2048,2048]{1,0:T(8,128)(2,1)} %slice_dynamic-update-slice_fusion, bf16[2048,768]{1,0:T(8,128)(2,1)} %all-gather.4.cloned.1.call-done), kind=kOutput, calls=%fused_computation.180 | convolution fusion | flops 6442450944 | bytes 17825792 | tf_op jit(solution)/shard_map/dot_general | solution.py:39
  157.8 18.5 %attend.1 = bf16[8,2,128,256]{3,2,1,0:T(8,128)(2,1)} custom-call(s32[8]{0:T(128)} %dynamic-slice_bitcast_fusion.owner_ref, f32[8,2,128,768]{3,2,1,0:T(8,128)} %bitcast.153, f32[1024,128]{1,0:T(8,128)} %get-tuple-element.381.cos_ref, f32[1024,128]{1,0:T(8,128)} %get-tuple-element.382.sin_ref, f32[2,1,1024]{2,1,0:T(1,128)} %compare_convert_fusion.live_ref, ...), custom_call_target="tpu_custom_call" | custom-call | flops 2147483648 | bytes 7864320 | tf_op jit(solution)/shard_map/attend/pallas_call | solution.py:105
  196.5 10.4 %collective-permute-done.8.refs_1_ = bf16[256,2048]{1,0:T(8,128)(2,1)} collective-permute-done((bf16[256,2048]{1,0:T(8,128)(2,1)S(1)}, bf16[256,2048]{1,0:T(8,128)(2,1)}, u32[]{:S(2)}, u32[]{:S(2)}) %collective-permute-start.8) | collective-permute-done | bytes 1048608 | tf_op jit(solution)/shard_map/ring_cotangent/ppermute | solution.py:404
  229.6 12.1 %all-to-all-done.1 = bf16[8,256,256]{1,2,0:T(8,128)(2,1)S(1)} async-done(((bf16[8,256,256]{1,2,0:T(8,128)(2,1)}), bf16[8,256,256]{1,2,0:T(8,128)(2,1)S(1)}, u32[]{:S(2)}, u32[]{:S(2)}) %all-to-all-start.1) | async-done | bytes 1048608 | tf_op jit(solution)/shard_map/all_to_all | solution.py:726
  267.1 17.7 %experts_forward.5 = (bf16[2048,2048]{1,0:T(8,128)(2,1)}, bf16[2048,2048]{1,0:T(8,128)(2,1)}, bf16[2048,2048]{1,0:T(8,128)(2,1)}, bf16[2048,2048]{1,0:T(8,128)(2...) custom-call(bf16[256,2048]{1,0:T(8,128)(2,1)} %copy-done.5, bf16[256,128]{1,0:T(8,128)(2,1)} %copy-done.40, ...), custom_call_target="tpu_custom_call" | custom-call | flops 6442450944 | bytes 30408704 | tf_op jit(solution)/shard_map/experts_forward/pallas_call | solution.py:272
  287.3 17.4 %collective-permute-done.15.refs_1_ = bf16[256,2048]{1,0:T(8,128)(2,1)S(1)} collective-permute-done((bf16[256,2048]{1,0:T(8,128)(2,1)}, bf16[256,2048]{1,0:T(8,128)(2,1)S(1)}, u32[]{:S(2)}, u32[]{:S(2)}) %collective-permute-start.15) | collective-permute-done | bytes 1048608 | tf_op jit(solution)/shard_map/ring_cotangent/ppermute | solution.py:404
  304.8 24.2 %experts_forward.6 = (bf16[2048,2048]{1,0:T(8,128)(2,1)}, bf16[2048,2048]{1,0:T(8,128)(2,1)}, bf16[2048,2048]{1,0:T(8,128)(2,1)}, bf16[2048,2048]{1,0:T(8,128)(2...) custom-call(bf16[256,2048]{1,0:T(8,128)(2,1)} %collective-permute-do, ...), custom_call_target="tpu_custom_call", output_to_operand_aliasing={{0}: (8, {}), {1}: (9, {}), {2}: (10, {}), {3}: (11, {})} | custom-call | flops 12884901888 | bytes 35651584 | tf_op jit(solution)/shard_map/experts_forward/pallas_call | solution.py:272
  336.2 23.6 %experts_forward.7 = (bf16[2048,2048]{1,0:T(8,128)(2,1)}, bf16[2048,2048]{1,0:T(8,128)(2,1)}, bf16[2048,2048]{1,0:T(8,128)(2,1)}, bf16[2048,2048]{1,0:T(8,128)(2...) custom-call(bf16[256,2048]{1,0:T(8,128)(2,1)} %copy-done.36, ...), custom_call_target="tpu_custom_call", output_to_operand_aliasing={{0}: (8, {}), {1}: (9, {}), {2}: (10, {}), {3}: (11, {})} | custom-call | flops 12884901888 | bytes 35651584 | tf_op jit(solution)/shard_map/experts_forward/pallas_call | solution.py:272
  369.4 23.7 %experts_forward.8 = (bf16[2048,2048]{1,0:T(8,128)(2,1)}, bf16[2048,2048]{1,0:T(8,128)(2,1)}, bf16[2048,2048]{1,0:T(8,128)(2,1)}, bf16[2048,2048]{1,0:T(8,128)(2...) custom-call(bf16[256,2048]{1,0:T(8,128)(2,1)} %copy-done.25, ...), custom_call_target="tpu_custom_call", output_to_operand_aliasing={{0}: (8, {}), {1}: (9, {}), {2}: (10, {}), {3}: (11, {})} | custom-call | flops 12884901888 | bytes 35651584 | tf_op jit(solution)/shard_map/experts_forward/pallas_call | solution.py:272
  395.5 17.8 %experts_forward.9 = (bf16[2048,2048]{1,0:T(8,128)(2,1)}, bf16[2048,2048]{1,0:T(8,128)(2,1)}, bf16[2048,2048]{1,0:T(8,128)(2,1)}, bf16[2048,2048]{1,0:T(8,128)(2...) custom-call(bf16[256,2048]{1,0:T(8,128)(2,1)} %pad_maximum_fusion.8., ...), custom_call_target="tpu_custom_call", output_to_operand_aliasing={{0}: (7, {}), {1}: (8, {}), {2}: (9, {}), {3}: (10, {})} | custom-call | flops 6442450944 | bytes 30408704 | tf_op jit(solution)/shard_map/experts_forward/pallas_call | solution.py:272
  417.7 17.2 %experts_backward.5 = (bf16[2048,2048]{1,0:T(8,128)(2,1)}, bf16[2048,2048]{1,0:T(8,128)(2,1)}, bf16[2048,2048]{1,0:T(8,128)(2,1)}, f32[256,128]{1,0:T(8,128)}, bf16[256,2048]{1,0:T(8,128)(2,1)}) custom-call(bf16[256,2048]{1,0:T(8,128)(2,1)} %pad_maximum_fusion.11.refs_0_, f32[256,2]{1,0:T(8,128)} %get-tuple-element.167.refs_1_, ...), custom_call_target="tpu_custom_call" | custom-call | flops 6442450944 | bytes 31457280 | tf_op jit(solution)/shard_map/experts_backward/pallas_call | solution.py:359
  439.4 23.9 %experts_backward.6 = (bf16[2048,2048]{1,0:T(8,128)(2,1)}, bf16[2048,2048]{1,0:T(8,128)(2,1)}, bf16[2048,2048]{1,0:T(8,128)(2,1)}, f32[512,128]{1,0:T(8,128)}, bf16[512,2048]{1,0:T(8,128)(2,1)}) custom-call(bf16[256,2048]{1,0:T(8,128)(2,1)} %copy-done.24, bf16[256,2048]{1,0:T(8,128)(2,1)} %copy-done.23, ...), custom_call_target="tpu_custom_call", output_to_operand_aliasing={{0}: (8, {}), {1}: (9, {}), {2}: (10, {})} | custom-call | flops 12884901888 | bytes 37748736 | tf_op jit(solution)/shard_map/experts_backward/pallas_call | solution.py:359
  472.0 24.0 %experts_backward.7 = (bf16[2048,2048]{1,0:T(8,128)(2,1)}, bf16[2048,2048]{1,0:T(8,128)(2,1)}, bf16[2048,2048]{1,0:T(8,128)(2,1)}, f32[512,128]{1,0:T(8,128)}, bf16[512,2048]{1,0:T(8,128)(2,1)}) custom-call(bf16[256,2048]{1,0:T(8,128)(2,1)} %collective-permute-done.13.refs_0_, ...), custom_call_target="tpu_custom_call", output_to_operand_aliasing={{0}: (8, {}), {1}: (9, {}), {2}: (10, {})} | custom-call | flops 12884901888 | bytes 37748736 | tf_op jit(solution)/shard_map/experts_backward/pallas_call | solution.py:359
  501.0 10.6 %collective-permute-done.30 = bf16[256,2176]{1,0:T(8,128)(2,1)S(1)} collective-permute-done((bf16[256,2176]{1,0:T(8,128)(2,1)S(1)}, bf16[256,2176]{1,0:T(8,128)(2,1)S(1)}, u32[]{:S(2)}, u32[]{:S(2)}) %collective-permute-start.30) | collective-permute-done | bytes 1114144 | tf_op jit(solution)/shard_map/ring_ffn_grad/ppermute | solution.py:404
  516.2 23.8 %experts_backward.8 = (bf16[2048,2048]{1,0:T(8,128)(2,1)}, bf16[2048,2048]{1,0:T(8,128)(2,1)}, bf16[2048,2048]{1,0:T(8,128)(2,1)}, f32[512,128]{1,0:T(8,128)}, bf16[512,2048]{1,0:T(8,128)(2,1)}) custom-call(bf16[256,2048]{1,0:T(8,128)(2,1)} %collective-permute-done.9.refs_0_, ...), custom_call_target="tpu_custom_call", output_to_operand_aliasing={{0}: (8, {}), {1}: (9, {}), {2}: (10, {})} | custom-call | flops 12884901888 | bytes 37748736 | tf_op jit(solution)/shard_map/experts_backward/pallas_call | solution.py:359
  545.1 17.2 %experts_backward.9 = (bf16[2048,2048]{1,0:T(8,128)(2,1)}, bf16[2048,2048]{1,0:T(8,128)(2,1)}, bf16[2048,2048]{1,0:T(8,128)(2,1)}, f32[256,128]{1,0:T(8,128)}, bf16[256,2048]{1,0:T(8,128)(2,1)}) custom-call(bf16[256,2048]{1,0:T(8,128)(2,1)} %bitcast.149, ...), custom_call_target="tpu_custom_call", output_to_operand_aliasing={{0}: (7, {}), {1}: (8, {}), {2}: (9, {})} | custom-call | flops 6442450944 | bytes 31457280 | tf_op jit(solution)/shard_map/experts_backward/pallas_call | solution.py:359
  564.5 15.2 %weights_out.2 = bf16[1024,2048]{1,0:T(8,128)(2,1)} custom-call(s32[4]{0:T(128)} %pad_add_fusion.index_ref, bf16[2048,2048]{1,0:T(8,128)(2,1)} %get-tuple-element.209.refs_0_.refs_1_.refs_2_.refs_3_, bf16[2048,2048]{1,0:T(8,128)(2,1)} %get-tuple-element.209.refs_0_.refs_1_.refs_2_.refs_3_, ...), custom_call_target="tpu_custom_call" | custom-call | flops 8589934592 | bytes 20971520 | tf_op jit(solution)/shard_map/weights_out/pallas_call | solution.py:538
  606.8 10.7 %collective-permute-done.34 = bf16[256,2048]{1,0:T(8,128)(2,1)} collective-permute-done((bf16[256,2048]{1,0:T(8,128)(2,1)}, bf16[256,2048]{1,0:T(8,128)(2,1)}, u32[]{:S(2)}, u32[]{:S(2)}) %collective-permute-start.34) | collective-permute-done | bytes 1048608 | tf_op jit(solution)/shard_map/ring_mixture/ppermute | solution.py:404
  623.6 16.1 %weights_out.3 = (bf16[512,2048]{1,0:T(8,128)(2,1)}, f32[512,2048]{1,0:T(8,128)}) custom-call(s32[8]{0:T(128)} %stack.100.index_ref, bf16[2048,2048]{1,0:T(8,128)(2,1)} %get-tuple-element.209.refs_0_.refs_1_.refs_2_.refs_3_, bf16[2048,2048]{1,0:T(8,128)(2,1)} %get-tuple-element.209.refs_0_.refs_1_.refs_2_.refs_3_, ...), custom_call_target="tpu_custom_call" | custom-call | flops 8589934592 | bytes 20971520 | tf_op jit(solution)/shard_map/weights_out/pallas_call | solution.py:538
  644.3 31.6 %attend_back.1 = (bf16[8,2,128,768]{3,2,1,0:T(8,128)(2,1)}, f32[2,2,2,128]{3,2,1,0:T(2,128)}) custom-call(s32[8]{0:T(128)} %dynamic-slice_bitcast_fusion.owner_ref, f32[8,2,128,768]{3,2,1,0:T(8,128)} %bitcast.154, bf16[8,2,128,256]{3,2,1,0:T(8,128)(2,1)} %bitcast.162, f32[1024,128]{1,0:T(8,128)} %get-tuple-element.381.cos_ref, ...), custom_call_target="tpu_custom_call" | custom-call | flops 5368709120 | bytes 11010048 | tf_op jit(solution)/shard_map/attend_back/pallas_call | solution.py:176
  675.9 11.4 %convolution_convert_fusion = bf16[2048,2048]{1,0:T(8,128)(2,1)} fusion(bf16[2048,768]{1,0:T(8,128)(2,1)} %bitcast.170, bf16[2048,768]{1,0:T(8,128)(2,1)} %all-gather.4.cloned.1.call-done), kind=kOutput, calls=%fused_computation.2 | convolution fusion | flops 6446645248 | bytes 14680064 | tf_op jit(solution)/shard_map/dot_general | solution.py:43
  689.3 15.5 %weights_gate.2 = bf16[1024,2048]{1,0:T(8,128)(2,1)} custom-call(s32[2]{0:T(128)} %pad_add_fusion.2.index_ref, bf16[2048,2048]{1,0:T(8,128)(2,1)} %get-tuple-element.223.refs_0_.refs_1_, bf16[2048,2048]{1,0:T(8,128)(2,1)} %get-tuple-element.223.refs_0_.refs_1_, bf16[2048,2048]{1,0:T(8,128)(2,1)} %get-tuple-element.220.refs_2_), custom_call_target="tpu_custom_call" | custom-call | flops 8589934592 | bytes 20971520 | tf_op jit(solution)/shard_map/weights_gate/pallas_call | solution.py:538
  716.4 15.8 %weights_gate.3 = (bf16[512,2048]{1,0:T(8,128)(2,1)}, f32[512,2048]{1,0:T(8,128)}) custom-call(s32[4]{0:T(128)} %pad_add_fusion.1.index_ref, bf16[2048,2048]{1,0:T(8,128)(2,1)} %get-tuple-element.223.refs_0_.refs_1_, bf16[2048,2048]{1,0:T(8,128)(2,1)} %get-tuple-element.223.refs_0_.refs_1_, bf16[2048,2048]{1,0:T(8,128)(2,1)} %get-tuple-element.220.refs_2_, ...), custom_call_target="tpu_custom_call" | custom-call | flops 8589934592 | bytes 20971520 | tf_op jit(solution)/shard_map/weights_gate/pallas_call | solution.py:538
  742.7 15.7 %weights_up.2 = bf16[1024,2048]{1,0:T(8,128)(2,1)} custom-call(s32[2]{0:T(128)} %pad_add_fusion.2.index_ref, bf16[2048,2048]{1,0:T(8,128)(2,1)} %get-tuple-element.223.refs_0_.refs_1_, bf16[2048,2048]{1,0:T(8,128)(2,1)} %get-tuple-element.223.refs_0_.refs_1_, bf16[2048,2048]{1,0:T(8,128)(2,1)} %get-tuple-element.224.refs_2_), custom_call_target="tpu_custom_call" | custom-call | flops 8589934592 | bytes 20971520 | tf_op jit(solution)/shard_map/weights_up/pallas_call | solution.py:538
  772.4 14.8 %collective-permute-done.47 = bf16[256,2048]{1,0:T(8,128)(2,1)S(1)} collective-permute-done((bf16[256,2048]{1,0:T(8,128)(2,1)}, bf16[256,2048]{1,0:T(8,128)(2,1)S(1)}, u32[]{:S(2)}, u32[]{:S(2)}) %collective-permute-start.47) | collective-permute-done | bytes 1048608 | tf_op jit(solution)/shard_map/ring_normed_grad/ppermute | solution.py:404
  797.7 17.4 %collective-permute-done.49 = bf16[256,2048]{1,0:T(8,128)(2,1)S(1)} collective-permute-done((bf16[256,2048]{1,0:T(8,128)(2,1)S(1)}, bf16[256,2048]{1,0:T(8,128)(2,1)S(1)}, u32[]{:S(2)}, u32[]{:S(2)}) %collective-permute-start.49) | collective-permute-done | bytes 1048608 | tf_op jit(solution)/shard_map/ring_normed_grad/ppermute | solution.py:404
  822.4 16.0 %weights_up.3 = (bf16[512,2048]{1,0:T(8,128)(2,1)}, f32[512,2048]{1,0:T(8,128)}) custom-call(s32[4]{0:T(128)} %pad_add_fusion.1.index_ref, bf16[2048,2048]{1,0:T(8,128)(2,1)} %get-tuple-element.223.refs_0_.refs_1_, bf16[2048,2048]{1,0:T(8,128)(2,1)} %get-tuple-element.223.refs_0_.refs_1_, bf16[2048,2048]{1,0:T(8,128)(2,1)} %get-tuple-element.224.refs_2_, ...), custom_call_target="tpu_custom_call" | custom-call | flops 8589934592 | bytes 20971520 | tf_op jit(solution)/shard_map/weights_up/pallas_call | solution.py:538
  867.3 17.3 %collective-permute-done.59 = bf16[512,2048]{1,0:T(8,128)(2,1)} collective-permute-done((bf16[512,2048]{1,0:T(8,128)(2,1)}, bf16[512,2048]{1,0:T(8,128)(2,1)}, u32[]{:S(2)}, u32[]{:S(2)}) %collective-permute-start.59) | collective-permute-done | bytes 2097184 | tf_op jit(solution)/shard_map/weights_up_groups/ppermute | solution.py:599
  (430 shorter events, 346.1 us)
Async XLA Ops:
  7.2 139.0 %all-gather.4.cloned.1.call-start = ((), (), s32[]{:S(2)}) async-start(), calls=%async_computation.7 | async-start | bytes 3932160 | tf_op jit(solution)/shard_map/all_gather | solution.py:695
  74.5 106.9 %all-gather.6.cloned.1.call-start = ((), (), s32[]{:S(2)}) async-start(), calls=%async_computation.8 | async-start | bytes 2359296 | tf_op jit(solution)/shard_map/all_gather | solution.py:702
  131.2 110.5 %all-gather.8.cloned.1.call-start = ((), (), s32[]{:S(2)}) async-start(), calls=%async_computation.9 | async-start | bytes 10485760 | tf_op jit(solution)/shard_map/all_gather | solution.py:723
  214.6 629.9 %reduce-scatter.6.cloned.1.call-start = ((), (), s32[]{:S(2)}) async-start(), calls=%async_computation.11 | async-start | bytes 10485760 | tf_op jit(solution)/shard_map/reduce_scatter | solution.py:844
  226.1 39.2 %collective-permute-start.39 = (f32[16]{0:T(128)S(1)}, f32[16]{0:T(128)S(1)}, u32[]{:S(2)}, u32[]{:S(2)}) collective-permute-start(f32[16]{0:T(128)S(1)} %slice_add_fusion.1), channel_id=1, source_target_pairs={{0,16},{8,24},{16,0},{24,8},{1,17},{9,25},{17,1},{25,9},{2,18},{10... | collective-permute-start | bytes 200 | tf_op jit(solution)/shard_map/ppermute | solution.py:472
  248.2 36.6 %collective-permute-start.11 = (bf16[256,2048]{1,0:T(8,128)(2,1)S(1)}, bf16[256,2048]{1,0:T(8,128)(2,1)}, u32[]{:S(2)}, u32[]{:S(2)}) collective-permute-start(bf16[256,2048]{1,0:T(8,128)(2,1)S(1)} %multiply_convert_fusion.refs_0_), channel_id=1, source_target_pairs={{0,1},{2,0},{4,2},{6,4},{7,6},{5,7},{3,5},{1,3},{8,9},{10,8},{12,1... | collective-permute-start | bytes 3145736 | tf_op jit(solution)/shard_map/ring_ffn/ppermute | solution.py:404
  248.4 36.4 %collective-permute-start.10 = (bf16[256,2048]{1,0:T(8,128)(2,1)S(1)}, bf16[256,2048]{1,0:T(8,128)(2,1)}, u32[]{:S(2)}, u32[]{:S(2)}) collective-permute-start(bf16[256,2048]{1,0:T(8,128)(2,1)S(1)} %multiply_convert_fusion.refs_0_), channel_id=1, source_target_pairs={{0,2},{2,4},{4,6},{6,7},{7,5},{5,3},{3,1},{1,0},{8,10},{10,12},{12... | collective-permute-start | bytes 3145736 | tf_op jit(solution)/shard_map/ring_ffn/ppermute | solution.py:404
  259.9 44.8 %collective-permute-start.15 = (bf16[256,2048]{1,0:T(8,128)(2,1)}, bf16[256,2048]{1,0:T(8,128)(2,1)S(1)}, u32[]{:S(2)}, u32[]{:S(2)}) collective-permute-start(bf16[256,2048]{1,0:T(8,128)(2,1)} %collective-permute-done.14.refs_1_), channel_id=1, source_target_pairs={{0,1},{2,0},{4,2},{6,4},{7,6},{5,7},{3,5},{1,3},{8,9},{10,8},{12,1... | collective-permute-start | bytes 3145736 | tf_op jit(solution)/shard_map/ring_cotangent/ppermute | solution.py:404
  260.0 44.7 %collective-permute-start.16 = (bf16[256,2048]{1,0:T(8,128)(2,1)}, bf16[256,2048]{1,0:T(8,128)(2,1)S(1)}, u32[]{:S(2)}, u32[]{:S(2)}) collective-permute-start(bf16[256,2048]{1,0:T(8,128)(2,1)} %collective-permute-done.13.refs_0_), channel_id=1, source_target_pairs={{0,2},{2,4},{4,6},{6,7},{7,5},{5,3},{3,1},{1,0},{8,10},{10,12},{12... | collective-permute-start | bytes 3145736 | tf_op jit(solution)/shard_map/ring_cotangent/ppermute | solution.py:404
  284.9 49.2 %collective-permute-start.12 = (bf16[256,2048]{1,0:T(8,128)(2,1)}, bf16[256,2048]{1,0:T(8,128)(2,1)S(1)}, u32[]{:S(2)}, u32[]{:S(2)}) collective-permute-start(bf16[256,2048]{1,0:T(8,128)(2,1)} %collective-permute-done.10.refs_0_), channel_id=1, source_target_pairs={{0,2},{2,4},{4,6},{6,7},{7,5},{5,3},{3,1},{1,0},{8,10},{10,12},{12... | collective-permute-start | bytes 3145736 | tf_op jit(solution)/shard_map/ring_ffn/ppermute | solution.py:404
  287.3 46.8 %collective-permute-start.17 = (bf16[256,2048]{1,0:T(8,128)(2,1)}, bf16[256,2048]{1,0:T(8,128)(2,1)S(1)}, u32[]{:S(2)}, u32[]{:S(2)}) collective-permute-start(bf16[256,2048]{1,0:T(8,128)(2,1)} %collective-permute-done.11.refs_1_), channel_id=1, source_target_pairs={{0,1},{2,0},{4,2},{6,4},{7,6},{5,7},{3,5},{1,3},{8,9},{10,8},{12,1... | collective-permute-start | bytes 3145736 | tf_op jit(solution)/shard_map/ring_ffn/ppermute | solution.py:404
  329.1 85.5 %collective-permute-start.24 = (bf16[128,2048]{1,0:T(8,128)(2,1)S(1)}, bf16[128,2048]{1,0:T(8,128)(2,1)S(1)}, u32[]{:S(2)}, u32[]{:S(2)}) collective-permute-start(bf16[128,2048]{1,0:T(8,128)(2,1)S(1)} %slice.340), channel_id=1, source_target_pairs={{0,2},{2,4},{4,6},{6,7},{7,5},{5,3},{3,1},{1,0},{8,10},{10,12},{12... | collective-permute-start | bytes 1572872 | tf_op jit(solution)/shard_map/ring_cotangent/ppermute | solution.py:404
  334.0 80.5 %collective-permute-start.25 = (bf16[128,2048]{1,0:T(8,128)(2,1)S(1)}, bf16[128,2048]{1,0:T(8,128)(2,1)S(1)}, u32[]{:S(2)}, u32[]{:S(2)}) collective-permute-start(bf16[128,2048]{1,0:T(8,128)(2,1)S(1)} %slice.341), channel_id=1, source_target_pairs={{0,1},{2,0},{4,2},{6,4},{7,6},{5,7},{3,5},{1,3},{8,9},{10,8},{12,1... | collective-permute-start | bytes 1572872 | tf_op jit(solution)/shard_map/ring_cotangent/ppermute | solution.py:404
  414.6 51.1 %collective-permute-start.23 = (bf16[128,2048]{1,0:T(8,128)(2,1)S(1)}, bf16[128,2048]{1,0:T(8,128)(2,1)S(1)}, u32[]{:S(2)}, u32[]{:S(2)}) collective-permute-start(bf16[128,2048]{1,0:T(8,128)(2,1)S(1)} %get-tuple-element.357), channel_id=1, source_target_pairs={{0,1},{2,0},{4,2},{6,4},{7,6},{5,7},{3,5},{1,3},{8,9},{10,8},{12,1... | collective-permute-start | bytes 1572872 | tf_op jit(solution)/shard_map/ring_mixture/ppermute | solution.py:404
  414.7 51.0 %collective-permute-start.22 = (bf16[128,2048]{1,0:T(8,128)(2,1)S(1)}, bf16[128,2048]{1,0:T(8,128)(2,1)S(1)}, u32[]{:S(2)}, u32[]{:S(2)}) collective-permute-start(bf16[128,2048]{1,0:T(8,128)(2,1)S(1)} %get-tuple-element.358), channel_id=1, source_target_pairs={{0,2},{2,4},{4,6},{6,7},{7,5},{5,3},{3,1},{1,0},{8,10},{10,12},{12... | collective-permute-start | bytes 1572872 | tf_op jit(solution)/shard_map/ring_mixture/ppermute | solution.py:404
  469.8 41.8 %collective-permute-start.30 = (bf16[256,2176]{1,0:T(8,128)(2,1)S(1)}, bf16[256,2176]{1,0:T(8,128)(2,1)S(1)}, u32[]{:S(2)}, u32[]{:S(2)}) collective-permute-start(bf16[256,2176]{1,0:T(8,128)(2,1)S(1)} %pad_maximum_fusion.5), channel_id=1, source_target_pairs={{0,2},{2,4},{4,6},{6,7},{7,5},{5,3},{3,1},{1,0},{8,10},{10,12},{12... | collective-permute-start | bytes 3342344 | tf_op jit(solution)/shard_map/ring_ffn_grad/ppermute | solution.py:404
  470.4 42.6 %collective-permute-start.31 = (bf16[256,2176]{1,0:T(8,128)(2,1)S(1)}, bf16[256,2176]{1,0:T(8,128)(2,1)S(1)}, u32[]{:S(2)}, u32[]{:S(2)}) collective-permute-start(bf16[256,2176]{1,0:T(8,128)(2,1)S(1)} %pad_maximum_fusion.6), channel_id=1, source_target_pairs={{0,1},{2,0},{4,2},{6,4},{7,6},{5,7},{3,5},{1,3},{8,9},{10,8},{12,1... | collective-permute-start | bytes 3342344 | tf_op jit(solution)/shard_map/ring_ffn_grad/ppermute | solution.py:404
  543.0 36.7 %collective-permute-start.37 = (bf16[256,2176]{1,0:T(8,128)(2,1)S(1)}, bf16[256,2176]{1,0:T(8,128)(2,1)S(1)}, u32[]{:S(2)}, u32[]{:S(2)}) collective-permute-start(bf16[256,2176]{1,0:T(8,128)(2,1)S(1)} %get-tuple-element.325), channel_id=1, source_target_pairs={{0,1},{2,0},{4,2},{6,4},{7,6},{5,7},{3,5},{1,3},{8,9},{10,8},{12,1... | collective-permute-start | bytes 3342344 | tf_op jit(solution)/shard_map/ring_ffn_grad/ppermute | solution.py:404
  543.8 35.9 %collective-permute-start.36 = (bf16[256,2176]{1,0:T(8,128)(2,1)S(1)}, bf16[256,2176]{1,0:T(8,128)(2,1)S(1)}, u32[]{:S(2)}, u32[]{:S(2)}) collective-permute-start(bf16[256,2176]{1,0:T(8,128)(2,1)S(1)} %get-tuple-element.326), channel_id=1, source_target_pairs={{0,2},{2,4},{4,6},{6,7},{7,5},{5,3},{3,1},{1,0},{8,10},{10,12},{12... | collective-permute-start | bytes 3342344 | tf_op jit(solution)/shard_map/ring_ffn_grad/ppermute | solution.py:404
  591.0 32.6 %collective-permute-start.40 = (bf16[1024,2048]{1,0:T(8,128)(2,1)}, bf16[1024,2048]{1,0:T(8,128)(2,1)}, u32[]{:S(2)}, u32[]{:S(2)}) collective-permute-start(bf16[1024,2048]{1,0:T(8,128)(2,1)} %weights_out.2), channel_id=1, source_target_pairs={{0,8},{8,0},{16,24},{24,16},{1,9},{9,1},{17,25},{25,17},{2,10},{10... | collective-permute-start | bytes 12582920 | tf_op jit(solution)/shard_map/weights_out_cores/ppermute | solution.py:581
  600.2 42.1 %all-to-all-start.2 = ((bf16[8,256,256]{2,1,0:T(8,128)(2,1)}), bf16[8,256,256]{2,1,0:T(8,128)(2,1)S(1)}, u32[]{:S(2)}, u32[]{:S(2)}) async-start(bf16[8,256,256]{2,1,0:T(8,128)(2,1)} %bitcast.128), calls=%async_computation.2 | async-start | bytes 2097152 | tf_op jit(solution)/shard_map/all_to_all | solution.py:835
  605.4 247.6 %reduce-scatter.4.cloned.1.call-start = ((), (), s32[]{:S(2)}) async-start(), calls=%async_computation.10 | async-start | bytes 3932160 | tf_op jit(solution)/shard_map/reduce_scatter | solution.py:890
  642.3 45.1 %collective-permute-start.41 = (bf16[256,2048]{1,0:T(8,128)(2,1)}, bf16[256,2048]{1,0:T(8,128)(2,1)S(1)}, u32[]{:S(2)}, u32[]{:S(2)}) collective-permute-start(bf16[256,2048]{1,0:T(8,128)(2,1)} %get-tuple-element.212), channel_id=1, source_target_pairs={{0,2},{2,4},{4,6},{6,7},{7,5},{5,3},{3,1},{1,0},{8,10},{10,12},{12... | collective-permute-start | bytes 3145736 | tf_op jit(solution)/shard_map/ring_mixture/ppermute | solution.py:404
  642.3 45.1 %collective-permute-start.42 = (bf16[256,2048]{1,0:T(8,128)(2,1)}, bf16[256,2048]{1,0:T(8,128)(2,1)S(1)}, u32[]{:S(2)}, u32[]{:S(2)}) collective-permute-start(bf16[256,2048]{1,0:T(8,128)(2,1)} %get-tuple-element.213), channel_id=1, source_target_pairs={{0,1},{2,0},{4,2},{6,4},{7,6},{5,7},{3,5},{1,3},{8,9},{10,8},{12,1... | collective-permute-start | bytes 3145736 | tf_op jit(solution)/shard_map/ring_mixture/ppermute | solution.py:404
  707.2 86.0 %collective-permute-start.60 = (bf16[512,2048]{1,0:T(8,128)(2,1)}, bf16[512,2048]{1,0:T(8,128)(2,1)}, u32[]{:S(2)}, u32[]{:S(2)}) collective-permute-start(bf16[512,2048]{1,0:T(8,128)(2,1)} %get-tuple-element.210), channel_id=1, source_target_pairs={{0,16},{8,24},{16,0},{24,8},{1,17},{9,25},{17,1},{25,9},{2,18},{10... | collective-permute-start | bytes 6291464 | tf_op jit(solution)/shard_map/weights_out_groups/ppermute | solution.py:599
  714.4 44.0 %collective-permute-start.46 = (bf16[128,2048]{1,0:T(8,128)(2,1)}, bf16[128,2048]{1,0:T(8,128)(2,1)S(1)}, u32[]{:S(2)}, u32[]{:S(2)}) collective-permute-start(bf16[128,2048]{1,0:T(8,128)(2,1)} %get-tuple-element.316), channel_id=1, source_target_pairs={{0,1},{2,0},{4,2},{6,4},{7,6},{5,7},{3,5},{1,3},{8,9},{10,8},{12,1... | collective-permute-start | bytes 1572872 | tf_op jit(solution)/shard_map/ring_normed_grad/ppermute | solution.py:404
  714.6 43.8 %collective-permute-start.45 = (bf16[128,2048]{1,0:T(8,128)(2,1)}, bf16[128,2048]{1,0:T(8,128)(2,1)S(1)}, u32[]{:S(2)}, u32[]{:S(2)}) collective-permute-start(bf16[128,2048]{1,0:T(8,128)(2,1)} %get-tuple-element.318), channel_id=1, source_target_pairs={{0,2},{2,4},{4,6},{6,7},{7,5},{5,3},{3,1},{1,0},{8,10},{10,12},{12... | collective-permute-start | bytes 1572872 | tf_op jit(solution)/shard_map/ring_normed_grad/ppermute | solution.py:404
  742.7 181.6 %reduce-scatter.8.cloned.1.call-start = ((), (), s32[]{:S(2)}) async-start(), calls=%async_computation.12 | async-start | bytes 2359296 | tf_op jit(solution)/shard_map/reduce_scatter | solution.py:892
  758.4 62.0 %collective-permute-start.44 = (bf16[1024,2048]{1,0:T(8,128)(2,1)}, bf16[1024,2048]{1,0:T(8,128)(2,1)S(1)}, u32[]{:S(2)}, u32[]{:S(2)}) collective-permute-start(bf16[1024,2048]{1,0:T(8,128)(2,1)} %weights_up.2), channel_id=1, source_target_pairs={{0,8},{8,0},{16,24},{24,16},{1,9},{9,1},{17,25},{25,17},{2,10},{10... | collective-permute-start | bytes 12582920 | tf_op jit(solution)/shard_map/weights_up_cores/ppermute | solution.py:581
  792.0 47.3 %collective-permute-start.58 = (bf16[512,2048]{1,0:T(8,128)(2,1)}, bf16[512,2048]{1,0:T(8,128)(2,1)S(1)}, u32[]{:S(2)}, u32[]{:S(2)}) collective-permute-start(bf16[512,2048]{1,0:T(8,128)(2,1)} %get-tuple-element.221), channel_id=1, source_target_pairs={{0,16},{8,24},{16,0},{24,8},{1,17},{9,25},{17,1},{25,9},{2,18},{10... | collective-permute-start | bytes 6291464 | tf_op jit(solution)/shard_map/weights_gate_groups/ppermute | solution.py:599
  838.4 46.2 %collective-permute-start.59 = (bf16[512,2048]{1,0:T(8,128)(2,1)}, bf16[512,2048]{1,0:T(8,128)(2,1)}, u32[]{:S(2)}, u32[]{:S(2)}) collective-permute-start(bf16[512,2048]{1,0:T(8,128)(2,1)} %get-tuple-element.225), channel_id=1, source_target_pairs={{0,16},{8,24},{16,0},{24,8},{1,17},{9,25},{17,1},{25,9},{2,18},{10... | collective-permute-start | bytes 6291464 | tf_op jit(solution)/shard_map/weights_up_groups/ppermute | solution.py:599
  853.0 37.9 %all-to-all-start.3 = ((bf16[8,64,768]{2,1,0:T(8,128)(2,1)}), bf16[8,64,768]{2,1,0:T(8,128)(2,1)S(1)}, u32[]{:S(2)}, u32[]{:S(2)}) async-start(bf16[8,64,768]{2,1,0:T(8,128)(2,1)} %bitcast.164), calls=%async_computation.4 | async-start | bytes 1572864 | tf_op jit(solution)/shard_map/all_to_all | solution.py:907
  (108 other events, 1718.4 us)
Sparse Core Ops, SparseCore 0:
  74.6 27.5 all-gather.3
  131.3 50.0 all-gather.5
  182.9 56.7 all-gather.7
  591.1 72.6 reduce-scatter.5
  742.8 38.8 reduce-scatter.3
  844.6 79.6 reduce-scatter.7

commit v5 on v4

--- a/solution.py
+++ b/solution.py
@@ -83,7 +83,7 @@
     owner_ref, proj_ref, cos_ref, sin_ref, live_ref, gain_ref, out_ref, q_scr, o_scr
 ):
     rows, slots = cos_ref.shape[0], proj_ref.shape[2]
-    step = min(TILE, rows)
+    step = min(WIDE, rows)
     _, _, queries, keys, values = load_heads(proj_ref, cos_ref, sin_ref, gain_ref)
     q_scr[...] = queries
     live = live_ref[0] > 0.0
@@ -132,7 +132,7 @@
     owner_ref, proj_ref, grad_ref, cos_ref, sin_ref, live_ref, gain_ref, out_ref, gain_out, q_scr, dq, dk, dv
 ):
     rows, slots = cos_ref.shape[0], proj_ref.shape[2]
-    step = min(TILE, rows)
+    step = min(WIDE, rows)
     scale = 1.0 / math.sqrt(HD)
     q_proj, k_proj, queries, keys, values = load_heads(proj_ref, cos_ref, sin_ref, gain_ref)
     q_scr[0] = queries

time: 944 us -> 941 us (level)
  no operation moved by 1% of the time
where the time goes in v5:
time: 941 us; the launch traced here: 931 us
  Pallas kernels  356 us (38%)
  waiting for transfers between devices  217 us (23%)
  other arithmetic  95.3 us (10%)
  starting transfers between devices  84.4 us (9%)
  local copies, waits for them, and re-layouts  80.9 us (9%)
  matrix products  54.6 us (6%)
  blocking collectives  24 us (3%)
  between operations  18.6 us (2%)
    ppermute x48, waiting for transfers between devices, ring_shift(): return lax.ppermute(rows, 'expert', pairs)  165 us
    pallas_call x5, Pallas kernels, experts_forward(): pl.pallas_call(functools.partial(experts_kernel, len(xs), len(held), tile...  107 us
    pallas_call x5, Pallas kernels, experts_backward(): pl.pallas_call(functools.partial(experts_back_kernel, len(outs), len(held...  106 us
    pallas_call x6, Pallas kernels, weight_part(): pl.pallas_call(functools.partial(weight_kernel, parts, adds, outs), grid_...  94.2 us
    ppermute x48, starting transfers between devices, ring_shift(): return lax.ppermute(rows, 'expert', pairs)  57.9 us
    unnamed x158, local copies, waits for them, and re-layouts  29.1 us
    pallas_call x1, Pallas kernels, attend_back(): pl.pallas_call(attend_back_kernel, grid_spec=pltpu.PrefetchScalarGridSpec...  28.5 us
    all_to_all x1, blocking collectives, body(): lax.all_to_all(after(w_cols.reshape(n_expert, row_count, 3 * cols), norme...  24 us
  transfers between devices with their start and end apart: 70, of which 30 were waited for; matrix products, arithmetic and copies ran while one was open for 21% of the time, Pallas kernels for 38%

profile of v5, /device:TPU:0, one launch (start us, length us, event | category | flops | bytes accessed | tf_op | source)
XLA Modules:
  0.0 931.1 jit_solution(6025024455291298647)
XLA Ops:
  29.4 19.7 %collective-permute-done.1 = bf16[256,2176]{1,0:T(8,128)(2,1)} collective-permute-done((bf16[256,2176]{1,0:T(8,128)(2,1)}, bf16[256,2176]{1,0:T(8,128)(2,1)}, u32[]{:S(2)}, u32[]{:S(2)}) %collective-permute-start.1) | collective-permute-done | bytes 1114144 | tf_op jit(solution)/shard_map/ring_normed/ppermute | solution.py:404
  50.5 24.0 %all_to_all.20 = bf16[8,64,768]{2,1,0:T(8,128)(2,1)} all-to-all(bf16[8,64,768]{2,1,0:T(8,128)(2,1)} %reshape.295), channel_id=1, replica_groups=mesh['dp'=4,'expert'=8] {'expert'}, dimensions={0} | all-to-all | bytes 1572864 | tf_op jit(solution)/shard_map/all_to_all | solution.py:684
  85.4 16.9 %collective-permute-done.3 = bf16[256,2176]{1,0:T(8,128)(2,1)S(1)} collective-permute-done((bf16[256,2176]{1,0:T(8,128)(2,1)}, bf16[256,2176]{1,0:T(8,128)(2,1)S(1)}, u32[]{:S(2)}, u32[]{:S(2)}) %collective-permute-start.3) | collective-permute-done | bytes 1114144 | tf_op jit(solution)/shard_map/ring_normed/ppermute | solution.py:404
  108.8 17.6 %collective-permute-done.5 = bf16[256,2176]{1,0:T(8,128)(2,1)S(1)} collective-permute-done((bf16[256,2176]{1,0:T(8,128)(2,1)S(1)}, bf16[256,2176]{1,0:T(8,128)(2,1)S(1)}, u32[]{:S(2)}, u32[]{:S(2)}) %collective-permute-start.5) | collective-permute-done | bytes 1114144 | tf_op jit(solution)/shard_map/ring_normed/ppermute | solution.py:404
  146.1 11.7 %fusion.36 = f32[2048,768]{1,0:T(8,128)} fusion(bf16[2048,2048]{1,0:T(8,128)(2,1)} %slice_dynamic-update-slice_fusion, bf16[2048,768]{1,0:T(8,128)(2,1)} %all-gather.4.cloned.1.call-done), kind=kOutput, calls=%fused_computation.180 | convolution fusion | flops 6442450944 | bytes 17825792 | tf_op jit(solution)/shard_map/dot_general | solution.py:39
  157.8 20.1 %attend.1 = bf16[8,2,128,256]{3,2,1,0:T(8,128)(2,1)} custom-call(s32[8]{0:T(128)} %dynamic-slice_bitcast_fusion.owner_ref, f32[8,2,128,768]{3,2,1,0:T(8,128)} %bitcast.153, f32[1024,128]{1,0:T(8,128)} %get-tuple-element.381.cos_ref, f32[1024,128]{1,0:T(8,128)} %get-tuple-element.382.sin_ref, f32[2,1,1024]{2,1,0:T(1,128)} %compare_convert_fusion.live_ref, ...), custom_call_target="tpu_custom_call" | custom-call | flops 2147483648 | bytes 7864320 | tf_op jit(solution)/shard_map/attend/pallas_call | solution.py:105
  196.5 10.5 %collective-permute-done.8.refs_1_ = bf16[256,2048]{1,0:T(8,128)(2,1)} collective-permute-done((bf16[256,2048]{1,0:T(8,128)(2,1)S(1)}, bf16[256,2048]{1,0:T(8,128)(2,1)}, u32[]{:S(2)}, u32[]{:S(2)}) %collective-permute-start.8) | collective-permute-done | bytes 1048608 | tf_op jit(solution)/shard_map/ring_cotangent/ppermute | solution.py:404
  229.6 12.1 %all-to-all-done.1 = bf16[8,256,256]{1,2,0:T(8,128)(2,1)S(1)} async-done(((bf16[8,256,256]{1,2,0:T(8,128)(2,1)}), bf16[8,256,256]{1,2,0:T(8,128)(2,1)S(1)}, u32[]{:S(2)}, u32[]{:S(2)}) %all-to-all-start.1) | async-done | bytes 1048608 | tf_op jit(solution)/shard_map/all_to_all | solution.py:726
  267.1 17.7 %experts_forward.5 = (bf16[2048,2048]{1,0:T(8,128)(2,1)}, bf16[2048,2048]{1,0:T(8,128)(2,1)}, bf16[2048,2048]{1,0:T(8,128)(2,1)}, bf16[2048,2048]{1,0:T(8,128)(2...) custom-call(bf16[256,2048]{1,0:T(8,128)(2,1)} %copy-done.5, bf16[256,128]{1,0:T(8,128)(2,1)} %copy-done.40, ...), custom_call_target="tpu_custom_call" | custom-call | flops 6442450944 | bytes 30408704 | tf_op jit(solution)/shard_map/experts_forward/pallas_call | solution.py:272
  287.3 17.4 %collective-permute-done.15.refs_1_ = bf16[256,2048]{1,0:T(8,128)(2,1)S(1)} collective-permute-done((bf16[256,2048]{1,0:T(8,128)(2,1)}, bf16[256,2048]{1,0:T(8,128)(2,1)S(1)}, u32[]{:S(2)}, u32[]{:S(2)}) %collective-permute-start.15) | collective-permute-done | bytes 1048608 | tf_op jit(solution)/shard_map/ring_cotangent/ppermute | solution.py:404
  304.8 24.2 %experts_forward.6 = (bf16[2048,2048]{1,0:T(8,128)(2,1)}, bf16[2048,2048]{1,0:T(8,128)(2,1)}, bf16[2048,2048]{1,0:T(8,128)(2,1)}, bf16[2048,2048]{1,0:T(8,128)(2...) custom-call(bf16[256,2048]{1,0:T(8,128)(2,1)} %collective-permute-do, ...), custom_call_target="tpu_custom_call", output_to_operand_aliasing={{0}: (8, {}), {1}: (9, {}), {2}: (10, {}), {3}: (11, {})} | custom-call | flops 12884901888 | bytes 35651584 | tf_op jit(solution)/shard_map/experts_forward/pallas_call | solution.py:272
  336.2 23.6 %experts_forward.7 = (bf16[2048,2048]{1,0:T(8,128)(2,1)}, bf16[2048,2048]{1,0:T(8,128)(2,1)}, bf16[2048,2048]{1,0:T(8,128)(2,1)}, bf16[2048,2048]{1,0:T(8,128)(2...) custom-call(bf16[256,2048]{1,0:T(8,128)(2,1)} %copy-done.36, ...), custom_call_target="tpu_custom_call", output_to_operand_aliasing={{0}: (8, {}), {1}: (9, {}), {2}: (10, {}), {3}: (11, {})} | custom-call | flops 12884901888 | bytes 35651584 | tf_op jit(solution)/shard_map/experts_forward/pallas_call | solution.py:272
  369.4 23.7 %experts_forward.8 = (bf16[2048,2048]{1,0:T(8,128)(2,1)}, bf16[2048,2048]{1,0:T(8,128)(2,1)}, bf16[2048,2048]{1,0:T(8,128)(2,1)}, bf16[2048,2048]{1,0:T(8,128)(2...) custom-call(bf16[256,2048]{1,0:T(8,128)(2,1)} %copy-done.25, ...), custom_call_target="tpu_custom_call", output_to_operand_aliasing={{0}: (8, {}), {1}: (9, {}), {2}: (10, {}), {3}: (11, {})} | custom-call | flops 12884901888 | bytes 35651584 | tf_op jit(solution)/shard_map/experts_forward/pallas_call | solution.py:272
  395.5 17.8 %experts_forward.9 = (bf16[2048,2048]{1,0:T(8,128)(2,1)}, bf16[2048,2048]{1,0:T(8,128)(2,1)}, bf16[2048,2048]{1,0:T(8,128)(2,1)}, bf16[2048,2048]{1,0:T(8,128)(2...) custom-call(bf16[256,2048]{1,0:T(8,128)(2,1)} %pad_maximum_fusion.8., ...), custom_call_target="tpu_custom_call", output_to_operand_aliasing={{0}: (7, {}), {1}: (8, {}), {2}: (9, {}), {3}: (10, {})} | custom-call | flops 6442450944 | bytes 30408704 | tf_op jit(solution)/shard_map/experts_forward/pallas_call | solution.py:272
  417.7 17.2 %experts_backward.5 = (bf16[2048,2048]{1,0:T(8,128)(2,1)}, bf16[2048,2048]{1,0:T(8,128)(2,1)}, bf16[2048,2048]{1,0:T(8,128)(2,1)}, f32[256,128]{1,0:T(8,128)}, bf16[256,2048]{1,0:T(8,128)(2,1)}) custom-call(bf16[256,2048]{1,0:T(8,128)(2,1)} %pad_maximum_fusion.11.refs_0_, f32[256,2]{1,0:T(8,128)} %get-tuple-element.167.refs_1_, ...), custom_call_target="tpu_custom_call" | custom-call | flops 6442450944 | bytes 31457280 | tf_op jit(solution)/shard_map/experts_backward/pallas_call | solution.py:359
  439.4 23.9 %experts_backward.6 = (bf16[2048,2048]{1,0:T(8,128)(2,1)}, bf16[2048,2048]{1,0:T(8,128)(2,1)}, bf16[2048,2048]{1,0:T(8,128)(2,1)}, f32[512,128]{1,0:T(8,128)}, bf16[512,2048]{1,0:T(8,128)(2,1)}) custom-call(bf16[256,2048]{1,0:T(8,128)(2,1)} %copy-done.24, bf16[256,2048]{1,0:T(8,128)(2,1)} %copy-done.23, ...), custom_call_target="tpu_custom_call", output_to_operand_aliasing={{0}: (8, {}), {1}: (9, {}), {2}: (10, {})} | custom-call | flops 12884901888 | bytes 37748736 | tf_op jit(solution)/shard_map/experts_backward/pallas_call | solution.py:359
  472.0 24.0 %experts_backward.7 = (bf16[2048,2048]{1,0:T(8,128)(2,1)}, bf16[2048,2048]{1,0:T(8,128)(2,1)}, bf16[2048,2048]{1,0:T(8,128)(2,1)}, f32[512,128]{1,0:T(8,128)}, bf16[512,2048]{1,0:T(8,128)(2,1)}) custom-call(bf16[256,2048]{1,0:T(8,128)(2,1)} %collective-permute-done.13.refs_0_, ...), custom_call_target="tpu_custom_call", output_to_operand_aliasing={{0}: (8, {}), {1}: (9, {}), {2}: (10, {})} | custom-call | flops 12884901888 | bytes 37748736 | tf_op jit(solution)/shard_map/experts_backward/pallas_call | solution.py:359
  501.0 10.6 %collective-permute-done.30 = bf16[256,2176]{1,0:T(8,128)(2,1)S(1)} collective-permute-done((bf16[256,2176]{1,0:T(8,128)(2,1)S(1)}, bf16[256,2176]{1,0:T(8,128)(2,1)S(1)}, u32[]{:S(2)}, u32[]{:S(2)}) %collective-permute-start.30) | collective-permute-done | bytes 1114144 | tf_op jit(solution)/shard_map/ring_ffn_grad/ppermute | solution.py:404
  516.2 23.8 %experts_backward.8 = (bf16[2048,2048]{1,0:T(8,128)(2,1)}, bf16[2048,2048]{1,0:T(8,128)(2,1)}, bf16[2048,2048]{1,0:T(8,128)(2,1)}, f32[512,128]{1,0:T(8,128)}, bf16[512,2048]{1,0:T(8,128)(2,1)}) custom-call(bf16[256,2048]{1,0:T(8,128)(2,1)} %collective-permute-done.9.refs_0_, ...), custom_call_target="tpu_custom_call", output_to_operand_aliasing={{0}: (8, {}), {1}: (9, {}), {2}: (10, {})} | custom-call | flops 12884901888 | bytes 37748736 | tf_op jit(solution)/shard_map/experts_backward/pallas_call | solution.py:359
  545.1 17.2 %experts_backward.9 = (bf16[2048,2048]{1,0:T(8,128)(2,1)}, bf16[2048,2048]{1,0:T(8,128)(2,1)}, bf16[2048,2048]{1,0:T(8,128)(2,1)}, f32[256,128]{1,0:T(8,128)}, bf16[256,2048]{1,0:T(8,128)(2,1)}) custom-call(bf16[256,2048]{1,0:T(8,128)(2,1)} %bitcast.149, ...), custom_call_target="tpu_custom_call", output_to_operand_aliasing={{0}: (7, {}), {1}: (8, {}), {2}: (9, {})} | custom-call | flops 6442450944 | bytes 31457280 | tf_op jit(solution)/shard_map/experts_backward/pallas_call | solution.py:359
  564.5 15.2 %weights_out.2 = bf16[1024,2048]{1,0:T(8,128)(2,1)} custom-call(s32[4]{0:T(128)} %pad_add_fusion.index_ref, bf16[2048,2048]{1,0:T(8,128)(2,1)} %get-tuple-element.209.refs_0_.refs_1_.refs_2_.refs_3_, bf16[2048,2048]{1,0:T(8,128)(2,1)} %get-tuple-element.209.refs_0_.refs_1_.refs_2_.refs_3_, ...), custom_call_target="tpu_custom_call" | custom-call | flops 8589934592 | bytes 20971520 | tf_op jit(solution)/shard_map/weights_out/pallas_call | solution.py:538
  606.8 10.7 %collective-permute-done.34 = bf16[256,2048]{1,0:T(8,128)(2,1)} collective-permute-done((bf16[256,2048]{1,0:T(8,128)(2,1)}, bf16[256,2048]{1,0:T(8,128)(2,1)}, u32[]{:S(2)}, u32[]{:S(2)}) %collective-permute-start.34) | collective-permute-done | bytes 1048608 | tf_op jit(solution)/shard_map/ring_mixture/ppermute | solution.py:404
  623.6 16.1 %weights_out.3 = (bf16[512,2048]{1,0:T(8,128)(2,1)}, f32[512,2048]{1,0:T(8,128)}) custom-call(s32[8]{0:T(128)} %stack.100.index_ref, bf16[2048,2048]{1,0:T(8,128)(2,1)} %get-tuple-element.209.refs_0_.refs_1_.refs_2_.refs_3_, bf16[2048,2048]{1,0:T(8,128)(2,1)} %get-tuple-element.209.refs_0_.refs_1_.refs_2_.refs_3_, ...), custom_call_target="tpu_custom_call" | custom-call | flops 8589934592 | bytes 20971520 | tf_op jit(solution)/shard_map/weights_out/pallas_call | solution.py:538
  644.3 28.5 %attend_back.1 = (bf16[8,2,128,768]{3,2,1,0:T(8,128)(2,1)}, f32[2,2,2,128]{3,2,1,0:T(2,128)}) custom-call(s32[8]{0:T(128)} %dynamic-slice_bitcast_fusion.owner_ref, f32[8,2,128,768]{3,2,1,0:T(8,128)} %bitcast.154, bf16[8,2,128,256]{3,2,1,0:T(8,128)(2,1)} %bitcast.162, f32[1024,128]{1,0:T(8,128)} %get-tuple-element.381.cos_ref, ...), custom_call_target="tpu_custom_call" | custom-call | flops 5368709120 | bytes 11010048 | tf_op jit(solution)/shard_map/attend_back/pallas_call | solution.py:176
  672.9 11.4 %convolution_convert_fusion = bf16[2048,2048]{1,0:T(8,128)(2,1)} fusion(bf16[2048,768]{1,0:T(8,128)(2,1)} %bitcast.170, bf16[2048,768]{1,0:T(8,128)(2,1)} %all-gather.4.cloned.1.call-done), kind=kOutput, calls=%fused_computation.2 | convolution fusion | flops 6446645248 | bytes 14680064 | tf_op jit(solution)/shard_map/dot_general | solution.py:43
  686.2 15.5 %weights_gate.2 = bf16[1024,2048]{1,0:T(8,128)(2,1)} custom-call(s32[2]{0:T(128)} %pad_add_fusion.2.index_ref, bf16[2048,2048]{1,0:T(8,128)(2,1)} %get-tuple-element.223.refs_0_.refs_1_, bf16[2048,2048]{1,0:T(8,128)(2,1)} %get-tuple-element.223.refs_0_.refs_1_, bf16[2048,2048]{1,0:T(8,128)(2,1)} %get-tuple-element.220.refs_2_), custom_call_target="tpu_custom_call" | custom-call | flops 8589934592 | bytes 20971520 | tf_op jit(solution)/shard_map/weights_gate/pallas_call | solution.py:538
  713.4 15.8 %weights_gate.3 = (bf16[512,2048]{1,0:T(8,128)(2,1)}, f32[512,2048]{1,0:T(8,128)}) custom-call(s32[4]{0:T(128)} %pad_add_fusion.1.index_ref, bf16[2048,2048]{1,0:T(8,128)(2,1)} %get-tuple-element.223.refs_0_.refs_1_, bf16[2048,2048]{1,0:T(8,128)(2,1)} %get-tuple-element.223.refs_0_.refs_1_, bf16[2048,2048]{1,0:T(8,128)(2,1)} %get-tuple-element.220.refs_2_, ...), custom_call_target="tpu_custom_call" | custom-call | flops 8589934592 | bytes 20971520 | tf_op jit(solution)/shard_map/weights_gate/pallas_call | solution.py:538
  739.7 15.7 %weights_up.2 = bf16[1024,2048]{1,0:T(8,128)(2,1)} custom-call(s32[2]{0:T(128)} %pad_add_fusion.2.index_ref, bf16[2048,2048]{1,0:T(8,128)(2,1)} %get-tuple-element.223.refs_0_.refs_1_, bf16[2048,2048]{1,0:T(8,128)(2,1)} %get-tuple-element.223.refs_0_.refs_1_, bf16[2048,2048]{1,0:T(8,128)(2,1)} %get-tuple-element.224.refs_2_), custom_call_target="tpu_custom_call" | custom-call | flops 8589934592 | bytes 20971520 | tf_op jit(solution)/shard_map/weights_up/pallas_call | solution.py:538
  769.3 14.9 %collective-permute-done.47 = bf16[256,2048]{1,0:T(8,128)(2,1)S(1)} collective-permute-done((bf16[256,2048]{1,0:T(8,128)(2,1)}, bf16[256,2048]{1,0:T(8,128)(2,1)S(1)}, u32[]{:S(2)}, u32[]{:S(2)}) %collective-permute-start.47) | collective-permute-done | bytes 1048608 | tf_op jit(solution)/shard_map/ring_normed_grad/ppermute | solution.py:404
  794.7 17.4 %collective-permute-done.49 = bf16[256,2048]{1,0:T(8,128)(2,1)S(1)} collective-permute-done((bf16[256,2048]{1,0:T(8,128)(2,1)S(1)}, bf16[256,2048]{1,0:T(8,128)(2,1)S(1)}, u32[]{:S(2)}, u32[]{:S(2)}) %collective-permute-start.49) | collective-permute-done | bytes 1048608 | tf_op jit(solution)/shard_map/ring_normed_grad/ppermute | solution.py:404
  819.4 16.0 %weights_up.3 = (bf16[512,2048]{1,0:T(8,128)(2,1)}, f32[512,2048]{1,0:T(8,128)}) custom-call(s32[4]{0:T(128)} %pad_add_fusion.1.index_ref, bf16[2048,2048]{1,0:T(8,128)(2,1)} %get-tuple-element.223.refs_0_.refs_1_, bf16[2048,2048]{1,0:T(8,128)(2,1)} %get-tuple-element.223.refs_0_.refs_1_, bf16[2048,2048]{1,0:T(8,128)(2,1)} %get-tuple-element.224.refs_2_, ...), custom_call_target="tpu_custom_call" | custom-call | flops 8589934592 | bytes 20971520 | tf_op jit(solution)/shard_map/weights_up/pallas_call | solution.py:538
  864.3 17.3 %collective-permute-done.59 = bf16[512,2048]{1,0:T(8,128)(2,1)} collective-permute-done((bf16[512,2048]{1,0:T(8,128)(2,1)}, bf16[512,2048]{1,0:T(8,128)(2,1)}, u32[]{:S(2)}, u32[]{:S(2)}) %collective-permute-start.59) | collective-permute-done | bytes 2097184 | tf_op jit(solution)/shard_map/weights_up_groups/ppermute | solution.py:599
  (430 shorter events, 344.3 us)
Async XLA Ops:
  7.2 139.0 %all-gather.4.cloned.1.call-start = ((), (), s32[]{:S(2)}) async-start(), calls=%async_computation.7 | async-start | bytes 3932160 | tf_op jit(solution)/shard_map/all_gather | solution.py:695
  74.5 106.9 %all-gather.6.cloned.1.call-start = ((), (), s32[]{:S(2)}) async-start(), calls=%async_computation.8 | async-start | bytes 2359296 | tf_op jit(solution)/shard_map/all_gather | solution.py:702
  131.2 110.5 %all-gather.8.cloned.1.call-start = ((), (), s32[]{:S(2)}) async-start(), calls=%async_computation.9 | async-start | bytes 10485760 | tf_op jit(solution)/shard_map/all_gather | solution.py:723
  214.6 626.9 %reduce-scatter.6.cloned.1.call-start = ((), (), s32[]{:S(2)}) async-start(), calls=%async_computation.11 | async-start | bytes 10485760 | tf_op jit(solution)/shard_map/reduce_scatter | solution.py:844
  226.1 39.2 %collective-permute-start.39 = (f32[16]{0:T(128)S(1)}, f32[16]{0:T(128)S(1)}, u32[]{:S(2)}, u32[]{:S(2)}) collective-permute-start(f32[16]{0:T(128)S(1)} %slice_add_fusion.1), channel_id=1, source_target_pairs={{0,16},{8,24},{16,0},{24,8},{1,17},{9,25},{17,1},{25,9},{2,18},{10... | collective-permute-start | bytes 200 | tf_op jit(solution)/shard_map/ppermute | solution.py:472
  248.2 36.6 %collective-permute-start.11 = (bf16[256,2048]{1,0:T(8,128)(2,1)S(1)}, bf16[256,2048]{1,0:T(8,128)(2,1)}, u32[]{:S(2)}, u32[]{:S(2)}) collective-permute-start(bf16[256,2048]{1,0:T(8,128)(2,1)S(1)} %multiply_convert_fusion.refs_0_), channel_id=1, source_target_pairs={{0,1},{2,0},{4,2},{6,4},{7,6},{5,7},{3,5},{1,3},{8,9},{10,8},{12,1... | collective-permute-start | bytes 3145736 | tf_op jit(solution)/shard_map/ring_ffn/ppermute | solution.py:404
  248.4 36.4 %collective-permute-start.10 = (bf16[256,2048]{1,0:T(8,128)(2,1)S(1)}, bf16[256,2048]{1,0:T(8,128)(2,1)}, u32[]{:S(2)}, u32[]{:S(2)}) collective-permute-start(bf16[256,2048]{1,0:T(8,128)(2,1)S(1)} %multiply_convert_fusion.refs_0_), channel_id=1, source_target_pairs={{0,2},{2,4},{4,6},{6,7},{7,5},{5,3},{3,1},{1,0},{8,10},{10,12},{12... | collective-permute-start | bytes 3145736 | tf_op jit(solution)/shard_map/ring_ffn/ppermute | solution.py:404
  259.9 44.8 %collective-permute-start.15 = (bf16[256,2048]{1,0:T(8,128)(2,1)}, bf16[256,2048]{1,0:T(8,128)(2,1)S(1)}, u32[]{:S(2)}, u32[]{:S(2)}) collective-permute-start(bf16[256,2048]{1,0:T(8,128)(2,1)} %collective-permute-done.14.refs_1_), channel_id=1, source_target_pairs={{0,1},{2,0},{4,2},{6,4},{7,6},{5,7},{3,5},{1,3},{8,9},{10,8},{12,1... | collective-permute-start | bytes 3145736 | tf_op jit(solution)/shard_map/ring_cotangent/ppermute | solution.py:404
  260.0 44.7 %collective-permute-start.16 = (bf16[256,2048]{1,0:T(8,128)(2,1)}, bf16[256,2048]{1,0:T(8,128)(2,1)S(1)}, u32[]{:S(2)}, u32[]{:S(2)}) collective-permute-start(bf16[256,2048]{1,0:T(8,128)(2,1)} %collective-permute-done.13.refs_0_), channel_id=1, source_target_pairs={{0,2},{2,4},{4,6},{6,7},{7,5},{5,3},{3,1},{1,0},{8,10},{10,12},{12... | collective-permute-start | bytes 3145736 | tf_op jit(solution)/shard_map/ring_cotangent/ppermute | solution.py:404
  284.9 49.2 %collective-permute-start.12 = (bf16[256,2048]{1,0:T(8,128)(2,1)}, bf16[256,2048]{1,0:T(8,128)(2,1)S(1)}, u32[]{:S(2)}, u32[]{:S(2)}) collective-permute-start(bf16[256,2048]{1,0:T(8,128)(2,1)} %collective-permute-done.10.refs_0_), channel_id=1, source_target_pairs={{0,2},{2,4},{4,6},{6,7},{7,5},{5,3},{3,1},{1,0},{8,10},{10,12},{12... | collective-permute-start | bytes 3145736 | tf_op jit(solution)/shard_map/ring_ffn/ppermute | solution.py:404
  287.3 46.8 %collective-permute-start.17 = (bf16[256,2048]{1,0:T(8,128)(2,1)}, bf16[256,2048]{1,0:T(8,128)(2,1)S(1)}, u32[]{:S(2)}, u32[]{:S(2)}) collective-permute-start(bf16[256,2048]{1,0:T(8,128)(2,1)} %collective-permute-done.11.refs_1_), channel_id=1, source_target_pairs={{0,1},{2,0},{4,2},{6,4},{7,6},{5,7},{3,5},{1,3},{8,9},{10,8},{12,1... | collective-permute-start | bytes 3145736 | tf_op jit(solution)/shard_map/ring_ffn/ppermute | solution.py:404
  329.1 85.5 %collective-permute-start.24 = (bf16[128,2048]{1,0:T(8,128)(2,1)S(1)}, bf16[128,2048]{1,0:T(8,128)(2,1)S(1)}, u32[]{:S(2)}, u32[]{:S(2)}) collective-permute-start(bf16[128,2048]{1,0:T(8,128)(2,1)S(1)} %slice.340), channel_id=1, source_target_pairs={{0,2},{2,4},{4,6},{6,7},{7,5},{5,3},{3,1},{1,0},{8,10},{10,12},{12... | collective-permute-start | bytes 1572872 | tf_op jit(solution)/shard_map/ring_cotangent/ppermute | solution.py:404
  334.0 80.5 %collective-permute-start.25 = (bf16[128,2048]{1,0:T(8,128)(2,1)S(1)}, bf16[128,2048]{1,0:T(8,128)(2,1)S(1)}, u32[]{:S(2)}, u32[]{:S(2)}) collective-permute-start(bf16[128,2048]{1,0:T(8,128)(2,1)S(1)} %slice.341), channel_id=1, source_target_pairs={{0,1},{2,0},{4,2},{6,4},{7,6},{5,7},{3,5},{1,3},{8,9},{10,8},{12,1... | collective-permute-start | bytes 1572872 | tf_op jit(solution)/shard_map/ring_cotangent/ppermute | solution.py:404
  414.6 51.1 %collective-permute-start.23 = (bf16[128,2048]{1,0:T(8,128)(2,1)S(1)}, bf16[128,2048]{1,0:T(8,128)(2,1)S(1)}, u32[]{:S(2)}, u32[]{:S(2)}) collective-permute-start(bf16[128,2048]{1,0:T(8,128)(2,1)S(1)} %get-tuple-element.357), channel_id=1, source_target_pairs={{0,1},{2,0},{4,2},{6,4},{7,6},{5,7},{3,5},{1,3},{8,9},{10,8},{12,1... | collective-permute-start | bytes 1572872 | tf_op jit(solution)/shard_map/ring_mixture/ppermute | solution.py:404
  414.7 51.1 %collective-permute-start.22 = (bf16[128,2048]{1,0:T(8,128)(2,1)S(1)}, bf16[128,2048]{1,0:T(8,128)(2,1)S(1)}, u32[]{:S(2)}, u32[]{:S(2)}) collective-permute-start(bf16[128,2048]{1,0:T(8,128)(2,1)S(1)} %get-tuple-element.358), channel_id=1, source_target_pairs={{0,2},{2,4},{4,6},{6,7},{7,5},{5,3},{3,1},{1,0},{8,10},{10,12},{12... | collective-permute-start | bytes 1572872 | tf_op jit(solution)/shard_map/ring_mixture/ppermute | solution.py:404
  469.8 41.8 %collective-permute-start.30 = (bf16[256,2176]{1,0:T(8,128)(2,1)S(1)}, bf16[256,2176]{1,0:T(8,128)(2,1)S(1)}, u32[]{:S(2)}, u32[]{:S(2)}) collective-permute-start(bf16[256,2176]{1,0:T(8,128)(2,1)S(1)} %pad_maximum_fusion.5), channel_id=1, source_target_pairs={{0,2},{2,4},{4,6},{6,7},{7,5},{5,3},{3,1},{1,0},{8,10},{10,12},{12... | collective-permute-start | bytes 3342344 | tf_op jit(solution)/shard_map/ring_ffn_grad/ppermute | solution.py:404
  470.4 42.6 %collective-permute-start.31 = (bf16[256,2176]{1,0:T(8,128)(2,1)S(1)}, bf16[256,2176]{1,0:T(8,128)(2,1)S(1)}, u32[]{:S(2)}, u32[]{:S(2)}) collective-permute-start(bf16[256,2176]{1,0:T(8,128)(2,1)S(1)} %pad_maximum_fusion.6), channel_id=1, source_target_pairs={{0,1},{2,0},{4,2},{6,4},{7,6},{5,7},{3,5},{1,3},{8,9},{10,8},{12,1... | collective-permute-start | bytes 3342344 | tf_op jit(solution)/shard_map/ring_ffn_grad/ppermute | solution.py:404
  543.0 36.7 %collective-permute-start.37 = (bf16[256,2176]{1,0:T(8,128)(2,1)S(1)}, bf16[256,2176]{1,0:T(8,128)(2,1)S(1)}, u32[]{:S(2)}, u32[]{:S(2)}) collective-permute-start(bf16[256,2176]{1,0:T(8,128)(2,1)S(1)} %get-tuple-element.325), channel_id=1, source_target_pairs={{0,1},{2,0},{4,2},{6,4},{7,6},{5,7},{3,5},{1,3},{8,9},{10,8},{12,1... | collective-permute-start | bytes 3342344 | tf_op jit(solution)/shard_map/ring_ffn_grad/ppermute | solution.py:404
  543.8 36.0 %collective-permute-start.36 = (bf16[256,2176]{1,0:T(8,128)(2,1)S(1)}, bf16[256,2176]{1,0:T(8,128)(2,1)S(1)}, u32[]{:S(2)}, u32[]{:S(2)}) collective-permute-start(bf16[256,2176]{1,0:T(8,128)(2,1)S(1)} %get-tuple-element.326), channel_id=1, source_target_pairs={{0,2},{2,4},{4,6},{6,7},{7,5},{5,3},{3,1},{1,0},{8,10},{10,12},{12... | collective-permute-start | bytes 3342344 | tf_op jit(solution)/shard_map/ring_ffn_grad/ppermute | solution.py:404
  591.0 32.6 %collective-permute-start.40 = (bf16[1024,2048]{1,0:T(8,128)(2,1)}, bf16[1024,2048]{1,0:T(8,128)(2,1)}, u32[]{:S(2)}, u32[]{:S(2)}) collective-permute-start(bf16[1024,2048]{1,0:T(8,128)(2,1)} %weights_out.2), channel_id=1, source_target_pairs={{0,8},{8,0},{16,24},{24,16},{1,9},{9,1},{17,25},{25,17},{2,10},{10... | collective-permute-start | bytes 12582920 | tf_op jit(solution)/shard_map/weights_out_cores/ppermute | solution.py:581
  600.2 42.1 %all-to-all-start.2 = ((bf16[8,256,256]{2,1,0:T(8,128)(2,1)}), bf16[8,256,256]{2,1,0:T(8,128)(2,1)S(1)}, u32[]{:S(2)}, u32[]{:S(2)}) async-start(bf16[8,256,256]{2,1,0:T(8,128)(2,1)} %bitcast.128), calls=%async_computation.2 | async-start | bytes 2097152 | tf_op jit(solution)/shard_map/all_to_all | solution.py:835
  605.4 244.6 %reduce-scatter.4.cloned.1.call-start = ((), (), s32[]{:S(2)}) async-start(), calls=%async_computation.10 | async-start | bytes 3932160 | tf_op jit(solution)/shard_map/reduce_scatter | solution.py:890
  642.3 42.0 %collective-permute-start.41 = (bf16[256,2048]{1,0:T(8,128)(2,1)}, bf16[256,2048]{1,0:T(8,128)(2,1)S(1)}, u32[]{:S(2)}, u32[]{:S(2)}) collective-permute-start(bf16[256,2048]{1,0:T(8,128)(2,1)} %get-tuple-element.212), channel_id=1, source_target_pairs={{0,2},{2,4},{4,6},{6,7},{7,5},{5,3},{3,1},{1,0},{8,10},{10,12},{12... | collective-permute-start | bytes 3145736 | tf_op jit(solution)/shard_map/ring_mixture/ppermute | solution.py:404
  642.3 42.0 %collective-permute-start.42 = (bf16[256,2048]{1,0:T(8,128)(2,1)}, bf16[256,2048]{1,0:T(8,128)(2,1)S(1)}, u32[]{:S(2)}, u32[]{:S(2)}) collective-permute-start(bf16[256,2048]{1,0:T(8,128)(2,1)} %get-tuple-element.213), channel_id=1, source_target_pairs={{0,1},{2,0},{4,2},{6,4},{7,6},{5,7},{3,5},{1,3},{8,9},{10,8},{12,1... | collective-permute-start | bytes 3145736 | tf_op jit(solution)/shard_map/ring_mixture/ppermute | solution.py:404
  704.1 86.1 %collective-permute-start.60 = (bf16[512,2048]{1,0:T(8,128)(2,1)}, bf16[512,2048]{1,0:T(8,128)(2,1)}, u32[]{:S(2)}, u32[]{:S(2)}) collective-permute-start(bf16[512,2048]{1,0:T(8,128)(2,1)} %get-tuple-element.210), channel_id=1, source_target_pairs={{0,16},{8,24},{16,0},{24,8},{1,17},{9,25},{17,1},{25,9},{2,18},{10... | collective-permute-start | bytes 6291464 | tf_op jit(solution)/shard_map/weights_out_groups/ppermute | solution.py:599
  711.4 44.0 %collective-permute-start.46 = (bf16[128,2048]{1,0:T(8,128)(2,1)}, bf16[128,2048]{1,0:T(8,128)(2,1)S(1)}, u32[]{:S(2)}, u32[]{:S(2)}) collective-permute-start(bf16[128,2048]{1,0:T(8,128)(2,1)} %get-tuple-element.316), channel_id=1, source_target_pairs={{0,1},{2,0},{4,2},{6,4},{7,6},{5,7},{3,5},{1,3},{8,9},{10,8},{12,1... | collective-permute-start | bytes 1572872 | tf_op jit(solution)/shard_map/ring_normed_grad/ppermute | solution.py:404
  711.6 43.7 %collective-permute-start.45 = (bf16[128,2048]{1,0:T(8,128)(2,1)}, bf16[128,2048]{1,0:T(8,128)(2,1)S(1)}, u32[]{:S(2)}, u32[]{:S(2)}) collective-permute-start(bf16[128,2048]{1,0:T(8,128)(2,1)} %get-tuple-element.318), channel_id=1, source_target_pairs={{0,2},{2,4},{4,6},{6,7},{7,5},{5,3},{3,1},{1,0},{8,10},{10,12},{12... | collective-permute-start | bytes 1572872 | tf_op jit(solution)/shard_map/ring_normed_grad/ppermute | solution.py:404
  739.7 181.5 %reduce-scatter.8.cloned.1.call-start = ((), (), s32[]{:S(2)}) async-start(), calls=%async_computation.12 | async-start | bytes 2359296 | tf_op jit(solution)/shard_map/reduce_scatter | solution.py:892
  755.4 62.0 %collective-permute-start.44 = (bf16[1024,2048]{1,0:T(8,128)(2,1)}, bf16[1024,2048]{1,0:T(8,128)(2,1)S(1)}, u32[]{:S(2)}, u32[]{:S(2)}) collective-permute-start(bf16[1024,2048]{1,0:T(8,128)(2,1)} %weights_up.2), channel_id=1, source_target_pairs={{0,8},{8,0},{16,24},{24,16},{1,9},{9,1},{17,25},{25,17},{2,10},{10... | collective-permute-start | bytes 12582920 | tf_op jit(solution)/shard_map/weights_up_cores/ppermute | solution.py:581
  789.1 47.3 %collective-permute-start.58 = (bf16[512,2048]{1,0:T(8,128)(2,1)}, bf16[512,2048]{1,0:T(8,128)(2,1)S(1)}, u32[]{:S(2)}, u32[]{:S(2)}) collective-permute-start(bf16[512,2048]{1,0:T(8,128)(2,1)} %get-tuple-element.221), channel_id=1, source_target_pairs={{0,16},{8,24},{16,0},{24,8},{1,17},{9,25},{17,1},{25,9},{2,18},{10... | collective-permute-start | bytes 6291464 | tf_op jit(solution)/shard_map/weights_gate_groups/ppermute | solution.py:599
  835.4 46.2 %collective-permute-start.59 = (bf16[512,2048]{1,0:T(8,128)(2,1)}, bf16[512,2048]{1,0:T(8,128)(2,1)}, u32[]{:S(2)}, u32[]{:S(2)}) collective-permute-start(bf16[512,2048]{1,0:T(8,128)(2,1)} %get-tuple-element.225), channel_id=1, source_target_pairs={{0,16},{8,24},{16,0},{24,8},{1,17},{9,25},{17,1},{25,9},{2,18},{10... | collective-permute-start | bytes 6291464 | tf_op jit(solution)/shard_map/weights_up_groups/ppermute | solution.py:599
  850.0 37.9 %all-to-all-start.3 = ((bf16[8,64,768]{2,1,0:T(8,128)(2,1)}), bf16[8,64,768]{2,1,0:T(8,128)(2,1)S(1)}, u32[]{:S(2)}, u32[]{:S(2)}) async-start(bf16[8,64,768]{2,1,0:T(8,128)(2,1)} %bitcast.164), calls=%async_computation.4 | async-start | bytes 1572864 | tf_op jit(solution)/shard_map/all_to_all | solution.py:907
  (108 other events, 1718.6 us)
Sparse Core Ops, SparseCore 0:
  74.6 27.5 all-gather.3
  131.3 50.0 all-gather.5
  182.9 56.7 all-gather.7
  591.1 72.6 reduce-scatter.5
  739.8 38.8 reduce-scatter.3
  841.6 79.4 reduce-scatter.7
